TPU v7x, 256 devices: a whole 4x4x8 slice. The times are simulated.
256 devices in a mesh: pb: 16 (over y, z_lo, core), ia: 16 (over z_hi, x).
Axes of the slice: x: 4, y: 4, z: 8 (z_hi: 4, z_lo: 2; z = z_hi * 2 + z_lo), core: 2. Of those that a mesh axis runs over, the one named last changes fastest.
Arguments:
- query_hidden: bfloat16 [32768, 2048], P(('pb', 'ia'))
- item_hidden: bfloat16 [8192, 2048], P(('ia', 'pb'))
- query_weight: bfloat16 [2048, 512], replicated, may hold values from -0.125 to 0.125
- item_weight: bfloat16 [2048, 512], replicated, may hold values from -0.125 to 0.125
- tile_list: int32 [64, 8], P('pb'), may hold values from 0 to 15, all different within a row
- item_counts: int32 [8192], replicated, may hold values from 1 to 4095
- positives: int32 [32768], P('pb'), may hold values from 0 to 8191
Outputs:
- losses: float32 [32768], P(('pb', 'ia'))
- grad_query: float32 [2048, 512], P(('pb', 'ia'))
- grad_item: float32 [2048, 512], P(('pb', 'ia'))
Inputs may be any that keep to these rules, and one draw needn't show every extreme that they name: `tile_list`: each row lists 8 different item blocks, and every item block is listed by some row.
All inputs are finite; a program needn't handle non-finite values.
Results may differ from a plain program's by a relative error of at most 0.0044.
Values may be sent and summed in bfloat16 or wider, within the bound.
No kernel may reach another device: no remote copies, remote signals or barrier semaphores. Data moves between devices by JAX's collectives and lax.ppermute only.
A program may use at most 128 MiB of HBM per device.

v0:
```python
import jax
import jax.numpy as jnp
from jax import lax
from jax.sharding import PartitionSpec as P

EMBED = 512
BLOCK = 512
IBLK = 1


EPS = 1e-06
TEMP = 0.05


def normalize(raw_rows):
    return raw_rows * lax.rsqrt(jnp.mean(raw_rows * raw_rows, axis=-1, keepdims=True) + EPS)


def backnorm(raw_rows, upstream):
    factor = lax.rsqrt(jnp.mean(raw_rows * raw_rows, axis=-1, keepdims=True) + EPS)
    normed = raw_rows * factor
    return factor * (upstream - normed * jnp.mean(normed * upstream, axis=-1, keepdims=True))


def local(query_hidden, item_hidden, query_weight, item_weight, tile_list, item_counts, positives):
    score_scale = 1.0 / (EMBED * TEMP)
    query_raw = jnp.dot(query_hidden, query_weight, preferred_element_type=jnp.float32)
    item_raw = jnp.dot(item_hidden, item_weight, preferred_element_type=jnp.float32)
    query_own = normalize(query_raw).astype(jnp.bfloat16)
    item_own = normalize(item_raw).astype(jnp.bfloat16)
    queries = lax.all_gather(query_own, "ia", axis=0, tiled=True)
    items = lax.all_gather(item_own, "pb", axis=0, tiled=True)
    column = lax.axis_index("ia")
    own_rows = query_hidden.shape[0]
    column_rows = items.shape[0]
    query_total = queries.shape[0]
    log_counts = jnp.log(item_counts.astype(jnp.float32))
    offsets = jnp.arange(BLOCK, dtype=jnp.int32)
    owners = jnp.full((IBLK,), column, jnp.int32)
    columns_held = owners.shape[0]
    global_blocks = owners * IBLK + jnp.arange(columns_held, dtype=jnp.int32) % IBLK
    active = jnp.any(tile_list[:, None, :] == global_blocks[None, :, None], axis=2).astype(
        jnp.int32
    )
    flat_mask = active.reshape(-1)
    candidates = flat_mask.shape[0]
    sort_keys = (1 - flat_mask) * candidates + jnp.arange(candidates, dtype=jnp.int32)
    visit_order = jnp.argsort(sort_keys)
    live_count = jnp.sum(flat_mask)
    loop_start = 0

    def tile_place(step_index):
        tile_index = visit_order[step_index]
        query_block = tile_index // columns_held
        item_column = tile_index % columns_held
        query_tile = lax.dynamic_slice_in_dim(queries, query_block * BLOCK, BLOCK, 0)
        return (query_block, item_column, query_tile, items)

    def tile_weights(step_index):
        query_block, item_column, query_tile, item_tile = tile_place(step_index)
        first_item = global_blocks[item_column] * BLOCK
        tile_logs = lax.dynamic_slice_in_dim(log_counts, first_item, BLOCK, 0)
        tile_targets = lax.dynamic_slice_in_dim(positives, query_block * BLOCK, BLOCK, 0)
        scores = lax.dot_general(
            query_tile, item_tile, (((1,), (1,)), ((), ())), preferred_element_type=jnp.float32
        )
        raw_weights = jnp.where(
            first_item + offsets[None, :] != tile_targets[:, None],
            jnp.exp(scores * score_scale - tile_logs[None, :]),
            0.0,
        )
        return (query_block, item_column, query_tile, item_tile, raw_weights)

    def sum_into(running, query_block, raw_weights):
        start_row = query_block * BLOCK
        current = lax.dynamic_slice_in_dim(running, start_row, BLOCK, 0)
        return lax.dynamic_update_slice_in_dim(
            running, current + jnp.sum(raw_weights, axis=1), start_row, 0
        )

    empty_sums = jnp.zeros((query_total,), jnp.float32)

    def add_sums(step_index, running):
        query_block, item_column, query_tile, item_tile, raw_weights = tile_weights(step_index)
        return sum_into(running, query_block, raw_weights)

    partial_sums = lax.fori_loop(loop_start, live_count, add_sums, empty_sums)
    owned = positives // column_rows == column
    target_local = jnp.where(owned, positives - column * column_rows, 0)
    target_rows = items[target_local]
    query_wide = queries.astype(jnp.float32)
    target_part = jnp.where(
        owned,
        jnp.sum(query_wide * target_rows.astype(jnp.float32), axis=-1) * score_scale
        - log_counts[positives],
        0.0,
    )
    totals, target_score = lax.psum((partial_sums, target_part), "ia")
    target_exp = jnp.exp(target_score)
    denominators = totals + target_exp
    all_losses = jnp.log(denominators) - target_score
    losses = lax.dynamic_slice_in_dim(all_losses, column * own_rows, own_rows, 0)
    coefficient = target_exp / denominators - 1.0

    def grads_into(running, query_block, query_tile, item_tile, raw_weights):
        query_acc, item_acc = running
        start_row = query_block * BLOCK
        tile_denoms = lax.dynamic_slice_in_dim(denominators, start_row, BLOCK, 0)
        weights = (raw_weights / tile_denoms[:, None]).astype(jnp.bfloat16)
        query_part = jnp.dot(weights, item_tile, preferred_element_type=jnp.float32)
        item_part = lax.dot_general(
            weights, query_tile, (((0,), (0,)), ((), ())), preferred_element_type=jnp.float32
        )
        query_acc = lax.dynamic_update_slice_in_dim(
            query_acc,
            lax.dynamic_slice_in_dim(query_acc, start_row, BLOCK, 0) + query_part,
            start_row,
            0,
        )
        item_acc = item_acc + item_part
        return (query_acc, item_acc)

    def add_grads(step_index, running):
        query_block, item_column, query_tile, item_tile, raw_weights = tile_weights(step_index)
        return grads_into(running, query_block, query_tile, item_tile, raw_weights)

    query_grad, item_grad = lax.fori_loop(
        loop_start,
        live_count,
        add_grads,
        (
            jnp.zeros((query_total, EMBED), jnp.float32),
            jnp.zeros((items.shape[0], EMBED), jnp.float32),
        ),
    )
    target_coef = jnp.where(owned, coefficient, 0.0)
    query_grad = (query_grad + target_coef[:, None] * target_rows.astype(jnp.float32)) * score_scale
    item_grad = item_grad.at[target_local].add(target_coef[:, None] * query_wide) * score_scale
    query_sum = lax.psum_scatter(query_grad, "ia", scatter_dimension=0, tiled=True)
    item_sum = lax.psum_scatter(item_grad, "pb", scatter_dimension=0, tiled=True)
    query_back = backnorm(query_raw, query_sum).astype(jnp.bfloat16)
    item_back = backnorm(item_raw, item_sum).astype(jnp.bfloat16)
    query_term = lax.dot_general(
        query_hidden, query_back, (((0,), (0,)), ((), ())), preferred_element_type=jnp.float32
    )
    item_term = lax.dot_general(
        item_hidden, item_back, (((0,), (0,)), ((), ())), preferred_element_type=jnp.float32
    )
    both_grads = lax.psum_scatter(
        jnp.concatenate([query_term, item_term], axis=1),
        ("pb", "ia"),
        scatter_dimension=0,
        tiled=True,
    )
    return (losses, both_grads[:, :EMBED], both_grads[:, EMBED:])


def solution(mesh):
    placed = (P(("pb", "ia"), None), P(("ia", "pb"), None), P(), P(), P("pb", None), P(), P("pb"))
    return jax.shard_map(
        local,
        mesh=mesh,
        in_specs=placed,
        out_specs=(P(("pb", "ia")), P(("pb", "ia"), None), P(("pb", "ia"), None)),
        check_vma=False,
    )
```

profile of v0, /device:TPU:0, one launch (start us, length us, event | category | flops | bytes accessed | tf_op | source)
XLA Modules:
  0.0 1689.9 jit_solution(945021247858147991)
XLA Ops:
  7.2 0.0 copy-start
  7.2 0.0 all-gather.2.cloned.1.call-start
  7.2 1.5 copy-done
  8.8 1.6 multiply_reduce_fusion.1
  10.3 0.8 multiply_convert_fusion.1
  11.1 0.0 all-gather.2.cloned.1.call-update
  11.1 0.0 reduce-scatter.8.cloned.1.call-start
  11.2 0.7 broadcast_clamp_fusion
  11.9 0.8 convert_log_fusion
  12.7 11.8 gather_fusion.1
  24.5 0.1 dynamic_slice.67
  24.6 0.1 compare_reduce_fusion
  24.7 0.6 iota_add_fusion.2
  25.3 0.8 sort.17
  26.1 2.2 multiply_reduce_fusion.3
  28.3 0.1 multiply_convert_fusion.4
  28.4 21.9 %all_gather.7 = bf16[512,512]{1,0:T(8,128)(2,1)S(1)} all-gather(bf16[32,512]{1,0:T(8,128)(2,1)S(1)} %multiply_convert_fusion.4), channel_id=1, replica_groups=mesh['pb'=16,'ia'=16] {'pb'}, dimensions={0}, use_global_device_ids=true | all-gather | bytes 557056 | tf_op jit(solution)/shard_map/all_gather | solution.py:32
  50.3 9.2 gather_fusion
  59.5 12.4 all-gather.2.cloned.1.call-done
  71.9 8.2 while.28
  72.5 0.6 dynamic_slice.104
  73.8 0.1 dynamic_slice.105
  73.8 1.6 fusion.58
  75.5 0.2 add_dynamic-update-slice_fusion.2
  76.3 0.6 dynamic_slice.104
  77.6 0.1 dynamic_slice.105
  77.6 1.6 fusion.58
  79.3 0.2 add_dynamic-update-slice_fusion.2
  80.1 2.8 fusion.21
  83.0 81.9 %all-reduce = (f32[2048]{0:T(1024)S(1)}, f32[2048]{0:T(1024)S(1)}) all-reduce(f32[2048]{0:T(1024)S(1)} %subtract_select_fusion, f32[2048]{0:T(1024)S(1)} %get-tuple-element.304), channel_id=1, replica_groups=mesh['pb'=16,'ia'=16] {'ia'}, use_global_device_ids=true, to_apply=%region_10.11 | all-reduce | flops 4096 | bytes 32768 | tf_op jit(solution)/shard_map/psum | solution.py:98
  164.9 1.1 broadcast_in_dim.56
  166.0 2.5 broadcast_in_dim.55
  168.6 17.5 %while.29 = (s32[]{:T(128)}, f32[2048,512]{1,0:T(8,128)}, f32[512,512]{1,0:T(8,128)}, s32[]{:T(128)}, s32[4]{0:T(128)S(1)}, /*index=5*/s32[]{:T(128)}, s32[2048]...) while((s32[]{:T(128)}, f32[2048,512]{1,0:T(8,128)}, ...), condition=%wide.region_12.13_spmd.clone, body=%wide.region_11.12_spmd.clone.sunk | while | flops 807404032 | bytes 16271689 | solution.py:127
  169.2 0.6 dynamic_slice.109
  170.5 0.1 dynamic_slice.110
  170.5 0.1 dynamic_slice.111
  170.6 1.7 fusion.65
  172.4 1.5 convolution_add_fusion.3
  173.9 3.0 fusion.66
  177.6 0.6 dynamic_slice.109
  178.9 0.1 dynamic_slice.110
  178.9 0.1 dynamic_slice.111
  179.0 1.7 fusion.65
  180.8 1.5 convolution_add_fusion.3
  182.3 3.1 fusion.66
  186.0 17.5 %scatter_custom_fusion = f32[512,512]{1,0:T(8,128)} fusion(f32[512,512]{1,0:T(8,128)} %get-tuple-element.306, s32[2048]{0:T(1024)S(1)} %get-tuple-element.405, bf16[2048,512]{1,0:T(8,128)(2,1)} %get-tuple-element.640, f32[2048]{0:T(1024)S(1)} %get-tuple-element.408), kind=kCustom, calls=%fused_computation.32 | custom fusion | flops 3145728 | bytes 3153920 | tf_op jit(solution)/shard_map/scatter-add | solution.py:138
  203.5 2.3 broadcast_multiply_fusion
  205.8 0.0 reduce-scatter.8.cloned.1.call-update
  205.8 0.0 reduce-scatter.6.cloned.1.call-start
  205.9 5.4 fusion.23
  211.3 0.0 reduce-scatter.6.cloned.1.call-update
  211.3 0.0 reduce-scatter.10.cloned.1.call-start
  211.4 74.0 %reduce-scatter.8.cloned.1.call-done = f32[32,512]{1,0:T(8,128)} async-done(((f32[512,512]{1,0:T(8,128)}), f32[32,512]{1,0:T(8,128)}) %reduce-scatter.8.cloned.1.call-update) | async-done | bytes 65552 | tf_op jit(solution)/shard_map/reduce_scatter | solution.py:140
  285.4 1.0 multiply_reduce_fusion.2
  286.4 3.6 convolution_bitcast_fusion
  290.0 93.3 %reduce-scatter.6.cloned.1.call-done = f32[128,512]{1,0:T(8,128)} async-done(((f32[2048,512]{1,0:T(8,128)}), f32[128,512]{1,0:T(8,128)}) %reduce-scatter.6.cloned.1.call-update) | async-done | bytes 262160 | tf_op jit(solution)/shard_map/reduce_scatter | solution.py:139
  383.3 1.3 multiply_reduce_fusion
  384.6 1.8 convolution_bitcast_fusion.1
  386.4 3.8 pad_maximum_fusion
  390.2 9.3 copy.16
  399.5 0.0 reduce-scatter.10.cloned.1.call-update
  399.5 0.6 dynamic-slice_subtract_fusion
  400.1 1281.9 %reduce-scatter.10.cloned.1.call-done = f32[8,1024]{1,0:T(8,128)} async-done(((f32[2048,1024]{1,0:T(8,128)}), f32[8,1024]{1,0:T(8,128)}) %reduce-scatter.10.cloned.1.call-update) | async-done | bytes 32784
  1682.0 1.3 fusion.33
  (30 shorter events, 0.1 us)
Async XLA Ops:
  7.2 1.6 copy-start
  7.2 64.7 %all-gather.2.cloned.1.call-start = ((), (), s32[]{:S(2)}) async-start(), calls=%async_computation.3 | async-start | bytes 2228224 | tf_op jit(solution)/shard_map/all_gather | solution.py:31
  11.1 274.3 %reduce-scatter.8.cloned.1.call-start = ((), (), s32[]{:S(2)}) async-start(), calls=%async_computation.5 | async-start | bytes 1114112 | tf_op jit(solution)/shard_map/reduce_scatter | solution.py:140
  12.7 11.9 copy-start.7
  12.7 13.5 copy-start.5
  50.3 21.6 %copy-start.6 = (s32[2048]{0:T(1024)S(1)}, s32[2048]{0:T(1024)}, u32[]{:S(2)}) copy-start(s32[2048]{0:T(1024)} %param.17) | copy-start | bytes 24580
  170.5 1.9 copy-start.1
  173.9 3.0 copy-start.2
  178.8 1.9 copy-start.1
  182.3 3.1 copy-start.2
  205.8 177.5 %reduce-scatter.6.cloned.1.call-start = ((), (), s32[]{:S(2)}) async-start(), calls=%async_computation.4 | async-start | bytes 4456448 | tf_op jit(solution)/shard_map/reduce_scatter | solution.py:139
  211.3 173.3 %copy-start.4 = (bf16[128,2048]{1,0:T(8,128)(2,1)S(1)}, bf16[128,2048]{1,0:T(8,128)(2,1)}, u32[]{:S(2)}) copy-start(bf16[128,2048]{1,0:T(8,128)(2,1)} %param.11) | copy-start | bytes 1572868
  211.3 1470.7 %reduce-scatter.10.cloned.1.call-start = ((), (), s32[]{:S(2)}) async-start(), calls=%async_computation.6 | async-start | bytes 8421376
  383.3 3.1 copy-start.3
Sparse Core Ops, SparseCore 0:
  11.2 60.5 all-gather.1
  205.9 79.3 reduce-scatter.7
  289.5 93.8 reduce-scatter.5
  399.7 1282.3 reduce-scatter.9
where the time goes:
time: 1690 us
  waiting for transfers between devices  1460 us (86%)
  blocking collectives  104 us (6%)
  local copies, waits for them, and re-layouts  39.7 us (2%)
  other arithmetic  39.1 us (2%)
  matrix products  25 us (1%)
    unnamed x5, waiting for transfers between devices  1280 us
    reduce_scatter x1, waiting for transfers between devices, local(): lax.psum_scatter(query_grad, 'ia', scatter_dimension=0, tiled=True)  93.3 us
    psum x1, blocking collectives, local(): totals, target_score = lax.psum((partial_sums, target_part), 'ia')  81.9 us
    reduce_scatter x1, waiting for transfers between devices, local(): lax.psum_scatter(item_grad, 'pb', scatter_dimension=0, tiled=True)  74 us
  transfers between devices with their start and end apart: 4, of which 4 were waited for; matrix products, arithmetic and copies ran while one was open for 2% of the time, Pallas kernels for 0%

commit v1 on v0

v1 whole, which is shorter than its diff:
```python
import functools

import jax
import jax.numpy as jnp
from jax import lax
from jax.experimental import pallas as pl
from jax.experimental.pallas import tpu as pltpu
from jax.sharding import Mesh, PartitionSpec as P

AXES = ("y", "zl", "c", "zh", "x")
EMBED = 512
TOWER = 2048
EPS = 1e-06
TEMP = 0.05
SCALE = 1.0 / (EMBED * TEMP)
BF = jnp.bfloat16
F32 = jnp.float32


def rotation(size, step):
    return [(i, (i + step) % size) for i in range(size)]


def shift(value, step):
    return lax.ppermute(value, "x", rotation(4, step))


def swap(value):
    return lax.ppermute(value, "c", rotation(2, 1))


def spread(value, axes, size):
    return lax.all_to_all(jnp.broadcast_to(value[None], (size,) + value.shape), axes, 0, 0, tiled=True)


VM = functools.partial(pl.BlockSpec, memory_space=pltpu.VMEM)
SM = functools.partial(pl.BlockSpec, memory_space=pltpu.SMEM)


def call(body, outs, ins, scratch=(), flops=0, smem=0):
    return pl.pallas_call(
        body,
        out_shape=tuple(jax.ShapeDtypeStruct(s, d) for s, d in outs),
        in_specs=[SM()] * smem + [VM()] * (len(ins) - smem),
        out_specs=tuple(VM() for _ in outs),
        scratch_shapes=list(scratch),
        compiler_params=pltpu.CompilerParams(vmem_limit_bytes=48 * 1024 * 1024),
        cost_estimate=pl.CostEstimate(flops=flops, bytes_accessed=4 << 20, transcendentals=0),
    )(*ins)


def tower_body(hidden_ref, weight_ref, raw_ref, unit_ref):
    raw = jnp.dot(hidden_ref[...], weight_ref[...], preferred_element_type=F32)
    raw_ref[...] = raw
    unit_ref[...] = (raw * lax.rsqrt(jnp.mean(raw * raw, axis=-1, keepdims=True) + EPS)).astype(BF)


def tower(hidden, weight):
    rows = hidden.shape[0]
    return call(
        tower_body,
        [((rows, EMBED), F32), ((rows, EMBED), BF)],
        [hidden, weight],
        flops=2 * rows * TOWER * EMBED,
    )


def picker(target_x, own_c, relative_c):
    n = lax.broadcasted_iota(jnp.int32, (1, 128), 1)
    k, zh, zl, y_lo = n & 7, (n >> 3) & 3, (n >> 5) & 1, (n >> 6) & 1
    core = own_c if relative_c == 0 else 1 - own_c
    source = ((((y_lo * 2 + zl) * 2 + core) * 4 + zh) * 4 + target_x) * 8 + k
    rows = lax.broadcasted_iota(jnp.int32, (1024, 128), 0)
    return jnp.where(rows == source, 1.0, 0.0).astype(BF)


def pick_columns(hidden_ref, out_ref, target_x, own_c):
    for relative_c in range(2):
        chosen = picker(target_x, own_c, relative_c)
        for y_hi in range(2):
            part = jnp.dot(
                hidden_ref[:, y_hi * 1024 : (y_hi + 1) * 1024], chosen, preferred_element_type=F32
            )
            start = relative_c * 256 + y_hi * 128
            out_ref[:, start : start + 128] = part.astype(BF)


def pick_query_body(place_ref, hidden_ref, *out_refs):
    for step in range(4):
        target_x = lax.rem(place_ref[0] + step, 4)
        pick_columns(hidden_ref, out_refs[step], target_x, place_ref[1])


def pick_item_body(place_ref, h0, h1, h2, h3, out_ref):
    for step, ref in enumerate((h0, h1, h2, h3)):
        pick_columns(ref, out_ref.at[step * 32 : (step + 1) * 32, :], place_ref[0], place_ref[1])


CHUNK = 256


def score_body(place_ref, q0, q1, q2, q3, own_ref, other_ref, logs_ref, listed_ref, hit_ref, exp_ref, sums_ref, query_ref):
    for step, ref in enumerate((q0, q1, q2, q3)):
        at = lax.rem(place_ref[0] + 4 - step, 4) * 128
        query_ref[pl.ds(pl.multiple_of(at, 128), 128), :] = ref[...]
    queries = query_ref[...]
    hit = hit_ref[...]
    total = jnp.zeros((1, 512), F32)
    target = jnp.zeros((1, 512), F32)
    for chunk in range(2048 // CHUNK):
        source, at = (own_ref, chunk * CHUNK) if chunk < 1024 // CHUNK else (other_ref, chunk * CHUNK - 1024)
        items = source[at : at + CHUNK, :]
        rows = slice(chunk * CHUNK, (chunk + 1) * CHUNK)
        dots = lax.dot_general(items, queries, (((1,), (1,)), ((), ())), preferred_element_type=F32)
        scores = dots * SCALE - logs_ref[rows, :]
        ids = lax.broadcasted_iota(jnp.int32, (CHUNK, 512), 0) + chunk * CHUNK
        mine = ids == hit
        live = jnp.where(mine | (listed_ref[rows, :] > 0), jnp.exp(scores), 0.0)
        exp_ref[rows, :] = live.astype(BF)
        total += jnp.sum(live, axis=0, keepdims=True)
        target += jnp.sum(jnp.where(mine, scores, 0.0), axis=0, keepdims=True)
    sums_ref[0:1, :] = total
    sums_ref[1:2, :] = target


def shadow_body(hit_ref, exp_ref, own_ref, other_ref, query_ref, up_ref, hot_ref, pull_ref):
    hit = hit_ref[...]
    queries = query_ref[...]
    for chunk in range(2048 // CHUNK):
        source, at = (own_ref, chunk * CHUNK) if chunk < 1024 // CHUNK else (other_ref, chunk * CHUNK - 1024)
        items = source[at : at + CHUNK, :]
        rows = slice(chunk * CHUNK, (chunk + 1) * CHUNK)
        ids = lax.broadcasted_iota(jnp.int32, (CHUNK, 512), 0) + chunk * CHUNK
        mine = jnp.where(ids == hit, 1.0, 0.0).astype(BF)
        pull_ref[rows, :] = jnp.dot(mine, queries, preferred_element_type=F32)
        up = lax.dot_general(exp_ref[rows, :], items, (((0,), (0,)), ((), ())), preferred_element_type=F32)
        hot = lax.dot_general(mine, items, (((0,), (0,)), ((), ())), preferred_element_type=F32)
        if chunk == 0:
            up_ref[...] = up
            hot_ref[...] = hot
        else:
            up_ref[...] += up
            hot_ref[...] += hot


def inverse_column(s0, s1, s2, s3):
    total = s0[0:1, :] + s1[0:1, :] + s2[0:1, :] + s3[0:1, :]
    inverse = jnp.broadcast_to(1.0 / total, (128, 512))
    return jnp.transpose(inverse)[:, 0:1]


def item_grad_body(s0, s1, s2, s3, exp_ref, query_ref, pull_ref, keep_ref, send_ref):
    scaled = (query_ref[...].astype(F32) * inverse_column(s0, s1, s2, s3)).astype(BF)
    for chunk in range(2048 // CHUNK):
        rows = slice(chunk * CHUNK, (chunk + 1) * CHUNK)
        part = jnp.dot(exp_ref[rows, :], scaled, preferred_element_type=F32) - pull_ref[rows, :]
        if chunk < 1024 // CHUNK:
            keep_ref[rows, :] = part
        else:
            send_ref[rows.start - 1024 : rows.stop - 1024, :] = part.astype(BF)


def query_grad_body(place_ref, s0, s1, s2, s3, up_ref, hot_ref, loss_ref, own_ref, v1, v2, v3):
    inverse = inverse_column(s0, s1, s2, s3)
    total = s0[0:1, :] + s1[0:1, :] + s2[0:1, :] + s3[0:1, :]
    target = s0[1:2, :] + s1[1:2, :] + s2[1:2, :] + s3[1:2, :]
    loss_ref[...] = jnp.log(total) - target
    up_ref_value = up_ref[...] * inverse - hot_ref[...]
    hot_ref[...] = up_ref_value
    for step, ref in enumerate((own_ref, v1, v2, v3)):
        at = pl.multiple_of(lax.rem(place_ref[0] + step, 4) * 128, 128)
        ref[...] = hot_ref[pl.ds(at, 128), :].astype(ref.dtype)


def back_body(raw_ref, *refs):
    out_ref = refs[-1]
    grad = refs[0][...].astype(F32)
    for ref in refs[1:-1]:
        grad = grad + ref[...].astype(F32)
    grad = grad * SCALE
    raw = raw_ref[...]
    factor = lax.rsqrt(jnp.mean(raw * raw, axis=-1, keepdims=True) + EPS)
    unit = raw * factor
    out_ref[...] = (factor * (grad - unit * jnp.mean(unit * grad, axis=-1, keepdims=True))).astype(BF)


def back_stack_body(raw_ref, grads_ref, out_ref):
    grad = grads_ref[0].astype(F32)
    for part in range(1, grads_ref.shape[0]):
        grad = grad + grads_ref[part].astype(F32)
    grad = grad * SCALE
    raw = raw_ref[...]
    factor = lax.rsqrt(jnp.mean(raw * raw, axis=-1, keepdims=True) + EPS)
    unit = raw * factor
    out_ref[...] = (factor * (grad - unit * jnp.mean(unit * grad, axis=-1, keepdims=True))).astype(BF)


def last_body(*refs):
    hq, bq, hi, bi, (keep_ref, send_ref) = refs[0:4], refs[4:8], refs[8], refs[9:13], refs[13:15]
    query = item = None
    for step in range(4):
        part = lax.dot_general(hq[step][...], bq[step][...], (((0,), (0,)), ((), ())), preferred_element_type=F32)
        query = part if query is None else query + part
        part = lax.dot_general(
            hi[step * 32 : (step + 1) * 32, :], bi[step][...], (((0,), (0,)), ((), ())), preferred_element_type=F32
        )
        item = part if item is None else item + part
    keep_ref[:, 0:EMBED] = query[0:256]
    keep_ref[:, EMBED:] = item[0:256]
    send_ref[:, 0:EMBED] = query[256:512].astype(BF)
    send_ref[:, EMBED:] = item[256:512].astype(BF)


def add_body(a_ref, b_ref, out_ref):
    out_ref[...] = (a_ref[...].astype(F32) + b_ref[...].astype(F32)).astype(out_ref.dtype)


def add(a, b, dtype):
    return call(add_body, [(a.shape, dtype)], [a, b])[0]


def add_stack_body(parts_ref, out_ref):
    total = parts_ref[0].astype(F32)
    for part in range(1, parts_ref.shape[0]):
        total = total + parts_ref[part].astype(F32)
    out_ref[...] = total.astype(out_ref.dtype)


def add_stack(parts, dtype):
    return call(add_stack_body, [(parts.shape[1:], dtype)], [parts])[0]


def local(query_hidden, item_hidden, query_weight, item_weight, tile_list, item_counts, positives):
    my_x, my_c, my_zh = lax.axis_index("x"), lax.axis_index("c"), lax.axis_index("zh")
    place = jnp.stack([my_x, my_c]).astype(jnp.int32)

    item_raw, item_unit = tower(item_hidden, item_weight)
    query_raw, query_unit = tower(query_hidden, query_weight)
    queries = [query_unit] + [shift(query_unit, k) for k in (1, 2, 3)]

    z_items = spread(item_unit, ("zl", "zh"), 8)
    own_items = spread(z_items.reshape(256, EMBED), "y", 4).reshape(1024, EMBED)
    other_items = swap(own_items)

    hidden_items = [item_hidden] + [shift(item_hidden, k) for k in (1, 2, 3)]
    picked = call(
        pick_query_body, [((128, EMBED), BF)] * 4, [place, query_hidden], smem=1, flops=2 * 128 * 2048 * 512
    )
    hidden_queries = [picked[0]] + [shift(picked[k], k) for k in (1, 2, 3)]
    hidden_items = call(
        pick_item_body, [((128, EMBED), BF)], [place] + hidden_items, smem=1, flops=2 * 128 * 1024 * 512
    )[0]

    counts = item_counts.reshape(4, 4, 4, 2, 2, 32)
    counts = lax.dynamic_index_in_dim(counts, my_x, 1, keepdims=False)
    counts = counts.transpose(3, 1, 2, 0, 4)
    counts = jnp.where(my_c == 0, counts, counts[::-1])
    logs = jnp.log(counts.astype(F32)).reshape(2048, 1)
    row_list = lax.dynamic_index_in_dim(tile_list, my_zh, 0, keepdims=False)
    blocks = jnp.arange(4, dtype=jnp.int32) * 4 + my_x
    listed = jnp.any(row_list[None, :] == blocks[:, None], axis=1)
    listed = jnp.broadcast_to(listed.astype(F32)[None, :, None], (16, 4, 32)).reshape(2048, 1)
    wanted = lax.dynamic_slice_in_dim(positives, my_zh * 512, 512, 0).reshape(1, 512)
    block, within = wanted >> 9, wanted & 511
    order = ((((within >> 5) & 1) ^ my_c) << 10) | ((within >> 6) << 7) | ((block >> 2) << 5) | (within & 31)
    hit = jnp.where((block & 3) == my_x, order, -1)

    exps, sums, query_rows = call(
        score_body,
        [((2048, 512), BF), ((2, 512), F32), ((512, EMBED), BF)],
        [place, *queries, own_items, other_items, logs, listed, hit],
        smem=1,
        flops=2 * 2048 * 512 * 512,
    )
    all_sums = [sums] + [shift(sums, k) for k in (1, 2, 3)]
    up, hot, pull = call(
        shadow_body,
        [((512, EMBED), F32), ((512, EMBED), F32), ((2048, EMBED), F32)],
        [hit, exps, own_items, other_items, query_rows],
        flops=6 * 2048 * 512 * 512,
    )
    keep, send = call(
        item_grad_body,
        [((1024, EMBED), F32), ((1024, EMBED), BF)],
        [*all_sums, exps, query_rows, pull],
        flops=2 * 2048 * 512 * 512,
    )
    came = swap(send)
    losses, v0, v1, v2, v3 = call(
        query_grad_body,
        [((1, 512), F32), ((128, EMBED), F32)] + [((128, EMBED), BF)] * 3,
        [place, *all_sums, up, hot],
        smem=1,
        flops=1 << 20,
    )
    losses = lax.dynamic_slice_in_dim(losses.reshape(512), my_x * 128, 128, 0)
    query_parts = [v0, shift(v1, 1), shift(v2, 2), shift(v3, 3)]
    query_back = call(back_body, [((128, EMBED), BF)], [query_raw, *query_parts])[0]
    query_backs = [query_back] + [shift(query_back, k) for k in (1, 2, 3)]

    item_part = add(keep, came, BF)
    item_part = lax.all_to_all(item_part.reshape(4, 256, EMBED), "y", 0, 0, tiled=True)
    item_part = add_stack(item_part, BF)
    item_part = lax.all_to_all(item_part.reshape(8, 32, EMBED), ("zl", "zh"), 0, 0, tiled=True)
    item_back = call(back_stack_body, [((32, EMBED), BF)], [item_raw, item_part])[0]
    item_backs = [item_back] + [shift(item_back, k) for k in (1, 2, 3)]

    keep, send = call(
        last_body,
        [((256, 2 * EMBED), F32), ((256, 2 * EMBED), BF)],
        [*hidden_queries, *query_backs, hidden_items, *item_backs],
        flops=2 * 640 * 512 * 512,
    )
    part = add(keep, swap(send), BF)
    part = lax.all_to_all(part.reshape(4, 64, 2 * EMBED), "y", 0, 0, tiled=True)
    part = add_stack(part, BF)
    part = lax.all_to_all(part.reshape(8, 8, 2 * EMBED), ("zl", "zh"), 0, 0, tiled=True)
    grads = add_stack(part, F32)
    return (losses, grads[:, :EMBED], grads[:, EMBED:])


def solution(mesh):
    inner = Mesh(mesh.devices.reshape(4, 2, 2, 4, 4), AXES)
    pb, ia = ("y", "zl", "c"), ("zh", "x")
    placed = (P(pb + ia, None), P(ia + pb, None), P(), P(), P(pb, None), P(), P(pb))
    return jax.shard_map(
        local,
        mesh=inner,
        in_specs=placed,
        out_specs=(P(pb + ia), P(pb + ia, None), P(pb + ia, None)),
        check_vma=False,
    )
```

time: 1690 us -> 164 us (0.10)
  waiting for transfers between devices: 1460 us -> 18.1 us
  starting transfers between devices: 0.16 us -> 43.9 us
  blocking collectives: 104 us -> 64.1 us
  other arithmetic: 39.1 us -> 1.06 us
  local copies, waits for them, and re-layouts: 39.7 us -> 8.13 us
  Pallas kernels: 0 us -> 25.3 us
  matrix products: 25 us -> 0 us
    unnamed x5 -> x0, waiting for transfers between devices: 1280 us -> none
    reduce_scatter x2 -> x0, waiting for transfers between devices: 167 us -> none  [the longest x1 93.3 us: local(): lax.psum_scatter(query_grad, 'ia', scatter_dimension=0, tiled=True)]
    psum x1 -> x0, blocking collectives: 81.9 us -> none  [local(): totals, target_score = lax.psum((partial_sums, target_part), 'ia')]
    all_to_all x0 -> x4, blocking collectives: none -> 64.1 us  [the longest x2 33.5 us: spread(): lax.all_to_all(jnp.broadcast_to(value[None], (size,) + value.shape), axes...]
    ppermute x0 -> x24, starting transfers between devices: none -> 31.2 us  [the longest x21 31 us: shift(): return lax.ppermute(value, 'x', rotation(4, step))]
    pallas_call x0 -> x16, Pallas kernels: none -> 25.3 us  [call(): pl.pallas_call(body, out_shape=tuple((jax.ShapeDtypeStruct(s, d) for s, d...]
    dot_general x12 -> x0, matrix products: 25 us -> none  [the longest x4 6.72 us: tile_weights(): lax.dot_general(query_tile, item_tile, (((1,), (1,)), ((), ())), preferre...]
    all_gather x1 -> x0, blocking collectives: 21.9 us -> none  [local(): items = lax.all_gather(item_own, 'pb', axis=0, tiled=True)]
  transfers between devices with their start and end apart: 4 -> 26, of which waited for: 4 -> 10; matrix products, arithmetic and copies ran while one was open for 2% -> 3% of each run, Pallas kernels for 0% -> 8%
where the time goes in v1:
time: 164 us; the launch traced here: 161 us
  blocking collectives  64.1 us (39%)
  starting transfers between devices  43.9 us (27%)
  Pallas kernels  25.3 us (15%)
  waiting for transfers between devices  18.1 us (11%)
  local copies, waits for them, and re-layouts  8.13 us (5%)
    all_to_all x2, blocking collectives, spread(): lax.all_to_all(jnp.broadcast_to(value[None], (size,) + value.shape), axes...  33.5 us
    ppermute x21, starting transfers between devices, shift(): return lax.ppermute(value, 'x', rotation(4, step))  31 us
    pallas_call x16, Pallas kernels, call(): pl.pallas_call(body, out_shape=tuple((jax.ShapeDtypeStruct(s, d) for s, d...  25.3 us
    all_to_all x1, blocking collectives, local(): lax.all_to_all(item_part.reshape(4, 256, EMBED), 'y', 0, 0, tiled=True)  18.1 us
    all_to_all x1, blocking collectives, local(): part = lax.all_to_all(part.reshape(4, 64, 2 * EMBED), 'y', 0, 0, tiled=True)  12.5 us
    all_to_all x1, waiting for transfers between devices, local(): lax.all_to_all(part.reshape(8, 8, 2 * EMBED), ('zl', 'zh'), 0, 0, tiled=T...  7.44 us
    all_to_all x1, starting transfers between devices, local(): lax.all_to_all(part.reshape(8, 8, 2 * EMBED), ('zl', 'zh'), 0, 0, tiled=T...  6.92 us
    ppermute x21, waiting for transfers between devices, shift(): return lax.ppermute(value, 'x', rotation(4, step))  6.12 us
  transfers between devices with their start and end apart: 26, of which 10 were waited for; matrix products, arithmetic and copies ran while one was open for 3% of the time, Pallas kernels for 8%

profile of v1, /device:TPU:0, one launch (start us, length us, event | category | flops | bytes accessed | tf_op | source)
XLA Modules:
  0.0 161.5 jit_solution(10798979400756594641)
XLA Ops:
  0.7 1.6 copy-done.2
  2.2 0.9 copy-done.6
  3.1 0.6 shard_map.95
  3.7 0.6 copy-done.8
  4.4 16.0 %all_to_all.30 = bf16[8,32,512]{2,1,0:T(8,128)(2,1)S(1)} all-to-all(bf16[8,32,512]{2,1,0:T(8,128)(2,1)S(1)} %broadcast_in_dim.11), channel_id=1, replica_groups=mesh['y'=4,'zl'=2,'c'=2,'zh'=4,'x'=4] {'zl','zh'}, dimensions={0} | all-to-all | bytes 524288 | tf_op jit(solution)/shard_map/all_to_all | solution.py:33
  20.5 17.5 %all_to_all.31 = bf16[4,256,512]{2,1,0:T(8,128)(2,1)S(1)} all-to-all(bf16[4,256,512]{2,1,0:T(8,128)(2,1)S(1)} %broadcast_in_dim.13), channel_id=1, replica_groups=mesh['y'=4,'zl'=2,'c'=2,'zh'=4,'x'=4] {'y'}, dimensions={0} | all-to-all | bytes 2097152 | tf_op jit(solution)/shard_map/all_to_all | solution.py:33
  38.0 0.5 shard_map.94
  38.5 1.6 collective-permute-start
  40.1 2.7 %collective-permute-start.1 = (bf16[128,512]{1,0:T(8,128)(2,1)S(1)}, bf16[128,512]{1,0:T(8,128)(2,1)}, u32[]{:S(2)}, u32[]{:S(2)}) collective-permute-start(bf16[128,512]{1,0:T(8,128)(2,1)S(1)} %get-tuple-element.26.q0), channel_id=1, source_target_pairs={{0,2},{1,3},{2,0},{3,1},{4,6},{5,7},{6,4},{7,5},{8,10},{9,11},{10,... | collective-permute-start | bytes 393224 | tf_op jit(solution)/shard_map/ppermute | solution.py:25
  42.8 1.4 collective-permute-start.2
  44.3 0.1 reshape.61
  44.5 0.2 compare_reduce_fusion
  44.8 1.1 reshape.68.logs_ref
  45.9 0.7 broadcast_in_dim.28
  46.6 1.8 %reshape.69.listed_ref = f32[2048,1]{1,0:T(8,128)S(1)} reshape(f32[16,4,32]{2,1,0:T(4,128)} %broadcast_in_dim.28) | data formatting | bytes 16384 | tf_op jit(solution)/shard_map/reshape | solution.py:262
  48.4 0.8 or_select_fusion
  49.2 0.4 collective-permute-done.1.q2
  49.6 4.9 %shard_map.96 = (bf16[2048,512]{1,0:T(8,128)(2,1)}, f32[2,512]{1,0:T(2,128)S(1)}, bf16[512,512]{1,0:T(8,128)(2,1)S(1)}) custom-call(s32[2]{0:T(128)S(1)} %pad_add_fusion.place_ref, bf16[128,512]{1,0:T(8,128)(2,1)S(1)} %get-tuple-element.26.q0, bf16[128,512]{1,0:T(8,128)(2,1)} %collective-permute-done.q1, bf16[128,512]{1,0:T(8,128)(2,1)} %collective-permute-done.1.q2, ...), custom_call_target="tpu_custom_call" | custom-call | flops 1073741824 | bytes 4194304 | tf_op jit(solution)/shard_map/pallas_call | solution.py:41
  54.5 1.3 collective-permute-start.4
  55.9 2.4 %collective-permute-start.5 = (f32[2,512]{1,0:T(2,128)S(1)}, f32[2,512]{1,0:T(2,128)S(1)}, u32[]{:S(2)}, u32[]{:S(2)}) collective-permute-start(f32[2,512]{1,0:T(2,128)S(1)} %get-tuple-element.28.s0), channel_id=1, source_target_pairs={{0,2},{1,3},{2,0},{3,1},{4,6},{5,7},{6,4},{7,5},{8,10},{9,11},{10,... | collective-permute-start | bytes 12296 | tf_op jit(solution)/shard_map/ppermute | solution.py:25
  58.3 1.6 collective-permute-start.6
  59.8 7.2 %shard_map.97 = (f32[512,512]{1,0:T(8,128)S(1)}, f32[512,512]{1,0:T(8,128)S(1)}, f32[2048,512]{1,0:T(8,128)}) custom-call(s32[1,512]{1,0:T(1,128)S(1)} %bitcast.24, bf16[2048,512]{1,0:T(8,128)(2,1)} %get-tuple-element.29.exp_ref, bf16[1024,512]{1,0:T(8,128)(2,1)S(1)} %bitcast.20, bf16[1024,512]{1,0:T(8,128)(2,1)} %collective-permute-done.3.other_ref, ...), custom_call_target="tpu_custom_call" | custom-call | flops 3221225472 | bytes 4194304 | tf_op jit(solution)/shard_map/pallas_call | solution.py:41
  67.1 3.7 %shard_map.102 = (f32[1024,512]{1,0:T(8,128)S(1)}, bf16[1024,512]{1,0:T(8,128)(2,1)S(1)}) custom-call(f32[2,512]{1,0:T(2,128)S(1)} %get-tuple-element.28.s0, f32[2,512]{1,0:T(2,128)S(1)} %collective-permute-done.4.s1, f32[2,512]{1,0:T(2,128)S(1)} %collective-permute-done.5.s2, f32[2,512]{1,0:T(2,128)S(1)} %collective-permute-done.6.s3, ...), custom_call_target="tpu_custom_call" | custom-call | flops 1073741824 | bytes 4194304 | tf_op jit(solution)/shard_map/pallas_call | solution.py:41
  70.8 0.1 collective-permute-start.19
  70.9 2.6 %collective-permute-done.19.b_ref = bf16[1024,512]{1,0:T(8,128)(2,1)S(1)} collective-permute-done((bf16[1024,512]{1,0:T(8,128)(2,1)S(1)}, bf16[1024,512]{1,0:T(8,128)(2,1)S(1)}, u32[]{:S(2)}, u32[]{:S(2)}) %collective-permute-start.19) | collective-permute-done | bytes 1048608 | tf_op jit(solution)/shard_map/ppermute | solution.py:29
  73.5 0.3 shard_map.103
  73.8 18.1 %all_to_all.32.parts_ref = bf16[4,256,512]{2,1,0:T(8,128)(2,1)S(1)} all-to-all(bf16[4,256,512]{2,1,0:T(8,128)(2,1)S(1)} %bitcast.21), channel_id=1, replica_groups=mesh['y'=4,'zl'=2,'c'=2,'zh'=4,'x'=4] {'y'}, dimensions={0} | all-to-all | bytes 2097152 | tf_op jit(solution)/shard_map/all_to_all | solution.py:302
  91.9 0.8 shard_map.104
  92.8 5.8 %all-to-all-start.3 = ((bf16[8,32,512]{2,1,0:T(8,128)(2,1)}), bf16[8,32,512]{2,1,0:T(8,128)(2,1)S(1)}, u32[]{:S(2)}, u32[]{:S(2)}) async-start(bf16[8,32,512]{2,1,0:T(8,128)(2,1)} %bitcast.10), calls=%async_computation.3 | async-start | bytes 524288 | tf_op jit(solution)/shard_map/all_to_all | solution.py:304
  98.5 0.9 shard_map.98
  99.4 0.5 collective-permute-start.10
  99.9 1.1 collective-permute-start.11
  101.1 1.9 %collective-permute-start.12 = (bf16[128,512]{1,0:T(8,128)(2,1)S(1)}, bf16[128,512]{1,0:T(8,128)(2,1)S(1)}, u32[]{:S(2)}, u32[]{:S(2)}) collective-permute-start(bf16[128,512]{1,0:T(8,128)(2,1)S(1)} %get-tuple-element.42), channel_id=1, source_target_pairs={{0,3},{1,0},{2,1},{3,2},{4,7},{5,4},{6,5},{7,6},{8,11},{9,8},{10,9... | collective-permute-start | bytes 393224 | tf_op jit(solution)/shard_map/ppermute | solution.py:25
  103.0 2.1 %shard_map.99 = (bf16[128,512]{1,0:T(8,128)(2,1)S(1)}, bf16[128,512]{1,0:T(8,128)(2,1)S(1)}, bf16[128,512]{1,0:T(8,128)(2,1)S(1)}, bf16[128,512]{1,0:T(8,128)(2,1)S(1)}) custom-call(s32[2]{0:T(128)S(1)} %pad_add_fusion.place_ref, bf16[128,2048]{1,0:T(8,128)(2,1)S(1)} %copy-done.5), custom_call_target="tpu_custom_call" | custom-call | flops 268435456 | bytes 4194304 | tf_op jit(solution)/shard_map/pallas_call | solution.py:41
  105.1 0.7 collective-permute-start.7
  105.8 2.2 %collective-permute-start.8 = (bf16[128,512]{1,0:T(8,128)(2,1)S(1)}, bf16[128,512]{1,0:T(8,128)(2,1)S(1)}, u32[]{:S(2)}, u32[]{:S(2)}) collective-permute-start(bf16[128,512]{1,0:T(8,128)(2,1)S(1)} %get-tuple-element.36), channel_id=1, source_target_pairs={{0,2},{1,3},{2,0},{3,1},{4,6},{5,7},{6,4},{7,5},{8,10},{9,11},{10,... | collective-permute-start | bytes 393224 | tf_op jit(solution)/shard_map/ppermute | solution.py:25
  108.0 1.9 %collective-permute-done.10.refs_1_ = bf16[128,512]{1,0:T(8,128)(2,1)S(1)} collective-permute-done((bf16[128,512]{1,0:T(8,128)(2,1)S(1)}, bf16[128,512]{1,0:T(8,128)(2,1)S(1)}, u32[]{:S(2)}, u32[]{:S(2)}) %collective-permute-start.10) | collective-permute-done | bytes 131104 | tf_op jit(solution)/shard_map/ppermute | solution.py:25
  109.9 0.6 collective-permute-start.9
  110.5 1.4 collective-permute-start.16
  111.9 0.1 collective-permute-start.17
  112.1 0.2 shard_map.100.refs_4_
  112.3 0.7 collective-permute-done.7.refs_1_
  113.0 2.2 %collective-permute-start.18 = (bf16[32,2048]{1,0:T(8,128)(2,1)S(1)}, bf16[32,2048]{1,0:T(8,128)(2,1)S(1)}, u32[]{:S(2)}, u32[]{:S(2)}) collective-permute-start(bf16[32,2048]{1,0:T(8,128)(2,1)S(1)} %copy-done.7), channel_id=1, source_target_pairs={{0,3},{1,0},{2,1},{3,2},{4,7},{5,4},{6,5},{7,6},{8,11},{9,8},{10,9... | collective-permute-start | bytes 393224 | tf_op jit(solution)/shard_map/ppermute | solution.py:25
  115.2 0.6 collective-permute-start.13
  115.8 0.5 collective-permute-done.9.refs_3_
  116.3 3.3 %collective-permute-start.14 = (bf16[128,512]{1,0:T(8,128)(2,1)S(1)}, bf16[128,512]{1,0:T(8,128)(2,1)S(1)}, u32[]{:S(2)}, u32[]{:S(2)}) collective-permute-start(bf16[128,512]{1,0:T(8,128)(2,1)S(1)} %shard_map.100.refs_4_), channel_id=1, source_target_pairs={{0,2},{1,3},{2,0},{3,1},{4,6},{5,7},{6,4},{7,5},{8,10},{9,11},{10,... | collective-permute-start | bytes 393224 | tf_op jit(solution)/shard_map/ppermute | solution.py:25
  119.6 1.7 %collective-permute-done.16.h1 = bf16[32,2048]{1,0:T(8,128)(2,1)S(1)} collective-permute-done((bf16[32,2048]{1,0:T(8,128)(2,1)S(1)}, bf16[32,2048]{1,0:T(8,128)(2,1)S(1)}, u32[]{:S(2)}, u32[]{:S(2)}) %collective-permute-start.16) | collective-permute-done | bytes 131104 | tf_op jit(solution)/shard_map/ppermute | solution.py:25
  121.3 0.2 shard_map.105.refs_9_
  121.5 2.1 %collective-permute-start.20 = (bf16[32,512]{1,0:T(8,128)(2,1)S(1)}, bf16[32,512]{1,0:T(8,128)(2,1)S(1)}, u32[]{:S(2)}, u32[]{:S(2)}) collective-permute-start(bf16[32,512]{1,0:T(8,128)(2,1)S(1)} %shard_map.105.refs_9_), channel_id=1, source_target_pairs={{0,1},{1,2},{2,3},{3,0},{4,5},{5,6},{6,7},{7,4},{8,9},{9,10},{10,1... | collective-permute-start | bytes 98312 | tf_op jit(solution)/shard_map/ppermute | solution.py:25
  123.6 1.9 %collective-permute-start.21 = (bf16[32,512]{1,0:T(8,128)(2,1)S(1)}, bf16[32,512]{1,0:T(8,128)(2,1)S(1)}, u32[]{:S(2)}, u32[]{:S(2)}) collective-permute-start(bf16[32,512]{1,0:T(8,128)(2,1)S(1)} %shard_map.105.refs_9_), channel_id=1, source_target_pairs={{0,2},{1,3},{2,0},{3,1},{4,6},{5,7},{6,4},{7,5},{8,10},{9,11},{10,... | collective-permute-start | bytes 98312 | tf_op jit(solution)/shard_map/ppermute | solution.py:25
  125.5 1.4 collective-permute-start.22
  126.8 1.7 %shard_map.101.refs_8_ = bf16[128,512]{1,0:T(8,128)(2,1)S(1)} custom-call(s32[2]{0:T(128)S(1)} %pad_add_fusion.place_ref, bf16[32,2048]{1,0:T(8,128)(2,1)S(1)} %copy-done.7, bf16[32,2048]{1,0:T(8,128)(2,1)S(1)} %collective-permute-done.16.h1, bf16[32,2048]{1,0:T(8,128)(2,1)S(1)} %collective-permute-done.17.h2, bf16[32,2048]{1,0:T(8,128)(2,1)S(1)} %collective-permute-done.18.h3), custom_call_target="tpu_custom_call" | custom-call | flops 134217728 | bytes 4194304 | tf_op jit(solution)/shard_map/pallas_call | solution.py:41
  128.6 0.4 collective-permute-done.21.refs_11_
  129.0 0.4 collective-permute-done.22.refs_12_
  129.4 1.3 shard_map.106
  130.7 0.1 collective-permute-start.23
  130.8 1.9 %collective-permute-done.23.b_ref = bf16[256,1024]{1,0:T(8,128)(2,1)S(1)} collective-permute-done((bf16[256,1024]{1,0:T(8,128)(2,1)S(1)}, bf16[256,1024]{1,0:T(8,128)(2,1)S(1)}, u32[]{:S(2)}, u32[]{:S(2)}) %collective-permute-start.23) | collective-permute-done | bytes 524320 | tf_op jit(solution)/shard_map/ppermute | solution.py:29
  132.7 0.1 shard_map.107
  132.8 12.5 %all_to_all.33.parts_ref = bf16[4,64,1024]{2,1,0:T(8,128)(2,1)S(1)} all-to-all(bf16[4,64,1024]{2,1,0:T(8,128)(2,1)S(1)} %bitcast.22), channel_id=1, replica_groups=mesh['y'=4,'zl'=2,'c'=2,'zh'=4,'x'=4] {'y'}, dimensions={0} | all-to-all | bytes 1048576 | tf_op jit(solution)/shard_map/all_to_all | solution.py:315
  145.2 0.7 shard_map.108
  145.9 6.9 %all-to-all-start.5 = ((bf16[8,8,1024]{2,1,0:T(8,128)(2,1)}), bf16[8,8,1024]{2,1,0:T(8,128)(2,1)S(1)}, u32[]{:S(2)}, u32[]{:S(2)}) async-start(bf16[8,8,1024]{2,1,0:T(8,128)(2,1)} %bitcast.12), calls=%async_computation.5 | async-start | bytes 262144 | tf_op jit(solution)/shard_map/all_to_all | solution.py:317
  152.9 0.5 fusion.3
  153.4 7.4 %all-to-all-done.5.parts_ref = bf16[8,8,1024]{2,1,0:T(8,128)(2,1)S(1)} async-done(((bf16[8,8,1024]{2,1,0:T(8,128)(2,1)}), bf16[8,8,1024]{2,1,0:T(8,128)(2,1)S(1)}, u32[]{:S(2)}, u32[]{:S(2)}) %all-to-all-start.5) | async-done | bytes 131104 | tf_op jit(solution)/shard_map/all_to_all | solution.py:317
  160.8 0.6 fusion.4
  (47 shorter events, 0.4 us)
Async XLA Ops:
  0.6 43.8 %copy-start = (s32[4,8]{1,0:T(4,128)S(1)}, s32[4,8]{1,0:T(4,128)}, u32[]{:S(2)}) copy-start(s32[4,8]{1,0:T(4,128)} %param.11) | copy-start | bytes 388
  0.6 1.6 copy-start.2
  2.2 0.9 copy-start.6
  3.7 0.6 copy-start.8
  4.3 33.6 %copy-start.1 = (bf16[2048,512]{1,0:T(8,128)(2,1)S(1)}, bf16[2048,512]{1,0:T(8,128)(2,1)}, u32[]{:S(2)}) copy-start(bf16[2048,512]{1,0:T(8,128)(2,1)} %weight_ref.2) | copy-start | bytes 6291460
  4.3 33.6 %copy-start.4 = (bf16[128,2048]{1,0:T(8,128)(2,1)S(1)}, bf16[128,2048]{1,0:T(8,128)(2,1)}, u32[]{:S(2)}) copy-start(bf16[128,2048]{1,0:T(8,128)(2,1)} %hidden_ref.5) | copy-start | bytes 1572868
  20.5 23.8 %copy-start.10 = (s32[8192]{0:T(1024)S(1)}, s32[8192]{0:T(1024)}, u32[]{:S(2)}) copy-start(s32[8192]{0:T(1024)} %param.12) | copy-start | bytes 98308
  38.0 11.7 %collective-permute-start.3 = (bf16[1024,512]{1,0:T(8,128)(2,1)S(1)}, bf16[1024,512]{1,0:T(8,128)(2,1)}, u32[]{:S(2)}, u32[]{:S(2)}) collective-permute-start(bf16[1024,512]{1,0:T(8,128)(2,1)S(1)} %bitcast.18), channel_id=1, source_target_pairs={{0,16},{16,0},{1,17},{17,1},{2,18},{18,2},{3,19},{19,3},{4,20},{20... | collective-permute-start | bytes 3145736 | tf_op jit(solution)/shard_map/ppermute | solution.py:29
  38.5 10.7 %collective-permute-start = (bf16[128,512]{1,0:T(8,128)(2,1)S(1)}, bf16[128,512]{1,0:T(8,128)(2,1)}, u32[]{:S(2)}, u32[]{:S(2)}) collective-permute-start(bf16[128,512]{1,0:T(8,128)(2,1)S(1)} %get-tuple-element.26.q0), channel_id=1, source_target_pairs={{0,1},{1,2},{2,3},{3,0},{4,5},{5,6},{6,7},{7,4},{8,9},{9,10},{10,1... | collective-permute-start | bytes 393224 | tf_op jit(solution)/shard_map/ppermute | solution.py:25
  40.1 9.5 %collective-permute-start.1 = (bf16[128,512]{1,0:T(8,128)(2,1)S(1)}, bf16[128,512]{1,0:T(8,128)(2,1)}, u32[]{:S(2)}, u32[]{:S(2)}) collective-permute-start(bf16[128,512]{1,0:T(8,128)(2,1)S(1)} %get-tuple-element.26.q0), channel_id=1, source_target_pairs={{0,2},{1,3},{2,0},{3,1},{4,6},{5,7},{6,4},{7,5},{8,10},{9,11},{10,... | collective-permute-start | bytes 393224 | tf_op jit(solution)/shard_map/ppermute | solution.py:25
  42.8 6.8 %collective-permute-start.2 = (bf16[128,512]{1,0:T(8,128)(2,1)S(1)}, bf16[128,512]{1,0:T(8,128)(2,1)}, u32[]{:S(2)}, u32[]{:S(2)}) collective-permute-start(bf16[128,512]{1,0:T(8,128)(2,1)S(1)} %get-tuple-element.26.q0), channel_id=1, source_target_pairs={{0,3},{1,0},{2,1},{3,2},{4,7},{5,4},{6,5},{7,6},{8,11},{9,8},{10,9... | collective-permute-start | bytes 393224 | tf_op jit(solution)/shard_map/ppermute | solution.py:25
  54.5 12.5 %collective-permute-start.4 = (f32[2,512]{1,0:T(2,128)S(1)}, f32[2,512]{1,0:T(2,128)S(1)}, u32[]{:S(2)}, u32[]{:S(2)}) collective-permute-start(f32[2,512]{1,0:T(2,128)S(1)} %get-tuple-element.28.s0), channel_id=1, source_target_pairs={{0,1},{1,2},{2,3},{3,0},{4,5},{5,6},{6,7},{7,4},{8,9},{9,10},{10,1... | collective-permute-start | bytes 12296 | tf_op jit(solution)/shard_map/ppermute | solution.py:25
  55.9 11.2 %collective-permute-start.5 = (f32[2,512]{1,0:T(2,128)S(1)}, f32[2,512]{1,0:T(2,128)S(1)}, u32[]{:S(2)}, u32[]{:S(2)}) collective-permute-start(f32[2,512]{1,0:T(2,128)S(1)} %get-tuple-element.28.s0), channel_id=1, source_target_pairs={{0,2},{1,3},{2,0},{3,1},{4,6},{5,7},{6,4},{7,5},{8,10},{9,11},{10,... | collective-permute-start | bytes 12296 | tf_op jit(solution)/shard_map/ppermute | solution.py:25
  58.3 8.8 %collective-permute-start.6 = (f32[2,512]{1,0:T(2,128)S(1)}, f32[2,512]{1,0:T(2,128)S(1)}, u32[]{:S(2)}, u32[]{:S(2)}) collective-permute-start(f32[2,512]{1,0:T(2,128)S(1)} %get-tuple-element.28.s0), channel_id=1, source_target_pairs={{0,3},{1,0},{2,1},{3,2},{4,7},{5,4},{6,5},{7,6},{8,11},{9,8},{10,9... | collective-permute-start | bytes 12296 | tf_op jit(solution)/shard_map/ppermute | solution.py:25
  59.8 7.3 %copy-start.3 = (bf16[2048,512]{1,0:T(8,128)(2,1)S(1)}, bf16[2048,512]{1,0:T(8,128)(2,1)}, u32[]{:S(2)}) copy-start(bf16[2048,512]{1,0:T(8,128)(2,1)} %get-tuple-element.29.exp_ref) | copy-start | bytes 6291460
  70.8 2.7 %collective-permute-start.19 = (bf16[1024,512]{1,0:T(8,128)(2,1)S(1)}, bf16[1024,512]{1,0:T(8,128)(2,1)S(1)}, u32[]{:S(2)}, u32[]{:S(2)}) collective-permute-start(bf16[1024,512]{1,0:T(8,128)(2,1)S(1)} %get-tuple-element.46), channel_id=1, source_target_pairs={{0,16},{16,0},{1,17},{17,1},{2,18},{18,2},{3,19},{19,3},{4,20},{20... | collective-permute-start | bytes 3145736 | tf_op jit(solution)/shard_map/ppermute | solution.py:29
  91.9 11.1 %copy-start.5 = (bf16[128,2048]{1,0:T(8,128)(2,1)S(1)}, bf16[128,2048]{1,0:T(8,128)(2,1)}, u32[]{:S(2)}) copy-start(bf16[128,2048]{1,0:T(8,128)(2,1)} %hidden_ref.5) | copy-start | bytes 1572868
  92.8 17.8 %copy-start.7 = (bf16[32,2048]{1,0:T(8,128)(2,1)S(1)}, bf16[32,2048]{1,0:T(8,128)(2,1)}, u32[]{:S(2)}) copy-start(bf16[32,2048]{1,0:T(8,128)(2,1)} %h0.1) | copy-start | bytes 393220
  92.8 28.5 %all-to-all-start.3 = ((bf16[8,32,512]{2,1,0:T(8,128)(2,1)}), bf16[8,32,512]{2,1,0:T(8,128)(2,1)S(1)}, u32[]{:S(2)}, u32[]{:S(2)}) async-start(bf16[8,32,512]{2,1,0:T(8,128)(2,1)} %bitcast.10), calls=%async_computation.3 | async-start | bytes 524288 | tf_op jit(solution)/shard_map/all_to_all | solution.py:304
  98.5 22.8 %copy-start.9 = (f32[32,512]{1,0:T(8,128)S(1)}, f32[32,512]{1,0:T(8,128)}, u32[]{:S(2)}) copy-start(f32[32,512]{1,0:T(8,128)} %copy-done.8) | copy-start | bytes 196612
  99.4 10.5 %collective-permute-start.10 = (bf16[128,512]{1,0:T(8,128)(2,1)S(1)}, bf16[128,512]{1,0:T(8,128)(2,1)S(1)}, u32[]{:S(2)}, u32[]{:S(2)}) collective-permute-start(bf16[128,512]{1,0:T(8,128)(2,1)S(1)} %get-tuple-element.40), channel_id=1, source_target_pairs={{0,1},{1,2},{2,3},{3,0},{4,5},{5,6},{6,7},{7,4},{8,9},{9,10},{10,1... | collective-permute-start | bytes 393224 | tf_op jit(solution)/shard_map/ppermute | solution.py:25
  99.9 10.6 %collective-permute-start.11 = (bf16[128,512]{1,0:T(8,128)(2,1)S(1)}, bf16[128,512]{1,0:T(8,128)(2,1)S(1)}, u32[]{:S(2)}, u32[]{:S(2)}) collective-permute-start(bf16[128,512]{1,0:T(8,128)(2,1)S(1)} %get-tuple-element.41), channel_id=1, source_target_pairs={{0,2},{1,3},{2,0},{3,1},{4,6},{5,7},{6,4},{7,5},{8,10},{9,11},{10,... | collective-permute-start | bytes 393224 | tf_op jit(solution)/shard_map/ppermute | solution.py:25
  101.1 10.9 %collective-permute-start.12 = (bf16[128,512]{1,0:T(8,128)(2,1)S(1)}, bf16[128,512]{1,0:T(8,128)(2,1)S(1)}, u32[]{:S(2)}, u32[]{:S(2)}) collective-permute-start(bf16[128,512]{1,0:T(8,128)(2,1)S(1)} %get-tuple-element.42), channel_id=1, source_target_pairs={{0,3},{1,0},{2,1},{3,2},{4,7},{5,4},{6,5},{7,6},{8,11},{9,8},{10,9... | collective-permute-start | bytes 393224 | tf_op jit(solution)/shard_map/ppermute | solution.py:25
  105.1 7.9 %collective-permute-start.7 = (bf16[128,512]{1,0:T(8,128)(2,1)S(1)}, bf16[128,512]{1,0:T(8,128)(2,1)S(1)}, u32[]{:S(2)}, u32[]{:S(2)}) collective-permute-start(bf16[128,512]{1,0:T(8,128)(2,1)S(1)} %get-tuple-element.35), channel_id=1, source_target_pairs={{0,1},{1,2},{2,3},{3,0},{4,5},{5,6},{6,7},{7,4},{8,9},{9,10},{10,1... | collective-permute-start | bytes 393224 | tf_op jit(solution)/shard_map/ppermute | solution.py:25
  105.8 9.4 %collective-permute-start.8 = (bf16[128,512]{1,0:T(8,128)(2,1)S(1)}, bf16[128,512]{1,0:T(8,128)(2,1)S(1)}, u32[]{:S(2)}, u32[]{:S(2)}) collective-permute-start(bf16[128,512]{1,0:T(8,128)(2,1)S(1)} %get-tuple-element.36), channel_id=1, source_target_pairs={{0,2},{1,3},{2,0},{3,1},{4,6},{5,7},{6,4},{7,5},{8,10},{9,11},{10,... | collective-permute-start | bytes 393224 | tf_op jit(solution)/shard_map/ppermute | solution.py:25
  109.9 6.4 %collective-permute-start.9 = (bf16[128,512]{1,0:T(8,128)(2,1)S(1)}, bf16[128,512]{1,0:T(8,128)(2,1)S(1)}, u32[]{:S(2)}, u32[]{:S(2)}) collective-permute-start(bf16[128,512]{1,0:T(8,128)(2,1)S(1)} %get-tuple-element.37), channel_id=1, source_target_pairs={{0,3},{1,0},{2,1},{3,2},{4,7},{5,4},{6,5},{7,6},{8,11},{9,8},{10,9... | collective-permute-start | bytes 393224 | tf_op jit(solution)/shard_map/ppermute | solution.py:25
  110.5 10.8 %collective-permute-start.16 = (bf16[32,2048]{1,0:T(8,128)(2,1)S(1)}, bf16[32,2048]{1,0:T(8,128)(2,1)S(1)}, u32[]{:S(2)}, u32[]{:S(2)}) collective-permute-start(bf16[32,2048]{1,0:T(8,128)(2,1)S(1)} %copy-done.7), channel_id=1, source_target_pairs={{0,1},{1,2},{2,3},{3,0},{4,5},{5,6},{6,7},{7,4},{8,9},{9,10},{10,1... | collective-permute-start | bytes 393224 | tf_op jit(solution)/shard_map/ppermute | solution.py:25
  111.9 9.5 %collective-permute-start.17 = (bf16[32,2048]{1,0:T(8,128)(2,1)S(1)}, bf16[32,2048]{1,0:T(8,128)(2,1)S(1)}, u32[]{:S(2)}, u32[]{:S(2)}) collective-permute-start(bf16[32,2048]{1,0:T(8,128)(2,1)S(1)} %copy-done.7), channel_id=1, source_target_pairs={{0,2},{1,3},{2,0},{3,1},{4,6},{5,7},{6,4},{7,5},{8,10},{9,11},{10,... | collective-permute-start | bytes 393224 | tf_op jit(solution)/shard_map/ppermute | solution.py:25
  113.0 10.6 %collective-permute-start.18 = (bf16[32,2048]{1,0:T(8,128)(2,1)S(1)}, bf16[32,2048]{1,0:T(8,128)(2,1)S(1)}, u32[]{:S(2)}, u32[]{:S(2)}) collective-permute-start(bf16[32,2048]{1,0:T(8,128)(2,1)S(1)} %copy-done.7), channel_id=1, source_target_pairs={{0,3},{1,0},{2,1},{3,2},{4,7},{5,4},{6,5},{7,6},{8,11},{9,8},{10,9... | collective-permute-start | bytes 393224 | tf_op jit(solution)/shard_map/ppermute | solution.py:25
  115.2 10.3 %collective-permute-start.13 = (bf16[128,512]{1,0:T(8,128)(2,1)S(1)}, bf16[128,512]{1,0:T(8,128)(2,1)S(1)}, u32[]{:S(2)}, u32[]{:S(2)}) collective-permute-start(bf16[128,512]{1,0:T(8,128)(2,1)S(1)} %shard_map.100.refs_4_), channel_id=1, source_target_pairs={{0,1},{1,2},{2,3},{3,0},{4,5},{5,6},{6,7},{7,4},{8,9},{9,10},{10,1... | collective-permute-start | bytes 393224 | tf_op jit(solution)/shard_map/ppermute | solution.py:25
  116.3 12.2 %collective-permute-start.14 = (bf16[128,512]{1,0:T(8,128)(2,1)S(1)}, bf16[128,512]{1,0:T(8,128)(2,1)S(1)}, u32[]{:S(2)}, u32[]{:S(2)}) collective-permute-start(bf16[128,512]{1,0:T(8,128)(2,1)S(1)} %shard_map.100.refs_4_), channel_id=1, source_target_pairs={{0,2},{1,3},{2,0},{3,1},{4,6},{5,7},{6,4},{7,5},{8,10},{9,11},{10,... | collective-permute-start | bytes 393224 | tf_op jit(solution)/shard_map/ppermute | solution.py:25
  121.3 7.3 %collective-permute-start.15 = (bf16[128,512]{1,0:T(8,128)(2,1)S(1)}, bf16[128,512]{1,0:T(8,128)(2,1)S(1)}, u32[]{:S(2)}, u32[]{:S(2)}) collective-permute-start(bf16[128,512]{1,0:T(8,128)(2,1)S(1)} %shard_map.100.refs_4_), channel_id=1, source_target_pairs={{0,3},{1,0},{2,1},{3,2},{4,7},{5,4},{6,5},{7,6},{8,11},{9,8},{10,9... | collective-permute-start | bytes 393224 | tf_op jit(solution)/shard_map/ppermute | solution.py:25
  121.5 7.1 %collective-permute-start.20 = (bf16[32,512]{1,0:T(8,128)(2,1)S(1)}, bf16[32,512]{1,0:T(8,128)(2,1)S(1)}, u32[]{:S(2)}, u32[]{:S(2)}) collective-permute-start(bf16[32,512]{1,0:T(8,128)(2,1)S(1)} %shard_map.105.refs_9_), channel_id=1, source_target_pairs={{0,1},{1,2},{2,3},{3,0},{4,5},{5,6},{6,7},{7,4},{8,9},{9,10},{10,1... | collective-permute-start | bytes 98312 | tf_op jit(solution)/shard_map/ppermute | solution.py:25
  123.6 5.4 %collective-permute-start.21 = (bf16[32,512]{1,0:T(8,128)(2,1)S(1)}, bf16[32,512]{1,0:T(8,128)(2,1)S(1)}, u32[]{:S(2)}, u32[]{:S(2)}) collective-permute-start(bf16[32,512]{1,0:T(8,128)(2,1)S(1)} %shard_map.105.refs_9_), channel_id=1, source_target_pairs={{0,2},{1,3},{2,0},{3,1},{4,6},{5,7},{6,4},{7,5},{8,10},{9,11},{10,... | collective-permute-start | bytes 98312 | tf_op jit(solution)/shard_map/ppermute | solution.py:25
  125.5 3.9 %collective-permute-start.22 = (bf16[32,512]{1,0:T(8,128)(2,1)S(1)}, bf16[32,512]{1,0:T(8,128)(2,1)S(1)}, u32[]{:S(2)}, u32[]{:S(2)}) collective-permute-start(bf16[32,512]{1,0:T(8,128)(2,1)S(1)} %shard_map.105.refs_9_), channel_id=1, source_target_pairs={{0,3},{1,0},{2,1},{3,2},{4,7},{5,4},{6,5},{7,6},{8,11},{9,8},{10,9... | collective-permute-start | bytes 98312 | tf_op jit(solution)/shard_map/ppermute | solution.py:25
  130.7 2.0 %collective-permute-start.23 = (bf16[256,1024]{1,0:T(8,128)(2,1)S(1)}, bf16[256,1024]{1,0:T(8,128)(2,1)S(1)}, u32[]{:S(2)}, u32[]{:S(2)}) collective-permute-start(bf16[256,1024]{1,0:T(8,128)(2,1)S(1)} %get-tuple-element.48), channel_id=1, source_target_pairs={{0,16},{16,0},{1,17},{17,1},{2,18},{18,2},{3,19},{19,3},{4,20},{20... | collective-permute-start | bytes 1572872 | tf_op jit(solution)/shard_map/ppermute | solution.py:29
  145.9 14.9 %all-to-all-start.5 = ((bf16[8,8,1024]{2,1,0:T(8,128)(2,1)}), bf16[8,8,1024]{2,1,0:T(8,128)(2,1)S(1)}, u32[]{:S(2)}, u32[]{:S(2)}) async-start(bf16[8,8,1024]{2,1,0:T(8,128)(2,1)} %bitcast.12), calls=%async_computation.5 | async-start | bytes 262144 | tf_op jit(solution)/shard_map/all_to_all | solution.py:317

commit v2 on v0

v2 whole, which is shorter than its diff:
```python
import functools

import jax
import jax.numpy as jnp
from jax import lax
from jax.experimental import pallas as pl
from jax.experimental.pallas import tpu as pltpu
from jax.sharding import Mesh, PartitionSpec as P

AXES = ("y", "zl", "c", "zh", "x")
EMBED = 512
TOWER = 2048
EPS = 1e-06
TEMP = 0.05
SCALE = 1.0 / (EMBED * TEMP)
BF = jnp.bfloat16
F32 = jnp.float32
I32 = jnp.int32
SLOTS = [(d, k) for d in range(2) for k in range(4)]


def shift(value, step, axis="x"):
    return lax.ppermute(value, axis, [(i, (i + step) % 4) for i in range(4)])


def around(value, axis="x"):
    return [value] + [shift(value, k, axis) for k in (1, 2, 3)]


def both_cores(value):
    return jnp.concatenate([value, swap(value)], axis=0)


def slots(value):
    return around(both_cores(value))


def after(value, *others):
    return lax.optimization_barrier((value, *others))[0]


def swap(value):
    return lax.ppermute(value, "c", [(0, 1), (1, 0)])


VM = functools.partial(pl.BlockSpec, memory_space=pltpu.VMEM)
SM = functools.partial(pl.BlockSpec, memory_space=pltpu.SMEM)


def call(body, outs, ins, scratch=(), flops=1 << 20, smem=0, moved=1 << 20):
    return pl.pallas_call(
        body,
        out_shape=tuple(jax.ShapeDtypeStruct(s, d) for s, d in outs),
        in_specs=[SM()] * smem + [VM()] * (len(ins) - smem),
        out_specs=tuple(VM() for _ in outs),
        scratch_shapes=list(scratch),
        compiler_params=pltpu.CompilerParams(vmem_limit_bytes=16 * 1024 * 1024),
        cost_estimate=pl.CostEstimate(flops=flops, bytes_accessed=moved, transcendentals=0),
    )(*ins)


def to_unit(raw):
    return (raw * lax.rsqrt(jnp.mean(raw * raw, axis=-1, keepdims=True) + EPS)).astype(BF)


def item_tower_body(hidden_hbm, weight_hbm, unit_ref, hidden, weight, sems):
    part = TOWER // 4
    copies = [pltpu.make_async_copy(hidden_hbm, hidden, sems.at[4])]
    for i in range(4):
        rows = pl.ds(i * part, part)
        copies.append(pltpu.make_async_copy(weight_hbm.at[rows], weight.at[rows], sems.at[i]))
    for copy in copies:
        copy.start()
    copies[0].wait()
    raw = None
    for i in range(4):
        copies[i + 1].wait()
        rows = slice(i * part, (i + 1) * part)
        term = jnp.dot(hidden[:, rows], weight[rows, :], preferred_element_type=F32)
        raw = term if raw is None else raw + term
    unit_ref[...] = jnp.broadcast_to(to_unit(raw)[None], unit_ref.shape)


def item_tower(hidden, weight):
    hbm = pl.BlockSpec(memory_space=pltpu.HBM)
    return pl.pallas_call(
        item_tower_body,
        out_shape=jax.ShapeDtypeStruct((8, 32, EMBED), BF),
        in_specs=[hbm, hbm],
        out_specs=VM(),
        scratch_shapes=[
            pltpu.VMEM((32, TOWER), BF),
            pltpu.VMEM((TOWER, EMBED), BF),
            pltpu.SemaphoreType.DMA((5,)),
        ],
        compiler_params=pltpu.CompilerParams(vmem_limit_bytes=60 * 1024 * 1024),
        cost_estimate=pl.CostEstimate(flops=2 * 32 * TOWER * EMBED, bytes_accessed=2 << 20, transcendentals=0),
    )(hidden, weight)


def item_raw_body(hidden_ref, weight_ref, raw_ref):
    raw_ref[...] = jnp.dot(hidden_ref[...], weight_ref[...], preferred_element_type=F32)


def query_tower_body(place_ref, hidden_ref, weight_ref, counts_ref, raw_ref, unit_ref, logs_ref, rows):
    raw = jnp.dot(hidden_ref[...], weight_ref[...], preferred_element_type=F32)
    raw_ref[...] = raw
    unit_ref[...] = to_unit(raw)
    rows[...] = jnp.ones_like(rows)
    for back in range(4):
        for zh in range(4):
            at = zh * 16 + place_ref[0] * 4 + lax.rem(place_ref[3] + 4 - back, 4)
            rows[back * 4 + zh : back * 4 + zh + 1, :] = counts_ref[pl.ds(at, 1), :].astype(F32)
    logs_ref[...] = jnp.transpose(jnp.log(rows[...]))


def pick_body(place_ref, query_ref, item_ref, *refs):
    own_refs, other_ref, both = refs[0:4], refs[4], refs[5]
    both[0:128, :] = query_ref[...]
    both[128:160, :] = item_ref[...]
    lane = lax.broadcasted_iota(I32, (1, 256), 1)
    n = lane & 127
    k, zh, zl, y_lo = n & 7, (n >> 3) & 3, (n >> 5) & 1, (n >> 6) & 1
    rows = lax.broadcasted_iota(I32, (1024, 256), 0)
    c = place_ref[1] ^ (lane >> 7)
    for forward in range(4):
        x = lax.rem(place_ref[0] + forward, 4)
        source = ((((y_lo * 2 + zl) * 2 + c) * 4 + zh) * 4 + x) * 8 + k
        chosen = jnp.where(rows == source, 1.0, 0.0).astype(BF)
        for y_hi in range(2):
            lanes = slice(y_hi * 128, (y_hi + 1) * 128)
            part = jnp.dot(
                both[:, y_hi * 1024 : (y_hi + 1) * 1024], chosen, preferred_element_type=F32
            ).astype(BF)
            own_refs[forward][:, lanes] = part[:, 0:128]
            other_ref[forward, :, lanes] = part[:, 128:256]


def hits_of(place_ref, own_positives, other_positives):
    x, c, zh, y = place_ref[0], place_ref[1], place_ref[2], place_ref[3]
    hits = []
    for d, k in SLOTS:
        ref = own_positives if d == 0 else other_positives
        wanted = ref[pl.ds(zh * 4 + lax.rem(x + 4 - k, 4), 1), :]
        block, within = wanted >> 9, wanted & 511
        back = (y + 4 - (within >> 7)) & 3
        row = (back << 8) | (((within >> 6) & 1) << 7) | ((block >> 2) << 5) | (within & 31)
        hits.append(jnp.where(((block & 3) == x) & (((within >> 5) & 1) == c), row, -1))
    return jnp.concatenate(hits, axis=1)


def score_body(place_ref, own_tiles, other_tiles, *refs):
    q_refs, i_refs, (logs_ref, own_positives, other_positives) = refs[0:4], refs[4:8], refs[8:11]
    exp_ref, sums_ref, query_ref, hit_ref = refs[11:15]
    for s, (d, k) in enumerate(SLOTS):
        query_ref[s * 128 : (s + 1) * 128, :] = q_refs[k][d * 128 : (d + 1) * 128, :]
    queries = query_ref[...]
    hit = hits_of(place_ref, own_positives, other_positives)
    hit_ref[...] = hit
    x, c, zh = place_ref[0], place_ref[1], place_ref[2]
    block_of_row = lax.broadcasted_iota(I32, (128, 1), 0) >> 5
    listed = []
    for tiles in (own_tiles, other_tiles):
        flags = jnp.zeros((128, 1), I32)
        for z in range(4):
            flag = jnp.int32(0)
            for entry in range(8):
                flag = flag | (tiles[zh, entry] == z * 4 + x).astype(I32)
            flags = jnp.where(block_of_row == z, flag, flags)
        listed.append(jnp.broadcast_to(flags, (128, 512)))
    listed = jnp.concatenate(listed, axis=1) > 0
    total = jnp.zeros((1, 1024), F32)
    target = jnp.zeros((1, 1024), F32)
    ids = lax.broadcasted_iota(I32, (128, 1024), 0)
    for y, items_ref in enumerate(i_refs):
        for zl in range(2):
            first = (y * 2 + zl) * 128
            items = items_ref[zl * 128 : (zl + 1) * 128, :]
            dots = lax.dot_general(items, queries, (((1,), (1,)), ((), ())), preferred_element_type=F32)
            at = pl.multiple_of(zl * 64 + c * 32, 32)
            logs = jnp.concatenate([logs_ref[pl.ds(at, 32), y * 4 + z : y * 4 + z + 1] for z in range(4)], axis=0)
            scores = dots * SCALE - logs
            mine = ids == hit - first
            live = jnp.where(mine | listed, jnp.exp(scores), 0.0)
            exp_ref[first : first + 128, :] = live.astype(BF)
            total += jnp.sum(live, axis=0, keepdims=True)
            target += jnp.sum(jnp.where(mine, scores, 0.0), axis=0, keepdims=True)
    for s in range(8):
        sums_ref[s : s + 1, :] = total[:, s * 128 : (s + 1) * 128]
        sums_ref[8 + s : 9 + s, :] = target[:, s * 128 : (s + 1) * 128]


CHUNK = 256


def shadow_body(hit_ref, exp_ref, i0, i1, i2, i3, query_ref, up_ref, hot_ref, pull_ref):
    hit = hit_ref[...]
    for chunk, items_ref in enumerate((i0, i1, i2, i3)):
        rows = slice(chunk * CHUNK, (chunk + 1) * CHUNK)
        ids = lax.broadcasted_iota(I32, (CHUNK, 1024), 0) + chunk * CHUNK
        mine = jnp.where(ids == hit, 1.0, 0.0).astype(BF)
        pull_ref[rows, :] = jnp.dot(mine, query_ref[...], preferred_element_type=F32)
        items = items_ref[...]
        up = lax.dot_general(exp_ref[rows, :], items, (((0,), (0,)), ((), ())), preferred_element_type=F32)
        hot = lax.dot_general(mine, items, (((0,), (0,)), ((), ())), preferred_element_type=F32)
        if chunk == 0:
            up_ref[...] = up
            hot_ref[...] = hot
        else:
            up_ref[...] += up
            hot_ref[...] += hot


def full_sums(refs, start):
    out = []
    for d, k in SLOTS:
        total = None
        for step in range(4):
            for flip in range(2):
                s = start + (d ^ flip) * 4 + (k - step) % 4
                part = refs[step][flip * 16 + s : flip * 16 + s + 1, :]
                total = part if total is None else total + part
        out.append(total)
    return jnp.concatenate(out, axis=1)


def inverse_column(total):
    return jnp.transpose(jnp.broadcast_to(1.0 / total, (128, 1024)))[:, 0:1]


def item_grad_body(s0, s1, s2, s3, exp_ref, query_ref, pull_ref, g0, g1, g2, g3):
    inverse = inverse_column(full_sums((s0, s1, s2, s3), 0))
    scaled = (query_ref[...].astype(F32) * inverse).astype(BF)
    for chunk, out_ref in enumerate((g0, g1, g2, g3)):
        rows = slice(chunk * CHUNK, (chunk + 1) * CHUNK)
        part = jnp.dot(exp_ref[rows, :], scaled, preferred_element_type=F32) - pull_ref[rows, :]
        out_ref[...] = part.astype(out_ref.dtype)


def query_grad_body(s0, s1, s2, s3, up_ref, hot_ref, loss_ref, keep_ref, send_ref):
    sums = (s0, s1, s2, s3)
    total = full_sums(sums, 0)
    inverse = inverse_column(total)
    loss_ref[...] = jnp.log(total[:, 0:128]) - full_sums(sums, 8)[:, 0:128]
    keep_ref[...] = up_ref[0:512, :] * inverse[0:512] - hot_ref[0:512, :]
    send_ref[...] = (up_ref[512:1024, :] * inverse[512:1024] - hot_ref[512:1024, :]).astype(BF)


def query_fold_body(keep_ref, came_ref, p0, p1, p2, p3, other_ref, grad_ref, o0, o1, o2, o3):
    for s, (picked_ref, ref) in enumerate(((p0, o0), (p1, o1), (p2, o2), (p3, o3))):
        rows = slice((4 - s) % 4 * 128, (4 - s) % 4 * 128 + 128)
        grad = keep_ref[rows, :] + came_ref[rows, :].astype(F32)
        if s == 0:
            grad_ref[...] = grad
        else:
            ref[0:128, :] = grad.astype(BF)
        ref[128:288, 0:256] = picked_ref[...]
        ref[128:288, 256:512] = other_ref[s]


def to_back(raw, grad):
    grad = grad * SCALE
    factor = lax.rsqrt(jnp.mean(raw * raw, axis=-1, keepdims=True) + EPS)
    unit = raw * factor
    return (factor * (grad - unit * jnp.mean(unit * grad, axis=-1, keepdims=True))).astype(BF)


def query_back_body(raw_ref, own_ref, v1, v2, v3, out_ref):
    grad = own_ref[...]
    for ref in (v1, v2, v3):
        grad = grad + ref[0:128, :].astype(F32)
    out_ref[...] = to_back(raw_ref[...], grad)


def item_back_body(raw_ref, grads_ref, out_ref):
    grad = grads_ref[0].astype(F32)
    for part in range(1, grads_ref.shape[0]):
        grad = grad + grads_ref[part].astype(F32)
    out_ref[...] = to_back(raw_ref[...], grad)


def last_query_body(h0, h1, h2, h3, *refs):
    hidden_refs, total = (h0, h1, h2, h3), None
    for s, (d, k) in enumerate(SLOTS):
        part = lax.dot_general(
            hidden_refs[k][128:256, d * 256 : (d + 1) * 256], refs[s][...], (((0,), (0,)), ((), ())), preferred_element_type=F32
        )
        total = part if total is None else total + part
    refs[8][...] = total


def last_item_body(place_ref, h0, h1, h2, h3, b0, b1, b2, b3, query_ref, o0, o1, o2, o3, item):
    hidden_refs, back_refs, total = (h0, h1, h2, h3), (b0, b1, b2, b3), None
    for d, k in SLOTS:
        part = lax.dot_general(
            hidden_refs[k][256:288, d * 256 : (d + 1) * 256],
            back_refs[k][d * 32 : (d + 1) * 32, :],
            (((0,), (0,)), ((), ())),
            preferred_element_type=F32,
        )
        total = part if total is None else total + part
    item[...] = total
    for back, out_ref in enumerate((o0, o1, o2, o3)):
        at = pl.multiple_of(lax.rem(place_ref[3] + 4 - back, 4) * 64, 64)
        out_ref[:, 0:EMBED] = query_ref[pl.ds(at, 64), :].astype(out_ref.dtype)
        out_ref[:, EMBED:] = item[pl.ds(at, 64), :].astype(out_ref.dtype)


def add_body(own_ref, p1, p2, p3, out_ref):
    total = own_ref[...] + p1[...].astype(F32) + p2[...].astype(F32) + p3[...].astype(F32)
    out_ref[...] = total.astype(BF).reshape(out_ref.shape)


def scatter_y(parts, shape):
    came = [shift(parts[k], 4 - k, "y") for k in (1, 2, 3)]
    return call(add_body, [(shape, BF)], [parts[0], *came])[0]


def split_body(parts_ref, query_ref, item_ref):
    total = parts_ref[0].astype(F32)
    for part in range(1, parts_ref.shape[0]):
        total = total + parts_ref[part].astype(F32)
    query_ref[...] = total[:, 0:EMBED]
    item_ref[...] = total[:, EMBED:]


def local(query_hidden, item_hidden, query_weight, item_weight, tile_list, item_counts, positives):
    place = jnp.stack([lax.axis_index(axis) for axis in ("x", "c", "zh", "y")]).astype(I32)
    counts = item_counts.reshape(64, 128)
    own_positives = positives.reshape(16, 128)

    item_units = item_tower(item_hidden, item_weight)
    z_items = lax.all_to_all(item_units, ("zl", "zh"), 0, 0, tiled=True).reshape(256, EMBED)

    query_raw, query_unit, logs = call(
        query_tower_body,
        [((128, EMBED), F32), ((128, EMBED), BF), ((128, 128), F32)],
        [place, after(query_hidden, item_units), query_weight, counts],
        scratch=[pltpu.VMEM((128, 128), F32)],
        smem=1,
        flops=1,
        moved=1,
    )
    queries = slots(query_unit)
    picked = call(
        pick_body,
        [((160, 256), BF)] * 4 + [((4, 160, 256), BF)],
        [place, query_hidden, after(item_hidden, query_unit)],
        scratch=[pltpu.VMEM((160, TOWER), BF)],
        smem=1,
        flops=1,
        moved=1,
    )
    z_items = after(z_items, query_unit, picked[4])
    other_picked = swap(after(picked[4], z_items))
    items = around(z_items, "y")

    own_positives, tile_list = after((own_positives, tile_list), z_items)
    other_positives = swap(own_positives)
    other_tiles = swap(tile_list)
    exps, sums, query_rows, hit = call(
        score_body,
        [((1024, 1024), BF), ((16, 128), F32), ((1024, EMBED), BF), ((1, 1024), I32)],
        [place, tile_list, other_tiles, *queries, *items, logs, own_positives, other_positives],
        smem=3,
        flops=2 * 1024 * 1024 * 512,
    )
    all_sums = around(both_cores(sums))
    up, hot, pull = call(
        shadow_body,
        [((1024, EMBED), F32), ((1024, EMBED), F32), ((1024, EMBED), F32)],
        [hit, exps, *items, query_rows],
        flops=6 * 1024 * 1024 * 512,
    )
    item_parts = call(
        item_grad_body,
        [((256, EMBED), F32)] + [((256, EMBED), BF)] * 3,
        [*all_sums, exps, query_rows, pull],
        flops=2 * 1024 * 1024 * 512,
    )
    item_part = scatter_y(item_parts, (8, 32, EMBED))

    losses, keep, send = call(
        query_grad_body,
        [((1, 128), F32), ((512, EMBED), F32), ((512, EMBED), BF)],
        [*all_sums, up, after(hot, item_parts[3])],
        moved=16 << 20,
    )
    own_grad, *hidden = call(
        query_fold_body,
        [((128, EMBED), F32)] + [((288, EMBED), BF)] * 4,
        [keep, swap(send), *picked[0:4], other_picked],
    )
    hidden = [hidden[0]] + [shift(hidden[k], k) for k in (1, 2, 3)]
    query_back = call(query_back_body, [((128, EMBED), BF)], [query_raw, own_grad, *hidden[1:]])[0]
    query_backs = around(query_back)
    query_backs = query_backs + [swap(part) for part in query_backs]
    query_last = call(
        last_query_body,
        [((256, EMBED), F32)],
        [*hidden, *query_backs],
        flops=2 * 1024 * 256 * 512,
        moved=4 << 20,
    )[0]

    item_part = after(item_part, query_back)
    item_raw = call(
        item_raw_body,
        [((32, EMBED), F32)],
        [after(item_hidden, item_part), item_weight],
        flops=2 * 32 * TOWER * EMBED,
    )[0]
    item_part = lax.all_to_all(item_part, ("zl", "zh"), 0, 0, tiled=True)
    item_back = call(item_back_body, [((32, EMBED), BF)], [item_raw, item_part])[0]
    item_backs = slots(item_back)

    parts = call(
        last_item_body,
        [((64, 2 * EMBED), F32)] + [((64, 2 * EMBED), BF)] * 3,
        [place, *hidden, *item_backs, query_last],
        scratch=[pltpu.VMEM((256, EMBED), F32)],
        smem=1,
        flops=2 * 256 * 256 * 512,
    )
    part = scatter_y(parts, (8, 8, 2 * EMBED))
    part = lax.all_to_all(part, ("zl", "zh"), 0, 0, tiled=True)
    grad_query, grad_item = call(split_body, [((8, EMBED), F32)] * 2, [part])
    return (losses.reshape(128), grad_query, grad_item)


def solution(mesh):
    inner = Mesh(mesh.devices.reshape(4, 2, 2, 4, 4), AXES)
    pb, ia = ("y", "zl", "c"), ("zh", "x")
    placed = (P(pb + ia, None), P(ia + pb, None), P(), P(), P(pb, None), P(), P(pb))
    return jax.shard_map(
        local,
        mesh=inner,
        in_specs=placed,
        out_specs=(P(pb + ia), P(pb + ia, None), P(pb + ia, None)),
        check_vma=False,
    )
```

time: 1690 us -> 131 us (0.08)
  waiting for transfers between devices: 1460 us -> 48 us
  blocking collectives: 104 us -> 11.8 us
  starting transfers between devices: 0.16 us -> 42.9 us
  other arithmetic: 39.1 us -> 0.09 us
  local copies, waits for them, and re-layouts: 39.7 us -> 4 us
  matrix products: 25 us -> 0 us
  Pallas kernels: 0 us -> 20.9 us
    unnamed x5 -> x0, waiting for transfers between devices: 1280 us -> none
    reduce_scatter x2 -> x0, waiting for transfers between devices: 167 us -> none  [the longest x1 93.3 us: local(): lax.psum_scatter(query_grad, 'ia', scatter_dimension=0, tiled=True)]
    psum x1 -> x0, blocking collectives: 81.9 us -> none  [local(): totals, target_score = lax.psum((partial_sums, target_part), 'ia')]
    ppermute x0 -> x35, waiting for transfers between devices: none -> 38.8 us  [the longest x24 35.2 us: shift(): return lax.ppermute(value, axis, [(i, (i + step) % 4) for i in range(4)])]
    ppermute x0 -> x35, starting transfers between devices: none -> 30.6 us  [the longest x24 28.7 us: shift(): return lax.ppermute(value, axis, [(i, (i + step) % 4) for i in range(4)])]
    dot_general x12 -> x0, matrix products: 25 us -> none  [the longest x4 6.72 us: tile_weights(): lax.dot_general(query_tile, item_tile, (((1,), (1,)), ((), ())), preferre...]
    all_gather x1 -> x0, blocking collectives: 21.9 us -> none  [local(): items = lax.all_gather(item_own, 'pb', axis=0, tiled=True)]
    pallas_call x0 -> x16, Pallas kernels: none -> 20.9 us  [the longest x15 18.2 us: call(): pl.pallas_call(body, out_shape=tuple((jax.ShapeDtypeStruct(s, d) for s, d...]
  transfers between devices with their start and end apart: 4 -> 37, of which waited for: 4 -> 21; matrix products, arithmetic and copies ran while one was open for 2% -> 0% of each run, Pallas kernels for 0% -> 7%
where the time goes in v2:
time: 131 us; the launch traced here: 129 us
  waiting for transfers between devices  48 us (37%)
  starting transfers between devices  42.9 us (33%)
  Pallas kernels  20.9 us (16%)
  blocking collectives  11.8 us (9%)
  local copies, waits for them, and re-layouts  4 us (3%)
    ppermute x24, waiting for transfers between devices, shift(): return lax.ppermute(value, axis, [(i, (i + step) % 4) for i in range(4)])  35.2 us
    ppermute x24, starting transfers between devices, shift(): return lax.ppermute(value, axis, [(i, (i + step) % 4) for i in range(4)])  28.7 us
    pallas_call x15, Pallas kernels, call(): pl.pallas_call(body, out_shape=tuple((jax.ShapeDtypeStruct(s, d) for s, d...  18.2 us
    all_to_all x1, blocking collectives, local(): part = lax.all_to_all(part, ('zl', 'zh'), 0, 0, tiled=True)  11.8 us
    all_to_all x1, starting transfers between devices, local(): lax.all_to_all(item_units, ('zl', 'zh'), 0, 0, tiled=True)  6.73 us
    all_to_all x1, starting transfers between devices, local(): item_part = lax.all_to_all(item_part, ('zl', 'zh'), 0, 0, tiled=True)  5.65 us
    all_to_all x1, waiting for transfers between devices, local(): item_part = lax.all_to_all(item_part, ('zl', 'zh'), 0, 0, tiled=True)  5.34 us
    unnamed x28, local copies, waits for them, and re-layouts  3.99 us
  transfers between devices with their start and end apart: 37, of which 21 were waited for; matrix products, arithmetic and copies ran while one was open for 0% of the time, Pallas kernels for 7%

profile of v2, /device:TPU:0, one launch (start us, length us, event | category | flops | bytes accessed | tf_op | source)
XLA Modules:
  0.0 128.7 jit_solution(16344328507599123990)
XLA Ops:
  0.7 2.8 %shard_map.94 = bf16[8,32,512]{2,1,0:T(8,128)(2,1)} custom-call(bf16[32,2048]{1,0:T(8,128)(2,1)} %hidden_ref.1, bf16[2048,512]{1,0:T(8,128)(2,1)} %weight_ref.3), custom_call_target="tpu_custom_call" | custom-call | flops 67108864 | bytes 2097152 | tf_op jit(solution)/shard_map/pallas_call | solution.py:86
  3.5 1.0 copy-done.2
  4.6 1.1 shard_map.95
  5.7 0.7 copy-done.8
  6.4 6.7 %all-to-all-start = ((bf16[8,32,512]{2,1,0:T(8,128)(2,1)}), bf16[8,32,512]{2,1,0:T(8,128)(2,1)S(1)}, u32[]{:S(2)}, u32[]{:S(2)}) async-start(bf16[8,32,512]{2,1,0:T(8,128)(2,1)} %shard_map.94), calls=%async_computation | async-start | bytes 524288 | tf_op jit(solution)/shard_map/all_to_all | solution.py:333
  13.2 2.8 %collective-permute-start.4 = (bf16[256,512]{1,0:T(8,128)(2,1)S(1)}, bf16[256,512]{1,0:T(8,128)(2,1)S(1)}, u32[]{:S(2)}, u32[]{:S(2)}) collective-permute-start(bf16[256,512]{1,0:T(8,128)(2,1)S(1)} %constant_dynamic-update-slice_fusion.refs_0_), channel_id=1, source_target_pairs={{0,3},{1,0},{2,1},{3,2},{4,7},{5,4},{6,5},{7,6},{8,11},{9,8},{10,9... | collective-permute-start | bytes 786440 | tf_op jit(solution)/shard_map/ppermute | solution.py:23
  16.0 0.8 collective-permute-start.3
  16.8 1.4 %shard_map.96 = (bf16[160,256]{1,0:T(8,128)(2,1)S(1)}, bf16[160,256]{1,0:T(8,128)(2,1)S(1)}, bf16[160,256]{1,0:T(8,128)(2,1)S(1)}, bf16[160,256]{1,0:T(8,128)(2,1)S(1)}, bf16[4,160,256]{2,1,0:T(8,128)(2,1)S(1)}) custom-call(s32[4]{0:T(128)S(1)} %pad_add_fusion.place_ref, bf16[128,2048]{1,0:T(8,128)(2,1)S(1)} %copy-done.3, bf16[32,2048]{1,0:T(8,128)(2,1)S(1)} %copy-done.4), custom_call_target="tpu_custom_call" | custom-call | flops 1 | bytes 1 | tf_op jit(solution)/shard_map/pallas_call | solution.py:51
  18.3 1.0 collective-permute-start.2
  19.2 3.9 %all-to-all-done = bf16[8,32,512]{2,1,0:T(8,128)(2,1)S(1)} async-done(((bf16[8,32,512]{2,1,0:T(8,128)(2,1)}), bf16[8,32,512]{2,1,0:T(8,128)(2,1)S(1)}, u32[]{:S(2)}, u32[]{:S(2)}) %all-to-all-start) | async-done | bytes 262176 | tf_op jit(solution)/shard_map/all_to_all | solution.py:333
  23.1 3.0 %collective-permute-start.7 = (bf16[256,512]{1,0:T(8,128)(2,1)S(1)}, bf16[256,512]{1,0:T(8,128)(2,1)S(1)}, u32[]{:S(2)}, u32[]{:S(2)}) collective-permute-start(bf16[256,512]{1,0:T(8,128)(2,1)S(1)} %bitcast.8), channel_id=1, source_target_pairs={{0,192},{64,0},{128,64},{192,128},{1,193},{65,1},{129,65},{193,129... | collective-permute-start | bytes 786440 | tf_op jit(solution)/shard_map/ppermute | solution.py:23
  26.1 0.6 collective-permute-start.6
  26.8 0.9 collective-permute-done.4.refs_3_
  27.6 1.6 %collective-permute-start.5 = (bf16[256,512]{1,0:T(8,128)(2,1)S(1)}, bf16[256,512]{1,0:T(8,128)(2,1)S(1)}, u32[]{:S(2)}, u32[]{:S(2)}) collective-permute-start(bf16[256,512]{1,0:T(8,128)(2,1)S(1)} %bitcast.10), channel_id=1, source_target_pairs={{0,64},{64,128},{128,192},{192,0},{1,65},{65,129},{129,193},{193,1... | collective-permute-start | bytes 786440 | tf_op jit(solution)/shard_map/ppermute | solution.py:23
  29.2 2.1 %collective-permute-done.2.refs_1_ = bf16[256,512]{1,0:T(8,128)(2,1)S(1)} collective-permute-done((bf16[256,512]{1,0:T(8,128)(2,1)S(1)}, bf16[256,512]{1,0:T(8,128)(2,1)S(1)}, u32[]{:S(2)}, u32[]{:S(2)}) %collective-permute-start.2) | collective-permute-done | bytes 262176 | tf_op jit(solution)/shard_map/ppermute | solution.py:23
  31.3 1.1 collective-permute-done.other_tiles
  32.5 3.4 %collective-permute-done.7.refs_7_.i3 = bf16[256,512]{1,0:T(8,128)(2,1)S(1)} collective-permute-done((bf16[256,512]{1,0:T(8,128)(2,1)S(1)}, bf16[256,512]{1,0:T(8,128)(2,1)S(1)}, u32[]{:S(2)}, u32[]{:S(2)}) %collective-permute-start.7) | collective-permute-done | bytes 262176 | tf_op jit(solution)/shard_map/ppermute | solution.py:23
  35.8 0.3 collective-permute-done.6.refs_6_.i2
  36.2 3.4 %collective-permute-done.5.refs_5_.i1 = bf16[256,512]{1,0:T(8,128)(2,1)S(1)} collective-permute-done((bf16[256,512]{1,0:T(8,128)(2,1)S(1)}, bf16[256,512]{1,0:T(8,128)(2,1)S(1)}, u32[]{:S(2)}, u32[]{:S(2)}) %collective-permute-start.5) | collective-permute-done | bytes 262176 | tf_op jit(solution)/shard_map/ppermute | solution.py:23
  39.5 3.8 %shard_map.97 = (bf16[1024,1024]{1,0:T(8,128)(2,1)S(1)}, f32[16,128]{1,0:T(8,128)S(1)}, bf16[1024,512]{1,0:T(8,128)(2,1)S(1)}, s32[1,1024]{1,0:T(1,128)S(1)}) custom-call(s32[4]{0:T(128)S(1)} %pad_add_fusion.place_ref, s32[4,8]{1,0:T(4,128)S(1)} %copy-done.12, s32[4,8]{1,0:T(4,128)S(1)} %collective-permute-done.other_tiles, ...), custom_call_target="tpu_custom_call" | custom-call | flops 1073741824 | bytes 1048576 | tf_op jit(solution)/shard_map/pallas_call | solution.py:51
  43.4 1.1 collective-permute-done.9
  44.6 2.9 %collective-permute-start.12 = (f32[32,128]{1,0:T(8,128)S(1)}, f32[32,128]{1,0:T(8,128)S(1)}, u32[]{:S(2)}, u32[]{:S(2)}) collective-permute-start(f32[32,128]{1,0:T(8,128)S(1)} %constant_dynamic-update-slice_fusion.2.s0), channel_id=1, source_target_pairs={{0,3},{1,0},{2,1},{3,2},{4,7},{5,4},{6,5},{7,6},{8,11},{9,8},{10,9... | collective-permute-start | bytes 49160 | tf_op jit(solution)/shard_map/ppermute | solution.py:23
  47.4 0.7 collective-permute-start.11
  48.2 0.9 collective-permute-start.10
  49.0 3.4 %shard_map.98 = (f32[1024,512]{1,0:T(8,128)S(1)}, f32[1024,512]{1,0:T(8,128)S(1)}, f32[1024,512]{1,0:T(8,128)S(1)}) custom-call(s32[1,1024]{1,0:T(1,128)S(1)} %get-tuple-element.54.hit_ref, bf16[1024,1024]{1,0:T(8,128)(2,1)S(1)} %get-tuple-element.55.exp_ref, bf16[256,512]{1,0:T(8,128)(2,1)S(1)} %bitcast.12, ...), custom_call_target="tpu_custom_call" | custom-call | flops 3221225472 | bytes 1048576 | tf_op jit(solution)/shard_map/pallas_call | solution.py:51
  52.7 0.4 collective-permute-done.10.s1
  53.1 1.7 %shard_map.99 = (f32[256,512]{1,0:T(8,128)S(1)}, bf16[256,512]{1,0:T(8,128)(2,1)S(1)}, bf16[256,512]{1,0:T(8,128)(2,1)S(1)}, bf16[256,512]{1,0:T(8,128)(2,1)S(1)}) custom-call(f32[32,128]{1,0:T(8,128)S(1)} %constant_dynamic-update-slice_fusion.2.s0, f32[32,128]{1,0:T(8,128)S(1)} %collective-permute-done.10.s1, f32[32,128]{1,0:T(8,128)S(1)} %collective-permute-done.11.s2, ...), custom_call_target="tpu_custom_call" | custom-call | flops 1073741824 | bytes 1048576 | tf_op jit(solution)/shard_map/pallas_call | solution.py:51
  54.8 0.9 shard_map.100
  55.7 0.5 collective-permute-start.14
  56.2 0.6 collective-permute-start.18
  56.8 1.3 collective-permute-done.14.other_ref
  58.2 1.4 %collective-permute-start.15 = (bf16[288,512]{1,0:T(8,128)(2,1)S(1)}, bf16[288,512]{1,0:T(8,128)(2,1)S(1)}, u32[]{:S(2)}, u32[]{:S(2)}) collective-permute-start(bf16[288,512]{1,0:T(8,128)(2,1)S(1)} %get-tuple-element.71), channel_id=1, source_target_pairs={{0,1},{1,2},{2,3},{3,0},{4,5},{5,6},{6,7},{7,4},{8,9},{9,10},{10,1... | collective-permute-start | bytes 884744 | tf_op jit(solution)/shard_map/ppermute | solution.py:23
  59.6 1.9 %collective-permute-start.16 = (bf16[288,512]{1,0:T(8,128)(2,1)S(1)}, bf16[288,512]{1,0:T(8,128)(2,1)S(1)}, u32[]{:S(2)}, u32[]{:S(2)}) collective-permute-start(bf16[288,512]{1,0:T(8,128)(2,1)S(1)} %get-tuple-element.72), channel_id=1, source_target_pairs={{0,2},{1,3},{2,0},{3,1},{4,6},{5,7},{6,4},{7,5},{8,10},{9,11},{10,... | collective-permute-start | bytes 884744 | tf_op jit(solution)/shard_map/ppermute | solution.py:23
  61.6 1.0 collective-permute-start.17
  62.6 0.7 collective-permute-start.19
  63.2 1.6 %collective-permute-done.18.p1 = bf16[256,512]{1,0:T(8,128)(2,1)S(1)} collective-permute-done((bf16[256,512]{1,0:T(8,128)(2,1)S(1)}, bf16[256,512]{1,0:T(8,128)(2,1)S(1)}, u32[]{:S(2)}, u32[]{:S(2)}) %collective-permute-start.18) | collective-permute-done | bytes 262176 | tf_op jit(solution)/shard_map/ppermute | solution.py:23
  64.9 8.5 %collective-permute-done.19.p2 = bf16[256,512]{1,0:T(8,128)(2,1)S(1)} collective-permute-done((bf16[256,512]{1,0:T(8,128)(2,1)S(1)}, bf16[256,512]{1,0:T(8,128)(2,1)S(1)}, u32[]{:S(2)}, u32[]{:S(2)}) %collective-permute-start.19) | collective-permute-done | bytes 262176 | tf_op jit(solution)/shard_map/ppermute | solution.py:23
  73.4 4.0 %collective-permute-done.20.p3 = bf16[256,512]{1,0:T(8,128)(2,1)S(1)} collective-permute-done((bf16[256,512]{1,0:T(8,128)(2,1)S(1)}, bf16[256,512]{1,0:T(8,128)(2,1)S(1)}, u32[]{:S(2)}, u32[]{:S(2)}) %collective-permute-start.20) | collective-permute-done | bytes 262176 | tf_op jit(solution)/shard_map/ppermute | solution.py:23
  77.5 0.7 copy-done.5
  78.4 5.6 %all-to-all-start.1 = ((bf16[8,32,512]{2,1,0:T(8,128)(2,1)}), bf16[8,32,512]{2,1,0:T(8,128)(2,1)}, u32[]{:S(2)}, u32[]{:S(2)}) async-start(bf16[8,32,512]{2,1,0:T(8,128)(2,1)} %copy-done.5), calls=%async_computation.1 | async-start | bytes 524288 | tf_op jit(solution)/shard_map/all_to_all | solution.py:413
  84.1 1.0 collective-permute-start.27
  85.1 2.0 %collective-permute-start.26 = (bf16[128,512]{1,0:T(8,128)(2,1)S(1)}, bf16[128,512]{1,0:T(8,128)(2,1)}, u32[]{:S(2)}, u32[]{:S(2)}) collective-permute-start(bf16[128,512]{1,0:T(8,128)(2,1)S(1)} %shard_map.103.refs_0_), channel_id=1, source_target_pairs={{0,2},{1,3},{2,0},{3,1},{4,6},{5,7},{6,4},{7,5},{8,10},{9,11},{10,... | collective-permute-start | bytes 393224 | tf_op jit(solution)/shard_map/ppermute | solution.py:23
  87.1 0.3 collective-permute-start.25
  87.4 0.4 shard_map.104.raw_ref
  87.8 0.6 copy-done.6
  88.5 5.3 %all-to-all-done.1.grads_ref = bf16[8,32,512]{2,1,0:T(8,128)(2,1)} async-done(((bf16[8,32,512]{2,1,0:T(8,128)(2,1)}), bf16[8,32,512]{2,1,0:T(8,128)(2,1)}, u32[]{:S(2)}, u32[]{:S(2)}) %all-to-all-start.1) | async-done | bytes 262176 | tf_op jit(solution)/shard_map/all_to_all | solution.py:413
  93.8 0.8 copy-done.7
  94.7 1.1 shard_map.105
  95.9 0.5 collective-permute-start.28
  96.5 0.4 collective-permute-start.30
  97.1 0.8 collective-permute-start.24
  97.9 2.2 %collective-permute-start.23 = (bf16[64,512]{1,0:T(8,128)(2,1)S(1)}, bf16[64,512]{1,0:T(8,128)(2,1)S(1)}, u32[]{:S(2)}, u32[]{:S(2)}) collective-permute-start(bf16[64,512]{1,0:T(8,128)(2,1)S(1)} %pad_maximum_fusion.b0), channel_id=1, source_target_pairs={{0,2},{1,3},{2,0},{3,1},{4,6},{5,7},{6,4},{7,5},{8,10},{9,11},{10,... | collective-permute-start | bytes 196616 | tf_op jit(solution)/shard_map/ppermute | solution.py:23
  100.1 0.4 collective-permute-start.22
  100.4 1.7 %shard_map.106.query_ref = f32[256,512]{1,0:T(8,128)S(1)} custom-call(bf16[288,512]{1,0:T(8,128)(2,1)S(1)} %get-tuple-element.70.h0, bf16[288,512]{1,0:T(8,128)(2,1)S(1)} %collective-permute-done.15.v1.h1, bf16[288,512]{1,0:T(8,128)(2,1)S(1)} %collective-permute-done.16.v2.h2, bf16[288,512]{1,0:T(8,128)(2,1)S(1)} %collective-permute-done.17.v3.h3, ...), custom_call_target="tpu_custom_call" | custom-call | flops 268435456 | bytes 4194304 | tf_op jit(solution)/shard_map/pallas_call | solution.py:51
  102.2 1.4 %collective-permute-done.23.b2 = bf16[64,512]{1,0:T(8,128)(2,1)S(1)} collective-permute-done((bf16[64,512]{1,0:T(8,128)(2,1)S(1)}, bf16[64,512]{1,0:T(8,128)(2,1)S(1)}, u32[]{:S(2)}, u32[]{:S(2)}) %collective-permute-start.23) | collective-permute-done | bytes 65568 | tf_op jit(solution)/shard_map/ppermute | solution.py:23
  103.6 1.9 %collective-permute-done.22.b1 = bf16[64,512]{1,0:T(8,128)(2,1)S(1)} collective-permute-done((bf16[64,512]{1,0:T(8,128)(2,1)S(1)}, bf16[64,512]{1,0:T(8,128)(2,1)S(1)}, u32[]{:S(2)}, u32[]{:S(2)}) %collective-permute-start.22) | collective-permute-done | bytes 65568 | tf_op jit(solution)/shard_map/ppermute | solution.py:23
  105.5 1.3 %shard_map.107 = (f32[64,1024]{1,0:T(8,128)S(1)}, bf16[64,1024]{1,0:T(8,128)(2,1)S(1)}, bf16[64,1024]{1,0:T(8,128)(2,1)S(1)}, bf16[64,1024]{1,0:T(8,128)(2,1)S(1)}) custom-call(s32[4]{0:T(128)S(1)} %pad_add_fusion.place_ref, bf16[288,512]{1,0:T(8,128)(2,1)S(1)} %get-tuple-element.70.h0, bf16[288,512]{1,0:T(8,128)(2,1)S(1)} %collective-permute-done.15.v1.h1, ...), custom_call_target="tpu_custom_call" | custom-call | flops 67108864 | bytes 1048576 | tf_op jit(solution)/shard_map/pallas_call | solution.py:51
  107.0 0.8 collective-permute-start.33
  107.9 1.2 collective-permute-start.34
  109.1 3.4 %collective-permute-done.32.p1 = bf16[64,1024]{1,0:T(8,128)(2,1)S(1)} collective-permute-done((bf16[64,1024]{1,0:T(8,128)(2,1)S(1)}, bf16[64,1024]{1,0:T(8,128)(2,1)S(1)}, u32[]{:S(2)}, u32[]{:S(2)}) %collective-permute-start.32) | collective-permute-done | bytes 131104 | tf_op jit(solution)/shard_map/ppermute | solution.py:23
  112.5 2.3 %collective-permute-done.33.p2 = bf16[64,1024]{1,0:T(8,128)(2,1)S(1)} collective-permute-done((bf16[64,1024]{1,0:T(8,128)(2,1)S(1)}, bf16[64,1024]{1,0:T(8,128)(2,1)S(1)}, u32[]{:S(2)}, u32[]{:S(2)}) %collective-permute-start.33) | collective-permute-done | bytes 131104 | tf_op jit(solution)/shard_map/ppermute | solution.py:23
  114.8 1.4 %collective-permute-done.34.p3 = bf16[64,1024]{1,0:T(8,128)(2,1)S(1)} collective-permute-done((bf16[64,1024]{1,0:T(8,128)(2,1)S(1)}, bf16[64,1024]{1,0:T(8,128)(2,1)S(1)}, u32[]{:S(2)}, u32[]{:S(2)}) %collective-permute-start.34) | collective-permute-done | bytes 131104 | tf_op jit(solution)/shard_map/ppermute | solution.py:23
  116.3 11.8 %all_to_all.15.parts_ref = bf16[8,8,1024]{2,1,0:T(8,128)(2,1)S(1)} all-to-all(bf16[8,8,1024]{2,1,0:T(8,128)(2,1)S(1)} %shard_map.108), channel_id=1, replica_groups=mesh['y'=4,'zl'=2,'c'=2,'zh'=4,'x'=4] {'zl','zh'}, dimensions={0} | all-to-all | bytes 262144 | tf_op jit(solution)/shard_map/all_to_all | solution.py:426
  128.1 0.6 shard_map.109
  (59 shorter events, 1.5 us)
Async XLA Ops:
  0.6 2.9 %copy-start.10 = (s32[8192]{0:T(1024)S(1)}, s32[8192]{0:T(1024)}, u32[]{:S(2)}) copy-start(s32[8192]{0:T(1024)} %param.12) | copy-start | bytes 98308
  0.6 2.9 %copy-start.1 = (bf16[2048,512]{1,0:T(8,128)(2,1)S(1)}, bf16[2048,512]{1,0:T(8,128)(2,1)}, u32[]{:S(2)}) copy-start(bf16[2048,512]{1,0:T(8,128)(2,1)} %weight_ref.2) | copy-start | bytes 6291460
  0.7 16.2 %copy-start.4 = (bf16[32,2048]{1,0:T(8,128)(2,1)S(1)}, bf16[32,2048]{1,0:T(8,128)(2,1)}, u32[]{:S(2)}) copy-start(bf16[32,2048]{1,0:T(8,128)(2,1)} %hidden_ref.1) | copy-start | bytes 393220
  3.5 1.0 copy-start.2
  4.6 12.2 %copy-start.3 = (bf16[128,2048]{1,0:T(8,128)(2,1)S(1)}, bf16[128,2048]{1,0:T(8,128)(2,1)}, u32[]{:S(2)}) copy-start(bf16[128,2048]{1,0:T(8,128)(2,1)} %query_ref.1) | copy-start | bytes 1572868
  4.6 24.6 %copy-start.11 = (s32[2048]{0:T(1024)S(1)}, s32[2048]{0:T(1024)}, u32[]{:S(2)}) copy-start(s32[2048]{0:T(1024)} %param.13) | copy-start | bytes 24580
  4.6 26.7 %copy-start.12 = (s32[4,8]{1,0:T(4,128)S(1)}, s32[4,8]{1,0:T(4,128)}, u32[]{:S(2)}) copy-start(s32[4,8]{1,0:T(4,128)} %own_tiles) | copy-start | bytes 388
  5.7 0.7 copy-start.8
  6.4 6.7 %collective-permute-start.1 = (bf16[128,512]{1,0:T(8,128)(2,1)S(1)}, bf16[128,512]{1,0:T(8,128)(2,1)S(1)}, u32[]{:S(2)}, u32[]{:S(2)}) collective-permute-start(bf16[128,512]{1,0:T(8,128)(2,1)S(1)} %get-tuple-element.46), channel_id=1, source_target_pairs={{0,16},{16,0},{1,17},{17,1},{2,18},{18,2},{3,19},{19,3},{4,20},{20... | collective-permute-start | bytes 393224 | tf_op jit(solution)/shard_map/ppermute | solution.py:43
  6.4 16.7 %all-to-all-start = ((bf16[8,32,512]{2,1,0:T(8,128)(2,1)}), bf16[8,32,512]{2,1,0:T(8,128)(2,1)S(1)}, u32[]{:S(2)}, u32[]{:S(2)}) async-start(bf16[8,32,512]{2,1,0:T(8,128)(2,1)} %shard_map.94), calls=%async_computation | async-start | bytes 524288 | tf_op jit(solution)/shard_map/all_to_all | solution.py:333
  13.2 14.4 %collective-permute-start.4 = (bf16[256,512]{1,0:T(8,128)(2,1)S(1)}, bf16[256,512]{1,0:T(8,128)(2,1)S(1)}, u32[]{:S(2)}, u32[]{:S(2)}) collective-permute-start(bf16[256,512]{1,0:T(8,128)(2,1)S(1)} %constant_dynamic-update-slice_fusion.refs_0_), channel_id=1, source_target_pairs={{0,3},{1,0},{2,1},{3,2},{4,7},{5,4},{6,5},{7,6},{8,11},{9,8},{10,9... | collective-permute-start | bytes 786440 | tf_op jit(solution)/shard_map/ppermute | solution.py:23
  16.0 13.2 %collective-permute-start.3 = (bf16[256,512]{1,0:T(8,128)(2,1)S(1)}, bf16[256,512]{1,0:T(8,128)(2,1)S(1)}, u32[]{:S(2)}, u32[]{:S(2)}) collective-permute-start(bf16[256,512]{1,0:T(8,128)(2,1)S(1)} %constant_dynamic-update-slice_fusion.refs_0_), channel_id=1, source_target_pairs={{0,2},{1,3},{2,0},{3,1},{4,6},{5,7},{6,4},{7,5},{8,10},{9,11},{10,... | collective-permute-start | bytes 786440 | tf_op jit(solution)/shard_map/ppermute | solution.py:23
  18.3 13.1 %collective-permute-start.2 = (bf16[256,512]{1,0:T(8,128)(2,1)S(1)}, bf16[256,512]{1,0:T(8,128)(2,1)S(1)}, u32[]{:S(2)}, u32[]{:S(2)}) collective-permute-start(bf16[256,512]{1,0:T(8,128)(2,1)S(1)} %constant_dynamic-update-slice_fusion.refs_0_), channel_id=1, source_target_pairs={{0,1},{1,2},{2,3},{3,0},{4,5},{5,6},{6,7},{7,4},{8,9},{9,10},{10,1... | collective-permute-start | bytes 786440 | tf_op jit(solution)/shard_map/ppermute | solution.py:23
  23.1 12.7 %collective-permute-start.7 = (bf16[256,512]{1,0:T(8,128)(2,1)S(1)}, bf16[256,512]{1,0:T(8,128)(2,1)S(1)}, u32[]{:S(2)}, u32[]{:S(2)}) collective-permute-start(bf16[256,512]{1,0:T(8,128)(2,1)S(1)} %bitcast.8), channel_id=1, source_target_pairs={{0,192},{64,0},{128,64},{192,128},{1,193},{65,1},{129,65},{193,129... | collective-permute-start | bytes 786440 | tf_op jit(solution)/shard_map/ppermute | solution.py:23
  26.1 10.0 %collective-permute-start.6 = (bf16[256,512]{1,0:T(8,128)(2,1)S(1)}, bf16[256,512]{1,0:T(8,128)(2,1)S(1)}, u32[]{:S(2)}, u32[]{:S(2)}) collective-permute-start(bf16[256,512]{1,0:T(8,128)(2,1)S(1)} %bitcast.9), channel_id=1, source_target_pairs={{0,128},{64,192},{128,0},{192,64},{1,129},{65,193},{129,1},{193,65... | collective-permute-start | bytes 786440 | tf_op jit(solution)/shard_map/ppermute | solution.py:23
  27.6 11.9 %collective-permute-start.5 = (bf16[256,512]{1,0:T(8,128)(2,1)S(1)}, bf16[256,512]{1,0:T(8,128)(2,1)S(1)}, u32[]{:S(2)}, u32[]{:S(2)}) collective-permute-start(bf16[256,512]{1,0:T(8,128)(2,1)S(1)} %bitcast.10), channel_id=1, source_target_pairs={{0,64},{64,128},{128,192},{192,0},{1,65},{65,129},{129,193},{193,1... | collective-permute-start | bytes 786440 | tf_op jit(solution)/shard_map/ppermute | solution.py:23
  29.2 3.3 %collective-permute-start.8 = (s32[16,128]{1,0:T(8,128)S(1)}, s32[16,128]{1,0:T(8,128)S(1)}, u32[]{:S(2)}, u32[]{:S(2)}) collective-permute-start(s32[16,128]{1,0:T(8,128)S(1)} %bitcast.14), channel_id=1, source_target_pairs={{0,16},{16,0},{1,17},{17,1},{2,18},{18,2},{3,19},{19,3},{4,20},{20... | collective-permute-start | bytes 24584 | tf_op jit(solution)/shard_map/ppermute | solution.py:43
  31.3 1.2 collective-permute-start
  43.3 1.3 collective-permute-start.9
  44.6 7.9 %collective-permute-start.12 = (f32[32,128]{1,0:T(8,128)S(1)}, f32[32,128]{1,0:T(8,128)S(1)}, u32[]{:S(2)}, u32[]{:S(2)}) collective-permute-start(f32[32,128]{1,0:T(8,128)S(1)} %constant_dynamic-update-slice_fusion.2.s0), channel_id=1, source_target_pairs={{0,3},{1,0},{2,1},{3,2},{4,7},{5,4},{6,5},{7,6},{8,11},{9,8},{10,9... | collective-permute-start | bytes 49160 | tf_op jit(solution)/shard_map/ppermute | solution.py:23
  47.4 5.2 %collective-permute-start.11 = (f32[32,128]{1,0:T(8,128)S(1)}, f32[32,128]{1,0:T(8,128)S(1)}, u32[]{:S(2)}, u32[]{:S(2)}) collective-permute-start(f32[32,128]{1,0:T(8,128)S(1)} %constant_dynamic-update-slice_fusion.2.s0), channel_id=1, source_target_pairs={{0,2},{1,3},{2,0},{3,1},{4,6},{5,7},{6,4},{7,5},{8,10},{9,11},{10,... | collective-permute-start | bytes 49160 | tf_op jit(solution)/shard_map/ppermute | solution.py:23
  48.2 5.0 %collective-permute-start.10 = (f32[32,128]{1,0:T(8,128)S(1)}, f32[32,128]{1,0:T(8,128)S(1)}, u32[]{:S(2)}, u32[]{:S(2)}) collective-permute-start(f32[32,128]{1,0:T(8,128)S(1)} %constant_dynamic-update-slice_fusion.2.s0), channel_id=1, source_target_pairs={{0,1},{1,2},{2,3},{3,0},{4,5},{5,6},{6,7},{7,4},{8,9},{9,10},{10,1... | collective-permute-start | bytes 49160 | tf_op jit(solution)/shard_map/ppermute | solution.py:23
  55.7 22.5 %copy-start.9 = (f32[128,512]{1,0:T(8,128)S(1)}, f32[128,512]{1,0:T(8,128)}, u32[]{:S(2)}) copy-start(f32[128,512]{1,0:T(8,128)} %copy-done.8) | copy-start | bytes 786436
  55.7 2.4 %collective-permute-start.13 = (bf16[512,512]{1,0:T(8,128)(2,1)S(1)}, bf16[512,512]{1,0:T(8,128)(2,1)S(1)}, u32[]{:S(2)}, u32[]{:S(2)}) collective-permute-start(bf16[512,512]{1,0:T(8,128)(2,1)S(1)} %get-tuple-element.64), channel_id=1, source_target_pairs={{0,16},{16,0},{1,17},{17,1},{2,18},{18,2},{3,19},{19,3},{4,20},{20... | collective-permute-start | bytes 1572872 | tf_op jit(solution)/shard_map/ppermute | solution.py:43
  55.7 2.4 %collective-permute-start.14 = (bf16[4,160,256]{2,1,0:T(8,128)(2,1)S(1)}, bf16[4,160,256]{2,1,0:T(8,128)(2,1)S(1)}, u32[]{:S(2)}, u32[]{:S(2)}) collective-permute-start(bf16[4,160,256]{2,1,0:T(8,128)(2,1)S(1)} %get-tuple-element.69), channel_id=1, source_target_pairs={{0,16},{16,0},{1,17},{17,1},{2,18},{18,2},{3,19},{19,3},{4,20},{20... | collective-permute-start | bytes 983048 | tf_op jit(solution)/shard_map/ppermute | solution.py:43
  56.2 8.6 %collective-permute-start.18 = (bf16[256,512]{1,0:T(8,128)(2,1)S(1)}, bf16[256,512]{1,0:T(8,128)(2,1)S(1)}, u32[]{:S(2)}, u32[]{:S(2)}) collective-permute-start(bf16[256,512]{1,0:T(8,128)(2,1)S(1)} %get-tuple-element.75), channel_id=1, source_target_pairs={{0,192},{64,0},{128,64},{192,128},{1,193},{65,1},{129,65},{193,129... | collective-permute-start | bytes 786440 | tf_op jit(solution)/shard_map/ppermute | solution.py:23
  58.2 29.1 %copy-start = (bf16[2048,512]{1,0:T(8,128)(2,1)S(1)}, bf16[2048,512]{1,0:T(8,128)(2,1)}, u32[]{:S(2)}) copy-start(bf16[2048,512]{1,0:T(8,128)(2,1)} %weight_ref.3) | copy-start | bytes 6291460
  58.2 19.9 %collective-permute-start.15 = (bf16[288,512]{1,0:T(8,128)(2,1)S(1)}, bf16[288,512]{1,0:T(8,128)(2,1)S(1)}, u32[]{:S(2)}, u32[]{:S(2)}) collective-permute-start(bf16[288,512]{1,0:T(8,128)(2,1)S(1)} %get-tuple-element.71), channel_id=1, source_target_pairs={{0,1},{1,2},{2,3},{3,0},{4,5},{5,6},{6,7},{7,4},{8,9},{9,10},{10,1... | collective-permute-start | bytes 884744 | tf_op jit(solution)/shard_map/ppermute | solution.py:23
  59.6 18.5 %collective-permute-start.16 = (bf16[288,512]{1,0:T(8,128)(2,1)S(1)}, bf16[288,512]{1,0:T(8,128)(2,1)S(1)}, u32[]{:S(2)}, u32[]{:S(2)}) collective-permute-start(bf16[288,512]{1,0:T(8,128)(2,1)S(1)} %get-tuple-element.72), channel_id=1, source_target_pairs={{0,2},{1,3},{2,0},{3,1},{4,6},{5,7},{6,4},{7,5},{8,10},{9,11},{10,... | collective-permute-start | bytes 884744 | tf_op jit(solution)/shard_map/ppermute | solution.py:23
  61.6 16.6 %collective-permute-start.17 = (bf16[288,512]{1,0:T(8,128)(2,1)S(1)}, bf16[288,512]{1,0:T(8,128)(2,1)S(1)}, u32[]{:S(2)}, u32[]{:S(2)}) collective-permute-start(bf16[288,512]{1,0:T(8,128)(2,1)S(1)} %get-tuple-element.73), channel_id=1, source_target_pairs={{0,3},{1,0},{2,1},{3,2},{4,7},{5,4},{6,5},{7,6},{8,11},{9,8},{10,9... | collective-permute-start | bytes 884744 | tf_op jit(solution)/shard_map/ppermute | solution.py:23
  62.6 10.8 %collective-permute-start.19 = (bf16[256,512]{1,0:T(8,128)(2,1)S(1)}, bf16[256,512]{1,0:T(8,128)(2,1)S(1)}, u32[]{:S(2)}, u32[]{:S(2)}) collective-permute-start(bf16[256,512]{1,0:T(8,128)(2,1)S(1)} %get-tuple-element.76), channel_id=1, source_target_pairs={{0,128},{64,192},{128,0},{192,64},{1,129},{65,193},{129,1},{193,65... | collective-permute-start | bytes 786440 | tf_op jit(solution)/shard_map/ppermute | solution.py:23
  64.8 12.5 %collective-permute-start.20 = (bf16[256,512]{1,0:T(8,128)(2,1)S(1)}, bf16[256,512]{1,0:T(8,128)(2,1)S(1)}, u32[]{:S(2)}, u32[]{:S(2)}) collective-permute-start(bf16[256,512]{1,0:T(8,128)(2,1)S(1)} %get-tuple-element.60), channel_id=1, source_target_pairs={{0,64},{64,128},{128,192},{192,0},{1,65},{65,129},{129,193},{193,1... | collective-permute-start | bytes 786440 | tf_op jit(solution)/shard_map/ppermute | solution.py:23
  77.4 0.7 copy-start.5
  78.4 15.4 %all-to-all-start.1 = ((bf16[8,32,512]{2,1,0:T(8,128)(2,1)}), bf16[8,32,512]{2,1,0:T(8,128)(2,1)}, u32[]{:S(2)}, u32[]{:S(2)}) async-start(bf16[8,32,512]{2,1,0:T(8,128)(2,1)} %copy-done.5), calls=%async_computation.1 | async-start | bytes 524288 | tf_op jit(solution)/shard_map/all_to_all | solution.py:413
  84.1 12.3 %collective-permute-start.27 = (bf16[128,512]{1,0:T(8,128)(2,1)S(1)}, bf16[128,512]{1,0:T(8,128)(2,1)}, u32[]{:S(2)}, u32[]{:S(2)}) collective-permute-start(bf16[128,512]{1,0:T(8,128)(2,1)S(1)} %shard_map.103.refs_0_), channel_id=1, source_target_pairs={{0,3},{1,0},{2,1},{3,2},{4,7},{5,4},{6,5},{7,6},{8,11},{9,8},{10,9... | collective-permute-start | bytes 393224 | tf_op jit(solution)/shard_map/ppermute | solution.py:23
  85.1 11.4 %collective-permute-start.26 = (bf16[128,512]{1,0:T(8,128)(2,1)S(1)}, bf16[128,512]{1,0:T(8,128)(2,1)}, u32[]{:S(2)}, u32[]{:S(2)}) collective-permute-start(bf16[128,512]{1,0:T(8,128)(2,1)S(1)} %shard_map.103.refs_0_), channel_id=1, source_target_pairs={{0,2},{1,3},{2,0},{3,1},{4,6},{5,7},{6,4},{7,5},{8,10},{9,11},{10,... | collective-permute-start | bytes 393224 | tf_op jit(solution)/shard_map/ppermute | solution.py:23
  87.1 9.8 %collective-permute-start.25 = (bf16[128,512]{1,0:T(8,128)(2,1)S(1)}, bf16[128,512]{1,0:T(8,128)(2,1)}, u32[]{:S(2)}, u32[]{:S(2)}) collective-permute-start(bf16[128,512]{1,0:T(8,128)(2,1)S(1)} %shard_map.103.refs_0_), channel_id=1, source_target_pairs={{0,1},{1,2},{2,3},{3,0},{4,5},{5,6},{6,7},{7,4},{8,9},{9,10},{10,1... | collective-permute-start | bytes 393224 | tf_op jit(solution)/shard_map/ppermute | solution.py:23
  87.8 0.6 copy-start.6
  93.8 0.8 copy-start.7
  95.8 1.3 %collective-permute-start.21 = (bf16[32,512]{1,0:T(8,128)(2,1)S(1)}, bf16[32,512]{1,0:T(8,128)(2,1)S(1)}, u32[]{:S(2)}, u32[]{:S(2)}) collective-permute-start(bf16[32,512]{1,0:T(8,128)(2,1)S(1)} %shard_map.105), channel_id=1, source_target_pairs={{0,16},{16,0},{1,17},{17,1},{2,18},{18,2},{3,19},{19,3},{4,20},{20... | collective-permute-start | bytes 98312 | tf_op jit(solution)/shard_map/ppermute | solution.py:43
  95.9 2.0 %collective-permute-start.28 = (bf16[128,512]{1,0:T(8,128)(2,1)S(1)}, bf16[128,512]{1,0:T(8,128)(2,1)S(1)}, u32[]{:S(2)}, u32[]{:S(2)}) collective-permute-start(bf16[128,512]{1,0:T(8,128)(2,1)S(1)} %shard_map.103.refs_0_), channel_id=1, source_target_pairs={{0,16},{16,0},{1,17},{17,1},{2,18},{18,2},{3,19},{19,3},{4,20},{20... | collective-permute-start | bytes 393224 | tf_op jit(solution)/shard_map/ppermute | solution.py:43
  96.4 3.7 %collective-permute-start.31 = (bf16[128,512]{1,0:T(8,128)(2,1)}, bf16[128,512]{1,0:T(8,128)(2,1)S(1)}, u32[]{:S(2)}, u32[]{:S(2)}) collective-permute-start(bf16[128,512]{1,0:T(8,128)(2,1)} %collective-permute-done.27.refs_3_), channel_id=1, source_target_pairs={{0,16},{16,0},{1,17},{17,1},{2,18},{18,2},{3,19},{19,3},{4,20},{20... | collective-permute-start | bytes 393224 | tf_op jit(solution)/shard_map/ppermute | solution.py:43
  96.5 4.0 %collective-permute-start.30 = (bf16[128,512]{1,0:T(8,128)(2,1)}, bf16[128,512]{1,0:T(8,128)(2,1)S(1)}, u32[]{:S(2)}, u32[]{:S(2)}) collective-permute-start(bf16[128,512]{1,0:T(8,128)(2,1)} %collective-permute-done.26.refs_2_), channel_id=1, source_target_pairs={{0,16},{16,0},{1,17},{17,1},{2,18},{18,2},{3,19},{19,3},{4,20},{20... | collective-permute-start | bytes 393224 | tf_op jit(solution)/shard_map/ppermute | solution.py:43
  96.9 3.5 %collective-permute-start.29 = (bf16[128,512]{1,0:T(8,128)(2,1)}, bf16[128,512]{1,0:T(8,128)(2,1)S(1)}, u32[]{:S(2)}, u32[]{:S(2)}) collective-permute-start(bf16[128,512]{1,0:T(8,128)(2,1)} %collective-permute-done.25.refs_1_), channel_id=1, source_target_pairs={{0,16},{16,0},{1,17},{17,1},{2,18},{18,2},{3,19},{19,3},{4,20},{20... | collective-permute-start | bytes 393224 | tf_op jit(solution)/shard_map/ppermute | solution.py:43
  97.1 5.1 %collective-permute-start.24 = (bf16[64,512]{1,0:T(8,128)(2,1)S(1)}, bf16[64,512]{1,0:T(8,128)(2,1)S(1)}, u32[]{:S(2)}, u32[]{:S(2)}) collective-permute-start(bf16[64,512]{1,0:T(8,128)(2,1)S(1)} %pad_maximum_fusion.b0), channel_id=1, source_target_pairs={{0,3},{1,0},{2,1},{3,2},{4,7},{5,4},{6,5},{7,6},{8,11},{9,8},{10,9... | collective-permute-start | bytes 196616 | tf_op jit(solution)/shard_map/ppermute | solution.py:23
  97.9 5.8 %collective-permute-start.23 = (bf16[64,512]{1,0:T(8,128)(2,1)S(1)}, bf16[64,512]{1,0:T(8,128)(2,1)S(1)}, u32[]{:S(2)}, u32[]{:S(2)}) collective-permute-start(bf16[64,512]{1,0:T(8,128)(2,1)S(1)} %pad_maximum_fusion.b0), channel_id=1, source_target_pairs={{0,2},{1,3},{2,0},{3,1},{4,6},{5,7},{6,4},{7,5},{8,10},{9,11},{10,... | collective-permute-start | bytes 196616 | tf_op jit(solution)/shard_map/ppermute | solution.py:23
  100.1 5.5 %collective-permute-start.22 = (bf16[64,512]{1,0:T(8,128)(2,1)S(1)}, bf16[64,512]{1,0:T(8,128)(2,1)S(1)}, u32[]{:S(2)}, u32[]{:S(2)}) collective-permute-start(bf16[64,512]{1,0:T(8,128)(2,1)S(1)} %pad_maximum_fusion.b0), channel_id=1, source_target_pairs={{0,1},{1,2},{2,3},{3,0},{4,5},{5,6},{6,7},{7,4},{8,9},{9,10},{10,1... | collective-permute-start | bytes 196616 | tf_op jit(solution)/shard_map/ppermute | solution.py:23
  106.9 5.6 %collective-permute-start.32 = (bf16[64,1024]{1,0:T(8,128)(2,1)S(1)}, bf16[64,1024]{1,0:T(8,128)(2,1)S(1)}, u32[]{:S(2)}, u32[]{:S(2)}) collective-permute-start(bf16[64,1024]{1,0:T(8,128)(2,1)S(1)} %get-tuple-element.82), channel_id=1, source_target_pairs={{0,192},{64,0},{128,64},{192,128},{1,193},{65,1},{129,65},{193,129... | collective-permute-start | bytes 393224 | tf_op jit(solution)/shard_map/ppermute | solution.py:23
  107.0 7.8 %collective-permute-start.33 = (bf16[64,1024]{1,0:T(8,128)(2,1)S(1)}, bf16[64,1024]{1,0:T(8,128)(2,1)S(1)}, u32[]{:S(2)}, u32[]{:S(2)}) collective-permute-start(bf16[64,1024]{1,0:T(8,128)(2,1)S(1)} %get-tuple-element.83), channel_id=1, source_target_pairs={{0,128},{64,192},{128,0},{192,64},{1,129},{65,193},{129,1},{193,65... | collective-permute-start | bytes 393224 | tf_op jit(solution)/shard_map/ppermute | solution.py:23
  107.9 8.3 %collective-permute-start.34 = (bf16[64,1024]{1,0:T(8,128)(2,1)S(1)}, bf16[64,1024]{1,0:T(8,128)(2,1)S(1)}, u32[]{:S(2)}, u32[]{:S(2)}) collective-permute-start(bf16[64,1024]{1,0:T(8,128)(2,1)S(1)} %get-tuple-element.84), channel_id=1, source_target_pairs={{0,64},{64,128},{128,192},{192,0},{1,65},{65,129},{129,193},{193,1... | collective-permute-start | bytes 393224 | tf_op jit(solution)/shard_map/ppermute | solution.py:23

commit v3 on v2

--- a/solution.py
+++ b/solution.py
@@ -150,10 +150,10 @@
 
 
 def score_body(place_ref, own_tiles, other_tiles, *refs):
-    q_refs, i_refs, (logs_ref, own_positives, other_positives) = refs[0:4], refs[4:8], refs[8:11]
-    exp_ref, sums_ref, query_ref, hit_ref = refs[11:15]
-    for s, (d, k) in enumerate(SLOTS):
-        query_ref[s * 128 : (s + 1) * 128, :] = q_refs[k][d * 128 : (d + 1) * 128, :]
+    q_refs, i_refs, (logs_ref, own_positives, other_positives) = refs[0:8], refs[8:12], refs[12:15]
+    exp_ref, sums_ref, query_ref, hit_ref = refs[15:19]
+    for s, ref in enumerate(q_refs):
+        query_ref[s * 128 : (s + 1) * 128, :] = ref[...]
     queries = query_ref[...]
     hit = hits_of(place_ref, own_positives, other_positives)
     hit_ref[...] = hit
@@ -341,7 +341,7 @@
         flops=1,
         moved=1,
     )
-    queries = slots(query_unit)
+    queries = around(query_unit)
     picked = call(
         pick_body,
         [((160, 256), BF)] * 4 + [((4, 160, 256), BF)],
@@ -354,6 +354,7 @@
     z_items = after(z_items, query_unit, picked[4])
     other_picked = swap(after(picked[4], z_items))
     items = around(z_items, "y")
+    queries = queries + [swap(after(part, z_items)) for part in queries]
 
     own_positives, tile_list = after((own_positives, tile_list), z_items)
     other_positives = swap(own_positives)
@@ -375,7 +376,7 @@
     item_parts = call(
         item_grad_body,
         [((256, EMBED), F32)] + [((256, EMBED), BF)] * 3,
-        [*all_sums, exps, query_rows, pull],
+        [*all_sums, exps, query_rows, after(pull, other_picked)],
         flops=2 * 1024 * 1024 * 512,
     )
     item_part = scatter_y(item_parts, (8, 32, EMBED))

time: 131 us -> 133 us (1.015)
  starting transfers between devices: 42.9 us -> 44.4 us
  waiting for transfers between devices: 48 us -> 49.4 us
    ppermute x24, waiting for transfers between devices: 35.2 us -> 38.9 us  [shift(): return lax.ppermute(value, axis, [(i, (i + step) % 4) for i in range(4)])]
    all_to_all x1, waiting for transfers between devices: 3.9 us -> 1 us  [local(): lax.all_to_all(item_units, ('zl', 'zh'), 0, 0, tiled=True)]
    all_to_all x1, starting transfers between devices: 5.65 us -> 7.02 us  [local(): item_part = lax.all_to_all(item_part, ('zl', 'zh'), 0, 0, tiled=True)]
    ppermute x11 -> x14, starting transfers between devices: 1.83 us -> 2.97 us  [swap(): return lax.ppermute(value, 'c', [(0, 1), (1, 0)])]
    unnamed x28 -> x25, local copies, waits for them, and re-layouts: 3.99 us -> 2.95 us
    ppermute x11 -> x14, waiting for transfers between devices: 3.65 us -> 3.42 us  [swap(): return lax.ppermute(value, 'c', [(0, 1), (1, 0)])]
  transfers between devices with their start and end apart: 37 -> 40, of which waited for: 21 -> 20; matrix products, arithmetic and copies ran while one was open for 0% -> 0% of each run, Pallas kernels for 7% -> 10%
where the time goes in v3:
time: 133 us; the launch traced here: 131 us
  waiting for transfers between devices  49.4 us (37%)
  starting transfers between devices  44.4 us (33%)
  Pallas kernels  20.9 us (16%)
  blocking collectives  12 us (9%)
  local copies, waits for them, and re-layouts  2.96 us (2%)
    ppermute x24, waiting for transfers between devices, shift(): return lax.ppermute(value, axis, [(i, (i + step) % 4) for i in range(4)])  38.9 us
    ppermute x24, starting transfers between devices, shift(): return lax.ppermute(value, axis, [(i, (i + step) % 4) for i in range(4)])  27.5 us
    pallas_call x15, Pallas kernels, call(): pl.pallas_call(body, out_shape=tuple((jax.ShapeDtypeStruct(s, d) for s, d...  18.2 us
    all_to_all x1, blocking collectives, local(): part = lax.all_to_all(part, ('zl', 'zh'), 0, 0, tiled=True)  12 us
    all_to_all x1, starting transfers between devices, local(): item_part = lax.all_to_all(item_part, ('zl', 'zh'), 0, 0, tiled=True)  7.02 us
    all_to_all x1, starting transfers between devices, local(): lax.all_to_all(item_units, ('zl', 'zh'), 0, 0, tiled=True)  6.87 us
    all_to_all x1, waiting for transfers between devices, local(): item_part = lax.all_to_all(item_part, ('zl', 'zh'), 0, 0, tiled=True)  6.1 us
    ppermute x14, waiting for transfers between devices, swap(): return lax.ppermute(value, 'c', [(0, 1), (1, 0)])  3.42 us
  transfers between devices with their start and end apart: 40, of which 20 were waited for; matrix products, arithmetic and copies ran while one was open for 0% of the time, Pallas kernels for 10%

profile of v3, /device:TPU:0, one launch (start us, length us, event | category | flops | bytes accessed | tf_op | source)
XLA Modules:
  0.0 130.6 jit_solution(2388508022598916965)
XLA Ops:
  0.7 2.8 %shard_map.94 = bf16[8,32,512]{2,1,0:T(8,128)(2,1)} custom-call(bf16[32,2048]{1,0:T(8,128)(2,1)} %hidden_ref.1, bf16[2048,512]{1,0:T(8,128)(2,1)} %weight_ref.3), custom_call_target="tpu_custom_call" | custom-call | flops 67108864 | bytes 2097152 | tf_op jit(solution)/shard_map/pallas_call | solution.py:86
  3.5 6.9 %all-to-all-start = ((bf16[8,32,512]{2,1,0:T(8,128)(2,1)}), bf16[8,32,512]{2,1,0:T(8,128)(2,1)S(1)}, u32[]{:S(2)}, u32[]{:S(2)}) async-start(bf16[8,32,512]{2,1,0:T(8,128)(2,1)} %shard_map.94), calls=%async_computation | async-start | bytes 524288 | tf_op jit(solution)/shard_map/all_to_all | solution.py:333
  10.5 1.1 shard_map.95
  11.6 0.7 copy-done.7
  12.3 1.5 %collective-permute-start.1 = (bf16[128,512]{1,0:T(8,128)(2,1)S(1)}, bf16[128,512]{1,0:T(8,128)(2,1)S(1)}, u32[]{:S(2)}, u32[]{:S(2)}) collective-permute-start(bf16[128,512]{1,0:T(8,128)(2,1)S(1)} %get-tuple-element.56.refs_0_), channel_id=1, source_target_pairs={{0,1},{1,2},{2,3},{3,0},{4,5},{5,6},{6,7},{7,4},{8,9},{9,10},{10,1... | collective-permute-start | bytes 393224 | tf_op jit(solution)/shard_map/ppermute | solution.py:23
  13.8 1.7 %collective-permute-start.3 = (bf16[128,512]{1,0:T(8,128)(2,1)S(1)}, bf16[128,512]{1,0:T(8,128)(2,1)S(1)}, u32[]{:S(2)}, u32[]{:S(2)}) collective-permute-start(bf16[128,512]{1,0:T(8,128)(2,1)S(1)} %get-tuple-element.56.refs_0_), channel_id=1, source_target_pairs={{0,3},{1,0},{2,1},{3,2},{4,7},{5,4},{6,5},{7,6},{8,11},{9,8},{10,9... | collective-permute-start | bytes 393224 | tf_op jit(solution)/shard_map/ppermute | solution.py:23
  15.5 1.8 %collective-permute-start.2 = (bf16[128,512]{1,0:T(8,128)(2,1)S(1)}, bf16[128,512]{1,0:T(8,128)(2,1)S(1)}, u32[]{:S(2)}, u32[]{:S(2)}) collective-permute-start(bf16[128,512]{1,0:T(8,128)(2,1)S(1)} %get-tuple-element.56.refs_0_), channel_id=1, source_target_pairs={{0,2},{1,3},{2,0},{3,1},{4,6},{5,7},{6,4},{7,5},{8,10},{9,11},{10,... | collective-permute-start | bytes 393224 | tf_op jit(solution)/shard_map/ppermute | solution.py:23
  17.3 1.4 %shard_map.96 = (bf16[160,256]{1,0:T(8,128)(2,1)S(1)}, bf16[160,256]{1,0:T(8,128)(2,1)S(1)}, bf16[160,256]{1,0:T(8,128)(2,1)S(1)}, bf16[160,256]{1,0:T(8,128)(2,1)S(1)}, bf16[4,160,256]{2,1,0:T(8,128)(2,1)S(1)}) custom-call(s32[4]{0:T(128)S(1)} %pad_add_fusion.place_ref, bf16[128,2048]{1,0:T(8,128)(2,1)S(1)} %copy-done.2, bf16[32,2048]{1,0:T(8,128)(2,1)S(1)} %copy-done.3), custom_call_target="tpu_custom_call" | custom-call | flops 1 | bytes 1 | tf_op jit(solution)/shard_map/pallas_call | solution.py:51
  18.8 1.0 all-to-all-done
  19.8 0.5 collective-permute-start
  20.4 0.4 collective-permute-start.5
  20.8 1.5 %collective-permute-done.2.refs_2_ = bf16[128,512]{1,0:T(8,128)(2,1)S(1)} collective-permute-done((bf16[128,512]{1,0:T(8,128)(2,1)S(1)}, bf16[128,512]{1,0:T(8,128)(2,1)S(1)}, u32[]{:S(2)}, u32[]{:S(2)}) %collective-permute-start.2) | collective-permute-done | bytes 131104 | tf_op jit(solution)/shard_map/ppermute | solution.py:23
  22.3 3.0 %collective-permute-start.10 = (bf16[256,512]{1,0:T(8,128)(2,1)S(1)}, bf16[256,512]{1,0:T(8,128)(2,1)S(1)}, u32[]{:S(2)}, u32[]{:S(2)}) collective-permute-start(bf16[256,512]{1,0:T(8,128)(2,1)S(1)} %bitcast.8), channel_id=1, source_target_pairs={{0,192},{64,0},{128,64},{192,128},{1,193},{65,1},{129,65},{193,129... | collective-permute-start | bytes 786440 | tf_op jit(solution)/shard_map/ppermute | solution.py:23
  25.3 0.6 collective-permute-start.9
  25.9 1.0 collective-permute-start.8
  26.9 0.5 collective-permute-start.7
  27.4 0.8 collective-permute-done.6.refs_6_
  28.4 7.1 %collective-permute-done.10.refs_11_.i3 = bf16[256,512]{1,0:T(8,128)(2,1)S(1)} collective-permute-done((bf16[256,512]{1,0:T(8,128)(2,1)S(1)}, bf16[256,512]{1,0:T(8,128)(2,1)S(1)}, u32[]{:S(2)}, u32[]{:S(2)}) %collective-permute-start.10) | collective-permute-done | bytes 262176 | tf_op jit(solution)/shard_map/ppermute | solution.py:23
  35.5 0.5 collective-permute-done.9.refs_10_.i2
  36.0 3.2 %collective-permute-done.8.refs_9_.i1 = bf16[256,512]{1,0:T(8,128)(2,1)S(1)} collective-permute-done((bf16[256,512]{1,0:T(8,128)(2,1)S(1)}, bf16[256,512]{1,0:T(8,128)(2,1)S(1)}, u32[]{:S(2)}, u32[]{:S(2)}) %collective-permute-start.8) | collective-permute-done | bytes 262176 | tf_op jit(solution)/shard_map/ppermute | solution.py:23
  39.2 3.8 %shard_map.97 = (bf16[1024,1024]{1,0:T(8,128)(2,1)S(1)}, f32[16,128]{1,0:T(8,128)S(1)}, bf16[1024,512]{1,0:T(8,128)(2,1)S(1)}, s32[1,1024]{1,0:T(1,128)S(1)}) custom-call(s32[4]{0:T(128)S(1)} %pad_add_fusion.place_ref, s32[4,8]{1,0:T(4,128)S(1)} %copy-done.11, s32[4,8]{1,0:T(4,128)S(1)} %collective-permute-done.other_tiles, ...), custom_call_target="tpu_custom_call" | custom-call | flops 1073741824 | bytes 1048576 | tf_op jit(solution)/shard_map/pallas_call | solution.py:51
  43.2 1.1 collective-permute-done.12
  44.3 3.8 %collective-permute-start.15 = (f32[32,128]{1,0:T(8,128)S(1)}, f32[32,128]{1,0:T(8,128)S(1)}, u32[]{:S(2)}, u32[]{:S(2)}) collective-permute-start(f32[32,128]{1,0:T(8,128)S(1)} %constant_dynamic-update-slice_fusion.s0), channel_id=1, source_target_pairs={{0,3},{1,0},{2,1},{3,2},{4,7},{5,4},{6,5},{7,6},{8,11},{9,8},{10,9... | collective-permute-start | bytes 49160 | tf_op jit(solution)/shard_map/ppermute | solution.py:23
  48.1 0.9 collective-permute-start.13
  49.0 3.4 %shard_map.98 = (f32[1024,512]{1,0:T(8,128)S(1)}, f32[1024,512]{1,0:T(8,128)S(1)}, f32[1024,512]{1,0:T(8,128)S(1)}) custom-call(s32[1,1024]{1,0:T(1,128)S(1)} %get-tuple-element.63.hit_ref, bf16[1024,1024]{1,0:T(8,128)(2,1)S(1)} %get-tuple-element.64.exp_ref, bf16[256,512]{1,0:T(8,128)(2,1)S(1)} %bitcast.12, ...), custom_call_target="tpu_custom_call" | custom-call | flops 3221225472 | bytes 1048576 | tf_op jit(solution)/shard_map/pallas_call | solution.py:51
  52.4 0.9 collective-permute-done.14.s2
  53.3 1.7 %shard_map.99 = (f32[256,512]{1,0:T(8,128)S(1)}, bf16[256,512]{1,0:T(8,128)(2,1)S(1)}, bf16[256,512]{1,0:T(8,128)(2,1)S(1)}, bf16[256,512]{1,0:T(8,128)(2,1)S(1)}) custom-call(f32[32,128]{1,0:T(8,128)S(1)} %constant_dynamic-update-slice_fusion.s0, f32[32,128]{1,0:T(8,128)S(1)} %collective-permute-done.13.s1, f32[32,128]{1,0:T(8,128)S(1)} %collective-permute-done.14.s2, ...), custom_call_target="tpu_custom_call" | custom-call | flops 1073741824 | bytes 1048576 | tf_op jit(solution)/shard_map/pallas_call | solution.py:51
  55.0 0.9 shard_map.100
  56.0 0.6 collective-permute-start.21
  56.6 1.3 collective-permute-done.17.came_ref
  58.0 1.8 %collective-permute-start.18 = (bf16[288,512]{1,0:T(8,128)(2,1)S(1)}, bf16[288,512]{1,0:T(8,128)(2,1)S(1)}, u32[]{:S(2)}, u32[]{:S(2)}) collective-permute-start(bf16[288,512]{1,0:T(8,128)(2,1)S(1)} %get-tuple-element.81), channel_id=1, source_target_pairs={{0,1},{1,2},{2,3},{3,0},{4,5},{5,6},{6,7},{7,4},{8,9},{9,10},{10,1... | collective-permute-start | bytes 884744 | tf_op jit(solution)/shard_map/ppermute | solution.py:23
  59.8 1.2 collective-permute-start.19
  61.0 1.8 %collective-permute-start.20 = (bf16[288,512]{1,0:T(8,128)(2,1)S(1)}, bf16[288,512]{1,0:T(8,128)(2,1)S(1)}, u32[]{:S(2)}, u32[]{:S(2)}) collective-permute-start(bf16[288,512]{1,0:T(8,128)(2,1)S(1)} %get-tuple-element.83), channel_id=1, source_target_pairs={{0,3},{1,0},{2,1},{3,2},{4,7},{5,4},{6,5},{7,6},{8,11},{9,8},{10,9... | collective-permute-start | bytes 884744 | tf_op jit(solution)/shard_map/ppermute | solution.py:23
  62.8 0.6 collective-permute-start.22
  63.4 1.4 %collective-permute-done.21.p1 = bf16[256,512]{1,0:T(8,128)(2,1)S(1)} collective-permute-done((bf16[256,512]{1,0:T(8,128)(2,1)S(1)}, bf16[256,512]{1,0:T(8,128)(2,1)S(1)}, u32[]{:S(2)}, u32[]{:S(2)}) %collective-permute-start.21) | collective-permute-done | bytes 262176 | tf_op jit(solution)/shard_map/ppermute | solution.py:23
  64.9 8.7 %collective-permute-done.22.p2 = bf16[256,512]{1,0:T(8,128)(2,1)S(1)} collective-permute-done((bf16[256,512]{1,0:T(8,128)(2,1)S(1)}, bf16[256,512]{1,0:T(8,128)(2,1)S(1)}, u32[]{:S(2)}, u32[]{:S(2)}) %collective-permute-start.22) | collective-permute-done | bytes 262176 | tf_op jit(solution)/shard_map/ppermute | solution.py:23
  73.6 4.1 %collective-permute-done.23.p3 = bf16[256,512]{1,0:T(8,128)(2,1)S(1)} collective-permute-done((bf16[256,512]{1,0:T(8,128)(2,1)S(1)}, bf16[256,512]{1,0:T(8,128)(2,1)S(1)}, u32[]{:S(2)}, u32[]{:S(2)}) %collective-permute-start.23) | collective-permute-done | bytes 262176 | tf_op jit(solution)/shard_map/ppermute | solution.py:23
  77.8 0.7 copy-done.4
  78.8 7.0 %all-to-all-start.1 = ((bf16[8,32,512]{2,1,0:T(8,128)(2,1)}), bf16[8,32,512]{2,1,0:T(8,128)(2,1)}, u32[]{:S(2)}, u32[]{:S(2)}) async-start(bf16[8,32,512]{2,1,0:T(8,128)(2,1)} %copy-done.4), calls=%async_computation.1 | async-start | bytes 524288 | tf_op jit(solution)/shard_map/all_to_all | solution.py:414
  85.8 0.8 collective-permute-start.30
  86.6 1.2 collective-permute-start.29
  87.8 0.5 collective-permute-start.28
  88.4 0.4 shard_map.104.raw_ref
  88.8 0.6 copy-done.5
  89.5 6.1 %all-to-all-done.1.grads_ref = bf16[8,32,512]{2,1,0:T(8,128)(2,1)} async-done(((bf16[8,32,512]{2,1,0:T(8,128)(2,1)}), bf16[8,32,512]{2,1,0:T(8,128)(2,1)}, u32[]{:S(2)}, u32[]{:S(2)}) %all-to-all-start.1) | async-done | bytes 262176 | tf_op jit(solution)/shard_map/all_to_all | solution.py:414
  95.6 0.8 copy-done.6
  96.4 1.1 shard_map.105
  97.7 0.5 collective-permute-start.31
  98.3 0.4 collective-permute-start.33
  98.9 0.8 collective-permute-start.27
  99.7 1.0 collective-permute-start.26
  100.7 0.7 collective-permute-start.25
  101.4 1.7 %shard_map.106.query_ref = f32[256,512]{1,0:T(8,128)S(1)} custom-call(bf16[288,512]{1,0:T(8,128)(2,1)S(1)} %get-tuple-element.80.h0, bf16[288,512]{1,0:T(8,128)(2,1)S(1)} %collective-permute-done.18.v1.h1, bf16[288,512]{1,0:T(8,128)(2,1)S(1)} %collective-permute-done.19.v2.h2, bf16[288,512]{1,0:T(8,128)(2,1)S(1)} %collective-permute-done.20.v3.h3, ...), custom_call_target="tpu_custom_call" | custom-call | flops 268435456 | bytes 4194304 | tf_op jit(solution)/shard_map/pallas_call | solution.py:51
  103.1 0.7 collective-permute-done.27.b3
  103.8 1.8 %collective-permute-done.26.b2 = bf16[64,512]{1,0:T(8,128)(2,1)S(1)} collective-permute-done((bf16[64,512]{1,0:T(8,128)(2,1)S(1)}, bf16[64,512]{1,0:T(8,128)(2,1)S(1)}, u32[]{:S(2)}, u32[]{:S(2)}) %collective-permute-start.26) | collective-permute-done | bytes 65568 | tf_op jit(solution)/shard_map/ppermute | solution.py:23
  105.5 1.2 collective-permute-done.25.b1
  106.8 1.3 %shard_map.107 = (f32[64,1024]{1,0:T(8,128)S(1)}, bf16[64,1024]{1,0:T(8,128)(2,1)S(1)}, bf16[64,1024]{1,0:T(8,128)(2,1)S(1)}, bf16[64,1024]{1,0:T(8,128)(2,1)S(1)}) custom-call(s32[4]{0:T(128)S(1)} %pad_add_fusion.place_ref, bf16[288,512]{1,0:T(8,128)(2,1)S(1)} %get-tuple-element.80.h0, bf16[288,512]{1,0:T(8,128)(2,1)S(1)} %collective-permute-done.18.v1.h1, ...), custom_call_target="tpu_custom_call" | custom-call | flops 67108864 | bytes 1048576 | tf_op jit(solution)/shard_map/pallas_call | solution.py:51
  108.5 0.7 collective-permute-start.36
  109.2 1.0 collective-permute-start.37
  110.2 4.3 %collective-permute-done.35.p1 = bf16[64,1024]{1,0:T(8,128)(2,1)S(1)} collective-permute-done((bf16[64,1024]{1,0:T(8,128)(2,1)S(1)}, bf16[64,1024]{1,0:T(8,128)(2,1)S(1)}, u32[]{:S(2)}, u32[]{:S(2)}) %collective-permute-start.35) | collective-permute-done | bytes 131104 | tf_op jit(solution)/shard_map/ppermute | solution.py:23
  114.5 1.5 %collective-permute-done.36.p2 = bf16[64,1024]{1,0:T(8,128)(2,1)S(1)} collective-permute-done((bf16[64,1024]{1,0:T(8,128)(2,1)S(1)}, bf16[64,1024]{1,0:T(8,128)(2,1)S(1)}, u32[]{:S(2)}, u32[]{:S(2)}) %collective-permute-start.36) | collective-permute-done | bytes 131104 | tf_op jit(solution)/shard_map/ppermute | solution.py:23
  116.0 1.9 %collective-permute-done.37.p3 = bf16[64,1024]{1,0:T(8,128)(2,1)S(1)} collective-permute-done((bf16[64,1024]{1,0:T(8,128)(2,1)S(1)}, bf16[64,1024]{1,0:T(8,128)(2,1)S(1)}, u32[]{:S(2)}, u32[]{:S(2)}) %collective-permute-start.37) | collective-permute-done | bytes 131104 | tf_op jit(solution)/shard_map/ppermute | solution.py:23
  118.0 12.0 %all_to_all.15.parts_ref = bf16[8,8,1024]{2,1,0:T(8,128)(2,1)S(1)} all-to-all(bf16[8,8,1024]{2,1,0:T(8,128)(2,1)S(1)} %shard_map.108), channel_id=1, replica_groups=mesh['y'=4,'zl'=2,'c'=2,'zh'=4,'x'=4] {'zl','zh'}, dimensions={0} | all-to-all | bytes 262144 | tf_op jit(solution)/shard_map/all_to_all | solution.py:427
  130.0 0.6 shard_map.109
  (61 shorter events, 1.8 us)
Async XLA Ops:
  0.6 9.8 %copy-start.2 = (bf16[128,2048]{1,0:T(8,128)(2,1)S(1)}, bf16[128,2048]{1,0:T(8,128)(2,1)}, u32[]{:S(2)}) copy-start(bf16[128,2048]{1,0:T(8,128)(2,1)} %query_ref.1) | copy-start | bytes 1572868
  0.6 9.8 %copy-start.9 = (s32[8192]{0:T(1024)S(1)}, s32[8192]{0:T(1024)}, u32[]{:S(2)}) copy-start(s32[8192]{0:T(1024)} %param.12) | copy-start | bytes 98308
  0.7 9.8 %copy-start.1 = (bf16[2048,512]{1,0:T(8,128)(2,1)S(1)}, bf16[2048,512]{1,0:T(8,128)(2,1)}, u32[]{:S(2)}) copy-start(bf16[2048,512]{1,0:T(8,128)(2,1)} %weight_ref.2) | copy-start | bytes 6291460
  3.5 13.9 %copy-start.3 = (bf16[32,2048]{1,0:T(8,128)(2,1)S(1)}, bf16[32,2048]{1,0:T(8,128)(2,1)}, u32[]{:S(2)}) copy-start(bf16[32,2048]{1,0:T(8,128)(2,1)} %hidden_ref.1) | copy-start | bytes 393220
  3.5 16.3 %copy-start.10 = (s32[2048]{0:T(1024)S(1)}, s32[2048]{0:T(1024)}, u32[]{:S(2)}) copy-start(s32[2048]{0:T(1024)} %param.13) | copy-start | bytes 24580
  3.5 16.3 %copy-start.11 = (s32[4,8]{1,0:T(4,128)S(1)}, s32[4,8]{1,0:T(4,128)}, u32[]{:S(2)}) copy-start(s32[4,8]{1,0:T(4,128)} %own_tiles) | copy-start | bytes 388
  3.5 16.3 %all-to-all-start = ((bf16[8,32,512]{2,1,0:T(8,128)(2,1)}), bf16[8,32,512]{2,1,0:T(8,128)(2,1)S(1)}, u32[]{:S(2)}, u32[]{:S(2)}) async-start(bf16[8,32,512]{2,1,0:T(8,128)(2,1)} %shard_map.94), calls=%async_computation | async-start | bytes 524288 | tf_op jit(solution)/shard_map/all_to_all | solution.py:333
  11.6 0.7 copy-start.7
  12.3 7.5 %collective-permute-start.1 = (bf16[128,512]{1,0:T(8,128)(2,1)S(1)}, bf16[128,512]{1,0:T(8,128)(2,1)S(1)}, u32[]{:S(2)}, u32[]{:S(2)}) collective-permute-start(bf16[128,512]{1,0:T(8,128)(2,1)S(1)} %get-tuple-element.56.refs_0_), channel_id=1, source_target_pairs={{0,1},{1,2},{2,3},{3,0},{4,5},{5,6},{6,7},{7,4},{8,9},{9,10},{10,1... | collective-permute-start | bytes 393224 | tf_op jit(solution)/shard_map/ppermute | solution.py:23
  13.8 6.6 %collective-permute-start.3 = (bf16[128,512]{1,0:T(8,128)(2,1)S(1)}, bf16[128,512]{1,0:T(8,128)(2,1)S(1)}, u32[]{:S(2)}, u32[]{:S(2)}) collective-permute-start(bf16[128,512]{1,0:T(8,128)(2,1)S(1)} %get-tuple-element.56.refs_0_), channel_id=1, source_target_pairs={{0,3},{1,0},{2,1},{3,2},{4,7},{5,4},{6,5},{7,6},{8,11},{9,8},{10,9... | collective-permute-start | bytes 393224 | tf_op jit(solution)/shard_map/ppermute | solution.py:23
  15.5 6.7 %collective-permute-start.2 = (bf16[128,512]{1,0:T(8,128)(2,1)S(1)}, bf16[128,512]{1,0:T(8,128)(2,1)S(1)}, u32[]{:S(2)}, u32[]{:S(2)}) collective-permute-start(bf16[128,512]{1,0:T(8,128)(2,1)S(1)} %get-tuple-element.56.refs_0_), channel_id=1, source_target_pairs={{0,2},{1,3},{2,0},{3,1},{4,6},{5,7},{6,4},{7,5},{8,10},{9,11},{10,... | collective-permute-start | bytes 393224 | tf_op jit(solution)/shard_map/ppermute | solution.py:23
  19.8 6.1 %collective-permute-start.11 = (s32[16,128]{1,0:T(8,128)S(1)}, s32[16,128]{1,0:T(8,128)S(1)}, u32[]{:S(2)}, u32[]{:S(2)}) collective-permute-start(s32[16,128]{1,0:T(8,128)S(1)} %bitcast.14), channel_id=1, source_target_pairs={{0,16},{16,0},{1,17},{17,1},{2,18},{18,2},{3,19},{19,3},{4,20},{20... | collective-permute-start | bytes 24584 | tf_op jit(solution)/shard_map/ppermute | solution.py:43
  19.8 5.5 %collective-permute-start = (s32[4,8]{1,0:T(4,128)S(1)}, s32[4,8]{1,0:T(4,128)S(1)}, u32[]{:S(2)}, u32[]{:S(2)}) collective-permute-start(s32[4,8]{1,0:T(4,128)S(1)} %copy-done.11), channel_id=1, source_target_pairs={{0,16},{16,0},{1,17},{17,1},{2,18},{18,2},{3,19},{19,3},{4,20},{20... | collective-permute-start | bytes 392 | tf_op jit(solution)/shard_map/ppermute | solution.py:43
  20.3 6.6 %collective-permute-start.4 = (bf16[128,512]{1,0:T(8,128)(2,1)S(1)}, bf16[128,512]{1,0:T(8,128)(2,1)S(1)}, u32[]{:S(2)}, u32[]{:S(2)}) collective-permute-start(bf16[128,512]{1,0:T(8,128)(2,1)S(1)} %get-tuple-element.56.refs_0_), channel_id=1, source_target_pairs={{0,16},{16,0},{1,17},{17,1},{2,18},{18,2},{3,19},{19,3},{4,20},{20... | collective-permute-start | bytes 393224 | tf_op jit(solution)/shard_map/ppermute | solution.py:43
  20.4 6.5 %collective-permute-start.5 = (bf16[128,512]{1,0:T(8,128)(2,1)S(1)}, bf16[128,512]{1,0:T(8,128)(2,1)S(1)}, u32[]{:S(2)}, u32[]{:S(2)}) collective-permute-start(bf16[128,512]{1,0:T(8,128)(2,1)S(1)} %collective-permute-done.1.refs_1_), channel_id=1, source_target_pairs={{0,16},{16,0},{1,17},{17,1},{2,18},{18,2},{3,19},{19,3},{4,20},{20... | collective-permute-start | bytes 393224 | tf_op jit(solution)/shard_map/ppermute | solution.py:43
  22.3 13.3 %collective-permute-start.10 = (bf16[256,512]{1,0:T(8,128)(2,1)S(1)}, bf16[256,512]{1,0:T(8,128)(2,1)S(1)}, u32[]{:S(2)}, u32[]{:S(2)}) collective-permute-start(bf16[256,512]{1,0:T(8,128)(2,1)S(1)} %bitcast.8), channel_id=1, source_target_pairs={{0,192},{64,0},{128,64},{192,128},{1,193},{65,1},{129,65},{193,129... | collective-permute-start | bytes 786440 | tf_op jit(solution)/shard_map/ppermute | solution.py:23
  25.3 10.8 %collective-permute-start.9 = (bf16[256,512]{1,0:T(8,128)(2,1)S(1)}, bf16[256,512]{1,0:T(8,128)(2,1)S(1)}, u32[]{:S(2)}, u32[]{:S(2)}) collective-permute-start(bf16[256,512]{1,0:T(8,128)(2,1)S(1)} %bitcast.9), channel_id=1, source_target_pairs={{0,128},{64,192},{128,0},{192,64},{1,129},{65,193},{129,1},{193,65... | collective-permute-start | bytes 786440 | tf_op jit(solution)/shard_map/ppermute | solution.py:23
  25.9 13.3 %collective-permute-start.8 = (bf16[256,512]{1,0:T(8,128)(2,1)S(1)}, bf16[256,512]{1,0:T(8,128)(2,1)S(1)}, u32[]{:S(2)}, u32[]{:S(2)}) collective-permute-start(bf16[256,512]{1,0:T(8,128)(2,1)S(1)} %bitcast.10), channel_id=1, source_target_pairs={{0,64},{64,128},{128,192},{192,0},{1,65},{65,129},{129,193},{193,1... | collective-permute-start | bytes 786440 | tf_op jit(solution)/shard_map/ppermute | solution.py:23
  26.9 1.3 %collective-permute-start.6 = (bf16[128,512]{1,0:T(8,128)(2,1)S(1)}, bf16[128,512]{1,0:T(8,128)(2,1)S(1)}, u32[]{:S(2)}, u32[]{:S(2)}) collective-permute-start(bf16[128,512]{1,0:T(8,128)(2,1)S(1)} %collective-permute-done.2.refs_2_), channel_id=1, source_target_pairs={{0,16},{16,0},{1,17},{17,1},{2,18},{18,2},{3,19},{19,3},{4,20},{20... | collective-permute-start | bytes 393224 | tf_op jit(solution)/shard_map/ppermute | solution.py:43
  26.9 1.5 %collective-permute-start.7 = (bf16[128,512]{1,0:T(8,128)(2,1)S(1)}, bf16[128,512]{1,0:T(8,128)(2,1)S(1)}, u32[]{:S(2)}, u32[]{:S(2)}) collective-permute-start(bf16[128,512]{1,0:T(8,128)(2,1)S(1)} %collective-permute-done.3.refs_3_), channel_id=1, source_target_pairs={{0,16},{16,0},{1,17},{17,1},{2,18},{18,2},{3,19},{19,3},{4,20},{20... | collective-permute-start | bytes 393224 | tf_op jit(solution)/shard_map/ppermute | solution.py:43
  28.2 24.2 %collective-permute-start.16 = (bf16[4,160,256]{2,1,0:T(8,128)(2,1)S(1)}, bf16[4,160,256]{2,1,0:T(8,128)(2,1)S(1)}, u32[]{:S(2)}, u32[]{:S(2)}) collective-permute-start(bf16[4,160,256]{2,1,0:T(8,128)(2,1)S(1)} %get-tuple-element.69), channel_id=1, source_target_pairs={{0,16},{16,0},{1,17},{17,1},{2,18},{18,2},{3,19},{19,3},{4,20},{20... | collective-permute-start | bytes 983048 | tf_op jit(solution)/shard_map/ppermute | solution.py:43
  43.0 1.3 collective-permute-start.12
  44.3 8.1 %collective-permute-start.15 = (f32[32,128]{1,0:T(8,128)S(1)}, f32[32,128]{1,0:T(8,128)S(1)}, u32[]{:S(2)}, u32[]{:S(2)}) collective-permute-start(f32[32,128]{1,0:T(8,128)S(1)} %constant_dynamic-update-slice_fusion.s0), channel_id=1, source_target_pairs={{0,3},{1,0},{2,1},{3,2},{4,7},{5,4},{6,5},{7,6},{8,11},{9,8},{10,9... | collective-permute-start | bytes 49160 | tf_op jit(solution)/shard_map/ppermute | solution.py:23
  48.1 5.2 %collective-permute-start.14 = (f32[32,128]{1,0:T(8,128)S(1)}, f32[32,128]{1,0:T(8,128)S(1)}, u32[]{:S(2)}, u32[]{:S(2)}) collective-permute-start(f32[32,128]{1,0:T(8,128)S(1)} %constant_dynamic-update-slice_fusion.s0), channel_id=1, source_target_pairs={{0,2},{1,3},{2,0},{3,1},{4,6},{5,7},{6,4},{7,5},{8,10},{9,11},{10,... | collective-permute-start | bytes 49160 | tf_op jit(solution)/shard_map/ppermute | solution.py:23
  48.1 5.2 %collective-permute-start.13 = (f32[32,128]{1,0:T(8,128)S(1)}, f32[32,128]{1,0:T(8,128)S(1)}, u32[]{:S(2)}, u32[]{:S(2)}) collective-permute-start(f32[32,128]{1,0:T(8,128)S(1)} %constant_dynamic-update-slice_fusion.s0), channel_id=1, source_target_pairs={{0,1},{1,2},{2,3},{3,0},{4,5},{5,6},{6,7},{7,4},{8,9},{9,10},{10,1... | collective-permute-start | bytes 49160 | tf_op jit(solution)/shard_map/ppermute | solution.py:23
  56.0 22.6 %copy-start.8 = (f32[128,512]{1,0:T(8,128)S(1)}, f32[128,512]{1,0:T(8,128)}, u32[]{:S(2)}) copy-start(f32[128,512]{1,0:T(8,128)} %copy-done.7) | copy-start | bytes 786436
  56.0 1.9 %collective-permute-start.17 = (bf16[512,512]{1,0:T(8,128)(2,1)S(1)}, bf16[512,512]{1,0:T(8,128)(2,1)S(1)}, u32[]{:S(2)}, u32[]{:S(2)}) collective-permute-start(bf16[512,512]{1,0:T(8,128)(2,1)S(1)} %get-tuple-element.75), channel_id=1, source_target_pairs={{0,16},{16,0},{1,17},{17,1},{2,18},{18,2},{3,19},{19,3},{4,20},{20... | collective-permute-start | bytes 1572872 | tf_op jit(solution)/shard_map/ppermute | solution.py:43
  56.0 8.9 %collective-permute-start.21 = (bf16[256,512]{1,0:T(8,128)(2,1)S(1)}, bf16[256,512]{1,0:T(8,128)(2,1)S(1)}, u32[]{:S(2)}, u32[]{:S(2)}) collective-permute-start(bf16[256,512]{1,0:T(8,128)(2,1)S(1)} %get-tuple-element.85), channel_id=1, source_target_pairs={{0,192},{64,0},{128,64},{192,128},{1,193},{65,1},{129,65},{193,129... | collective-permute-start | bytes 786440 | tf_op jit(solution)/shard_map/ppermute | solution.py:23
  58.0 30.4 %copy-start = (bf16[2048,512]{1,0:T(8,128)(2,1)S(1)}, bf16[2048,512]{1,0:T(8,128)(2,1)}, u32[]{:S(2)}) copy-start(bf16[2048,512]{1,0:T(8,128)(2,1)} %weight_ref.3) | copy-start | bytes 6291460
  58.0 20.6 %collective-permute-start.18 = (bf16[288,512]{1,0:T(8,128)(2,1)S(1)}, bf16[288,512]{1,0:T(8,128)(2,1)S(1)}, u32[]{:S(2)}, u32[]{:S(2)}) collective-permute-start(bf16[288,512]{1,0:T(8,128)(2,1)S(1)} %get-tuple-element.81), channel_id=1, source_target_pairs={{0,1},{1,2},{2,3},{3,0},{4,5},{5,6},{6,7},{7,4},{8,9},{9,10},{10,1... | collective-permute-start | bytes 884744 | tf_op jit(solution)/shard_map/ppermute | solution.py:23
  59.8 18.8 %collective-permute-start.19 = (bf16[288,512]{1,0:T(8,128)(2,1)S(1)}, bf16[288,512]{1,0:T(8,128)(2,1)S(1)}, u32[]{:S(2)}, u32[]{:S(2)}) collective-permute-start(bf16[288,512]{1,0:T(8,128)(2,1)S(1)} %get-tuple-element.82), channel_id=1, source_target_pairs={{0,2},{1,3},{2,0},{3,1},{4,6},{5,7},{6,4},{7,5},{8,10},{9,11},{10,... | collective-permute-start | bytes 884744 | tf_op jit(solution)/shard_map/ppermute | solution.py:23
  61.0 17.5 %collective-permute-start.20 = (bf16[288,512]{1,0:T(8,128)(2,1)S(1)}, bf16[288,512]{1,0:T(8,128)(2,1)S(1)}, u32[]{:S(2)}, u32[]{:S(2)}) collective-permute-start(bf16[288,512]{1,0:T(8,128)(2,1)S(1)} %get-tuple-element.83), channel_id=1, source_target_pairs={{0,3},{1,0},{2,1},{3,2},{4,7},{5,4},{6,5},{7,6},{8,11},{9,8},{10,9... | collective-permute-start | bytes 884744 | tf_op jit(solution)/shard_map/ppermute | solution.py:23
  62.8 10.8 %collective-permute-start.22 = (bf16[256,512]{1,0:T(8,128)(2,1)S(1)}, bf16[256,512]{1,0:T(8,128)(2,1)S(1)}, u32[]{:S(2)}, u32[]{:S(2)}) collective-permute-start(bf16[256,512]{1,0:T(8,128)(2,1)S(1)} %get-tuple-element.86), channel_id=1, source_target_pairs={{0,128},{64,192},{128,0},{192,64},{1,129},{65,193},{129,1},{193,65... | collective-permute-start | bytes 786440 | tf_op jit(solution)/shard_map/ppermute | solution.py:23
  64.9 12.8 %collective-permute-start.23 = (bf16[256,512]{1,0:T(8,128)(2,1)S(1)}, bf16[256,512]{1,0:T(8,128)(2,1)S(1)}, u32[]{:S(2)}, u32[]{:S(2)}) collective-permute-start(bf16[256,512]{1,0:T(8,128)(2,1)S(1)} %get-tuple-element.71), channel_id=1, source_target_pairs={{0,64},{64,128},{128,192},{192,0},{1,65},{65,129},{129,193},{193,1... | collective-permute-start | bytes 786440 | tf_op jit(solution)/shard_map/ppermute | solution.py:23
  77.8 0.7 copy-start.4
  78.8 16.8 %all-to-all-start.1 = ((bf16[8,32,512]{2,1,0:T(8,128)(2,1)}), bf16[8,32,512]{2,1,0:T(8,128)(2,1)}, u32[]{:S(2)}, u32[]{:S(2)}) async-start(bf16[8,32,512]{2,1,0:T(8,128)(2,1)} %copy-done.4), calls=%async_computation.1 | async-start | bytes 524288 | tf_op jit(solution)/shard_map/all_to_all | solution.py:414
  85.8 12.3 %collective-permute-start.30 = (bf16[128,512]{1,0:T(8,128)(2,1)S(1)}, bf16[128,512]{1,0:T(8,128)(2,1)}, u32[]{:S(2)}, u32[]{:S(2)}) collective-permute-start(bf16[128,512]{1,0:T(8,128)(2,1)S(1)} %shard_map.103.refs_0_), channel_id=1, source_target_pairs={{0,3},{1,0},{2,1},{3,2},{4,7},{5,4},{6,5},{7,6},{8,11},{9,8},{10,9... | collective-permute-start | bytes 393224 | tf_op jit(solution)/shard_map/ppermute | solution.py:23
  86.6 11.6 %collective-permute-start.29 = (bf16[128,512]{1,0:T(8,128)(2,1)S(1)}, bf16[128,512]{1,0:T(8,128)(2,1)}, u32[]{:S(2)}, u32[]{:S(2)}) collective-permute-start(bf16[128,512]{1,0:T(8,128)(2,1)S(1)} %shard_map.103.refs_0_), channel_id=1, source_target_pairs={{0,2},{1,3},{2,0},{3,1},{4,6},{5,7},{6,4},{7,5},{8,10},{9,11},{10,... | collective-permute-start | bytes 393224 | tf_op jit(solution)/shard_map/ppermute | solution.py:23
  87.8 10.8 %collective-permute-start.28 = (bf16[128,512]{1,0:T(8,128)(2,1)S(1)}, bf16[128,512]{1,0:T(8,128)(2,1)}, u32[]{:S(2)}, u32[]{:S(2)}) collective-permute-start(bf16[128,512]{1,0:T(8,128)(2,1)S(1)} %shard_map.103.refs_0_), channel_id=1, source_target_pairs={{0,1},{1,2},{2,3},{3,0},{4,5},{5,6},{6,7},{7,4},{8,9},{9,10},{10,1... | collective-permute-start | bytes 393224 | tf_op jit(solution)/shard_map/ppermute | solution.py:23
  88.8 0.6 copy-start.5
  95.6 0.8 copy-start.6
  97.6 1.3 collective-permute-start.24
  97.7 2.0 %collective-permute-start.31 = (bf16[128,512]{1,0:T(8,128)(2,1)S(1)}, bf16[128,512]{1,0:T(8,128)(2,1)S(1)}, u32[]{:S(2)}, u32[]{:S(2)}) collective-permute-start(bf16[128,512]{1,0:T(8,128)(2,1)S(1)} %shard_map.103.refs_0_), channel_id=1, source_target_pairs={{0,16},{16,0},{1,17},{17,1},{2,18},{18,2},{3,19},{19,3},{4,20},{20... | collective-permute-start | bytes 393224 | tf_op jit(solution)/shard_map/ppermute | solution.py:43
  98.2 2.5 %collective-permute-start.34 = (bf16[128,512]{1,0:T(8,128)(2,1)}, bf16[128,512]{1,0:T(8,128)(2,1)S(1)}, u32[]{:S(2)}, u32[]{:S(2)}) collective-permute-start(bf16[128,512]{1,0:T(8,128)(2,1)} %collective-permute-done.30.refs_3_), channel_id=1, source_target_pairs={{0,16},{16,0},{1,17},{17,1},{2,18},{18,2},{3,19},{19,3},{4,20},{20... | collective-permute-start | bytes 393224 | tf_op jit(solution)/shard_map/ppermute | solution.py:43
  98.3 3.1 %collective-permute-start.33 = (bf16[128,512]{1,0:T(8,128)(2,1)}, bf16[128,512]{1,0:T(8,128)(2,1)S(1)}, u32[]{:S(2)}, u32[]{:S(2)}) collective-permute-start(bf16[128,512]{1,0:T(8,128)(2,1)} %collective-permute-done.29.refs_2_), channel_id=1, source_target_pairs={{0,16},{16,0},{1,17},{17,1},{2,18},{18,2},{3,19},{19,3},{4,20},{20... | collective-permute-start | bytes 393224 | tf_op jit(solution)/shard_map/ppermute | solution.py:43
  98.7 2.7 %collective-permute-start.32 = (bf16[128,512]{1,0:T(8,128)(2,1)}, bf16[128,512]{1,0:T(8,128)(2,1)S(1)}, u32[]{:S(2)}, u32[]{:S(2)}) collective-permute-start(bf16[128,512]{1,0:T(8,128)(2,1)} %collective-permute-done.28.refs_1_), channel_id=1, source_target_pairs={{0,16},{16,0},{1,17},{17,1},{2,18},{18,2},{3,19},{19,3},{4,20},{20... | collective-permute-start | bytes 393224 | tf_op jit(solution)/shard_map/ppermute | solution.py:43
  98.9 4.9 %collective-permute-start.27 = (bf16[64,512]{1,0:T(8,128)(2,1)S(1)}, bf16[64,512]{1,0:T(8,128)(2,1)S(1)}, u32[]{:S(2)}, u32[]{:S(2)}) collective-permute-start(bf16[64,512]{1,0:T(8,128)(2,1)S(1)} %pad_maximum_fusion.b0), channel_id=1, source_target_pairs={{0,3},{1,0},{2,1},{3,2},{4,7},{5,4},{6,5},{7,6},{8,11},{9,8},{10,9... | collective-permute-start | bytes 196616 | tf_op jit(solution)/shard_map/ppermute | solution.py:23
  99.7 5.8 %collective-permute-start.26 = (bf16[64,512]{1,0:T(8,128)(2,1)S(1)}, bf16[64,512]{1,0:T(8,128)(2,1)S(1)}, u32[]{:S(2)}, u32[]{:S(2)}) collective-permute-start(bf16[64,512]{1,0:T(8,128)(2,1)S(1)} %pad_maximum_fusion.b0), channel_id=1, source_target_pairs={{0,2},{1,3},{2,0},{3,1},{4,6},{5,7},{6,4},{7,5},{8,10},{9,11},{10,... | collective-permute-start | bytes 196616 | tf_op jit(solution)/shard_map/ppermute | solution.py:23
  100.7 6.1 %collective-permute-start.25 = (bf16[64,512]{1,0:T(8,128)(2,1)S(1)}, bf16[64,512]{1,0:T(8,128)(2,1)S(1)}, u32[]{:S(2)}, u32[]{:S(2)}) collective-permute-start(bf16[64,512]{1,0:T(8,128)(2,1)S(1)} %pad_maximum_fusion.b0), channel_id=1, source_target_pairs={{0,1},{1,2},{2,3},{3,0},{4,5},{5,6},{6,7},{7,4},{8,9},{9,10},{10,1... | collective-permute-start | bytes 196616 | tf_op jit(solution)/shard_map/ppermute | solution.py:23
  108.1 6.4 %collective-permute-start.35 = (bf16[64,1024]{1,0:T(8,128)(2,1)S(1)}, bf16[64,1024]{1,0:T(8,128)(2,1)S(1)}, u32[]{:S(2)}, u32[]{:S(2)}) collective-permute-start(bf16[64,1024]{1,0:T(8,128)(2,1)S(1)} %get-tuple-element.92), channel_id=1, source_target_pairs={{0,192},{64,0},{128,64},{192,128},{1,193},{65,1},{129,65},{193,129... | collective-permute-start | bytes 393224 | tf_op jit(solution)/shard_map/ppermute | solution.py:23
  108.5 7.5 %collective-permute-start.36 = (bf16[64,1024]{1,0:T(8,128)(2,1)S(1)}, bf16[64,1024]{1,0:T(8,128)(2,1)S(1)}, u32[]{:S(2)}, u32[]{:S(2)}) collective-permute-start(bf16[64,1024]{1,0:T(8,128)(2,1)S(1)} %get-tuple-element.93), channel_id=1, source_target_pairs={{0,128},{64,192},{128,0},{192,64},{1,129},{65,193},{129,1},{193,65... | collective-permute-start | bytes 393224 | tf_op jit(solution)/shard_map/ppermute | solution.py:23
  109.2 8.7 %collective-permute-start.37 = (bf16[64,1024]{1,0:T(8,128)(2,1)S(1)}, bf16[64,1024]{1,0:T(8,128)(2,1)S(1)}, u32[]{:S(2)}, u32[]{:S(2)}) collective-permute-start(bf16[64,1024]{1,0:T(8,128)(2,1)S(1)} %get-tuple-element.94), channel_id=1, source_target_pairs={{0,64},{64,128},{128,192},{192,0},{1,65},{65,129},{129,193},{193,1... | collective-permute-start | bytes 393224 | tf_op jit(solution)/shard_map/ppermute | solution.py:23

commit v4 on v2

--- a/solution.py
+++ b/solution.py
@@ -47,14 +47,14 @@
 SM = functools.partial(pl.BlockSpec, memory_space=pltpu.SMEM)
 
 
-def call(body, outs, ins, scratch=(), flops=1 << 20, smem=0, moved=1 << 20):
+def call(body, outs, ins, scratch=(), flops=1 << 20, smem=0, moved=1 << 20, limit=16):
     return pl.pallas_call(
         body,
         out_shape=tuple(jax.ShapeDtypeStruct(s, d) for s, d in outs),
         in_specs=[SM()] * smem + [VM()] * (len(ins) - smem),
         out_specs=tuple(VM() for _ in outs),
         scratch_shapes=list(scratch),
-        compiler_params=pltpu.CompilerParams(vmem_limit_bytes=16 * 1024 * 1024),
+        compiler_params=pltpu.CompilerParams(vmem_limit_bytes=limit * 1024 * 1024),
         cost_estimate=pl.CostEstimate(flops=flops, bytes_accessed=moved, transcendentals=0),
     )(*ins)
 
@@ -311,9 +311,9 @@
     out_ref[...] = total.astype(BF).reshape(out_ref.shape)
 
 
-def scatter_y(parts, shape):
+def scatter_y(parts, shape, limit=16):
     came = [shift(parts[k], 4 - k, "y") for k in (1, 2, 3)]
-    return call(add_body, [(shape, BF)], [parts[0], *came])[0]
+    return call(add_body, [(shape, BF)], [parts[0], *came], limit=limit)[0]
 
 
 def split_body(parts_ref, query_ref, item_ref):
@@ -411,7 +411,7 @@
         flops=2 * 32 * TOWER * EMBED,
     )[0]
     item_part = lax.all_to_all(item_part, ("zl", "zh"), 0, 0, tiled=True)
-    item_back = call(item_back_body, [((32, EMBED), BF)], [item_raw, item_part])[0]
+    item_back = call(item_back_body, [((32, EMBED), BF)], [item_raw, item_part], limit=60)[0]
     item_backs = slots(item_back)
 
     parts = call(

time: 131 us -> 131 us (level)
    unnamed x28 -> x26, local copies, waits for them, and re-layouts: 3.99 us -> 3.11 us
  transfers between devices with their start and end apart: 37 -> 37, of which waited for: 21 -> 21; matrix products, arithmetic and copies ran while one was open for 0% -> 1% of each run, Pallas kernels for 7% -> 7%
where the time goes in v4:
time: 131 us; the launch traced here: 129 us
  waiting for transfers between devices  47.5 us (36%)
  starting transfers between devices  42.8 us (33%)
  Pallas kernels  21.6 us (16%)
  blocking collectives  12.6 us (10%)
  local copies, waits for them, and re-layouts  3.12 us (2%)
    ppermute x24, waiting for transfers between devices, shift(): return lax.ppermute(value, axis, [(i, (i + step) % 4) for i in range(4)])  34.4 us
    ppermute x24, starting transfers between devices, shift(): return lax.ppermute(value, axis, [(i, (i + step) % 4) for i in range(4)])  28.7 us
    pallas_call x15, Pallas kernels, call(): pl.pallas_call(body, out_shape=tuple((jax.ShapeDtypeStruct(s, d) for s, d...  18.8 us
    all_to_all x1, blocking collectives, local(): part = lax.all_to_all(part, ('zl', 'zh'), 0, 0, tiled=True)  12.6 us
    all_to_all x1, starting transfers between devices, local(): lax.all_to_all(item_units, ('zl', 'zh'), 0, 0, tiled=True)  6.73 us
    all_to_all x1, starting transfers between devices, local(): item_part = lax.all_to_all(item_part, ('zl', 'zh'), 0, 0, tiled=True)  5.64 us
    all_to_all x1, waiting for transfers between devices, local(): item_part = lax.all_to_all(item_part, ('zl', 'zh'), 0, 0, tiled=True)  5.34 us
    all_to_all x1, waiting for transfers between devices, local(): lax.all_to_all(item_units, ('zl', 'zh'), 0, 0, tiled=True)  3.91 us
  transfers between devices with their start and end apart: 37, of which 21 were waited for; matrix products, arithmetic and copies ran while one was open for 1% of the time, Pallas kernels for 7%

profile of v4, /device:TPU:0, one launch (start us, length us, event | category | flops | bytes accessed | tf_op | source)
XLA Modules:
  0.0 129.4 jit_solution(11785318397113961270)
XLA Ops:
  0.7 2.8 %shard_map.94 = bf16[8,32,512]{2,1,0:T(8,128)(2,1)} custom-call(bf16[32,2048]{1,0:T(8,128)(2,1)} %hidden_ref.1, bf16[2048,512]{1,0:T(8,128)(2,1)} %weight_ref.3), custom_call_target="tpu_custom_call" | custom-call | flops 67108864 | bytes 2097152 | tf_op jit(solution)/shard_map/pallas_call | solution.py:86
  3.5 1.0 copy-done.2
  4.6 1.1 shard_map.95
  5.7 0.7 copy-done.7
  6.4 6.7 %all-to-all-start = ((bf16[8,32,512]{2,1,0:T(8,128)(2,1)}), bf16[8,32,512]{2,1,0:T(8,128)(2,1)S(1)}, u32[]{:S(2)}, u32[]{:S(2)}) async-start(bf16[8,32,512]{2,1,0:T(8,128)(2,1)} %shard_map.94), calls=%async_computation | async-start | bytes 524288 | tf_op jit(solution)/shard_map/all_to_all | solution.py:333
  13.2 2.8 %collective-permute-start.4 = (bf16[256,512]{1,0:T(8,128)(2,1)S(1)}, bf16[256,512]{1,0:T(8,128)(2,1)S(1)}, u32[]{:S(2)}, u32[]{:S(2)}) collective-permute-start(bf16[256,512]{1,0:T(8,128)(2,1)S(1)} %constant_dynamic-update-slice_fusion.refs_0_), channel_id=1, source_target_pairs={{0,3},{1,0},{2,1},{3,2},{4,7},{5,4},{6,5},{7,6},{8,11},{9,8},{10,9... | collective-permute-start | bytes 786440 | tf_op jit(solution)/shard_map/ppermute | solution.py:23
  16.0 0.8 collective-permute-start.3
  16.8 1.4 %shard_map.96 = (bf16[160,256]{1,0:T(8,128)(2,1)S(1)}, bf16[160,256]{1,0:T(8,128)(2,1)S(1)}, bf16[160,256]{1,0:T(8,128)(2,1)S(1)}, bf16[160,256]{1,0:T(8,128)(2,1)S(1)}, bf16[4,160,256]{2,1,0:T(8,128)(2,1)S(1)}) custom-call(s32[4]{0:T(128)S(1)} %pad_add_fusion.place_ref, bf16[128,2048]{1,0:T(8,128)(2,1)S(1)} %copy-done.3, bf16[32,2048]{1,0:T(8,128)(2,1)S(1)} %copy-done.4), custom_call_target="tpu_custom_call" | custom-call | flops 1 | bytes 1 | tf_op jit(solution)/shard_map/pallas_call | solution.py:51
  18.2 1.0 collective-permute-start.2
  19.2 3.9 %all-to-all-done = bf16[8,32,512]{2,1,0:T(8,128)(2,1)S(1)} async-done(((bf16[8,32,512]{2,1,0:T(8,128)(2,1)}), bf16[8,32,512]{2,1,0:T(8,128)(2,1)S(1)}, u32[]{:S(2)}, u32[]{:S(2)}) %all-to-all-start) | async-done | bytes 262176 | tf_op jit(solution)/shard_map/all_to_all | solution.py:333
  23.1 3.0 %collective-permute-start.7 = (bf16[256,512]{1,0:T(8,128)(2,1)S(1)}, bf16[256,512]{1,0:T(8,128)(2,1)S(1)}, u32[]{:S(2)}, u32[]{:S(2)}) collective-permute-start(bf16[256,512]{1,0:T(8,128)(2,1)S(1)} %bitcast.8), channel_id=1, source_target_pairs={{0,192},{64,0},{128,64},{192,128},{1,193},{65,1},{129,65},{193,129... | collective-permute-start | bytes 786440 | tf_op jit(solution)/shard_map/ppermute | solution.py:23
  26.1 0.6 collective-permute-start.6
  26.7 0.9 collective-permute-done.4.refs_3_
  27.6 1.6 %collective-permute-start.5 = (bf16[256,512]{1,0:T(8,128)(2,1)S(1)}, bf16[256,512]{1,0:T(8,128)(2,1)S(1)}, u32[]{:S(2)}, u32[]{:S(2)}) collective-permute-start(bf16[256,512]{1,0:T(8,128)(2,1)S(1)} %bitcast.10), channel_id=1, source_target_pairs={{0,64},{64,128},{128,192},{192,0},{1,65},{65,129},{129,193},{193,1... | collective-permute-start | bytes 786440 | tf_op jit(solution)/shard_map/ppermute | solution.py:23
  29.2 2.1 %collective-permute-done.2.refs_1_ = bf16[256,512]{1,0:T(8,128)(2,1)S(1)} collective-permute-done((bf16[256,512]{1,0:T(8,128)(2,1)S(1)}, bf16[256,512]{1,0:T(8,128)(2,1)S(1)}, u32[]{:S(2)}, u32[]{:S(2)}) %collective-permute-start.2) | collective-permute-done | bytes 262176 | tf_op jit(solution)/shard_map/ppermute | solution.py:23
  31.3 1.1 collective-permute-done.other_tiles
  32.4 3.4 %collective-permute-done.7.refs_7_.i3 = bf16[256,512]{1,0:T(8,128)(2,1)S(1)} collective-permute-done((bf16[256,512]{1,0:T(8,128)(2,1)S(1)}, bf16[256,512]{1,0:T(8,128)(2,1)S(1)}, u32[]{:S(2)}, u32[]{:S(2)}) %collective-permute-start.7) | collective-permute-done | bytes 262176 | tf_op jit(solution)/shard_map/ppermute | solution.py:23
  35.8 0.3 collective-permute-done.6.refs_6_.i2
  36.1 3.4 %collective-permute-done.5.refs_5_.i1 = bf16[256,512]{1,0:T(8,128)(2,1)S(1)} collective-permute-done((bf16[256,512]{1,0:T(8,128)(2,1)S(1)}, bf16[256,512]{1,0:T(8,128)(2,1)S(1)}, u32[]{:S(2)}, u32[]{:S(2)}) %collective-permute-start.5) | collective-permute-done | bytes 262176 | tf_op jit(solution)/shard_map/ppermute | solution.py:23
  39.5 3.8 %shard_map.97 = (bf16[1024,1024]{1,0:T(8,128)(2,1)S(1)}, f32[16,128]{1,0:T(8,128)S(1)}, bf16[1024,512]{1,0:T(8,128)(2,1)S(1)}, s32[1,1024]{1,0:T(1,128)S(1)}) custom-call(s32[4]{0:T(128)S(1)} %pad_add_fusion.place_ref, s32[4,8]{1,0:T(4,128)S(1)} %copy-done.11, s32[4,8]{1,0:T(4,128)S(1)} %collective-permute-done.other_tiles, ...), custom_call_target="tpu_custom_call" | custom-call | flops 1073741824 | bytes 1048576 | tf_op jit(solution)/shard_map/pallas_call | solution.py:51
  43.4 1.1 collective-permute-done.9
  44.6 2.9 %collective-permute-start.12 = (f32[32,128]{1,0:T(8,128)S(1)}, f32[32,128]{1,0:T(8,128)S(1)}, u32[]{:S(2)}, u32[]{:S(2)}) collective-permute-start(f32[32,128]{1,0:T(8,128)S(1)} %constant_dynamic-update-slice_fusion.2.s0), channel_id=1, source_target_pairs={{0,3},{1,0},{2,1},{3,2},{4,7},{5,4},{6,5},{7,6},{8,11},{9,8},{10,9... | collective-permute-start | bytes 49160 | tf_op jit(solution)/shard_map/ppermute | solution.py:23
  47.4 0.7 collective-permute-start.11
  48.1 0.9 collective-permute-start.10
  49.0 3.4 %shard_map.98 = (f32[1024,512]{1,0:T(8,128)S(1)}, f32[1024,512]{1,0:T(8,128)S(1)}, f32[1024,512]{1,0:T(8,128)S(1)}) custom-call(s32[1,1024]{1,0:T(1,128)S(1)} %get-tuple-element.54.hit_ref, bf16[1024,1024]{1,0:T(8,128)(2,1)S(1)} %get-tuple-element.55.exp_ref, bf16[256,512]{1,0:T(8,128)(2,1)S(1)} %bitcast.12, ...), custom_call_target="tpu_custom_call" | custom-call | flops 3221225472 | bytes 1048576 | tf_op jit(solution)/shard_map/pallas_call | solution.py:51
  52.7 0.4 collective-permute-done.10.s1
  53.1 1.7 %shard_map.99 = (f32[256,512]{1,0:T(8,128)S(1)}, bf16[256,512]{1,0:T(8,128)(2,1)S(1)}, bf16[256,512]{1,0:T(8,128)(2,1)S(1)}, bf16[256,512]{1,0:T(8,128)(2,1)S(1)}) custom-call(f32[32,128]{1,0:T(8,128)S(1)} %constant_dynamic-update-slice_fusion.2.s0, f32[32,128]{1,0:T(8,128)S(1)} %collective-permute-done.10.s1, f32[32,128]{1,0:T(8,128)S(1)} %collective-permute-done.11.s2, ...), custom_call_target="tpu_custom_call" | custom-call | flops 1073741824 | bytes 1048576 | tf_op jit(solution)/shard_map/pallas_call | solution.py:51
  54.7 0.9 shard_map.100
  55.7 0.5 collective-permute-start.14
  56.2 0.6 collective-permute-start.18
  56.8 1.3 collective-permute-done.14.other_ref
  58.2 1.4 %collective-permute-start.15 = (bf16[288,512]{1,0:T(8,128)(2,1)S(1)}, bf16[288,512]{1,0:T(8,128)(2,1)S(1)}, u32[]{:S(2)}, u32[]{:S(2)}) collective-permute-start(bf16[288,512]{1,0:T(8,128)(2,1)S(1)} %get-tuple-element.71), channel_id=1, source_target_pairs={{0,1},{1,2},{2,3},{3,0},{4,5},{5,6},{6,7},{7,4},{8,9},{9,10},{10,1... | collective-permute-start | bytes 884744 | tf_op jit(solution)/shard_map/ppermute | solution.py:23
  59.6 1.9 %collective-permute-start.16 = (bf16[288,512]{1,0:T(8,128)(2,1)S(1)}, bf16[288,512]{1,0:T(8,128)(2,1)S(1)}, u32[]{:S(2)}, u32[]{:S(2)}) collective-permute-start(bf16[288,512]{1,0:T(8,128)(2,1)S(1)} %get-tuple-element.72), channel_id=1, source_target_pairs={{0,2},{1,3},{2,0},{3,1},{4,6},{5,7},{6,4},{7,5},{8,10},{9,11},{10,... | collective-permute-start | bytes 884744 | tf_op jit(solution)/shard_map/ppermute | solution.py:23
  61.5 1.0 collective-permute-start.17
  62.5 0.7 collective-permute-start.19
  63.2 1.6 %collective-permute-done.18.p1 = bf16[256,512]{1,0:T(8,128)(2,1)S(1)} collective-permute-done((bf16[256,512]{1,0:T(8,128)(2,1)S(1)}, bf16[256,512]{1,0:T(8,128)(2,1)S(1)}, u32[]{:S(2)}, u32[]{:S(2)}) %collective-permute-start.18) | collective-permute-done | bytes 262176 | tf_op jit(solution)/shard_map/ppermute | solution.py:23
  64.8 8.5 %collective-permute-done.19.p2 = bf16[256,512]{1,0:T(8,128)(2,1)S(1)} collective-permute-done((bf16[256,512]{1,0:T(8,128)(2,1)S(1)}, bf16[256,512]{1,0:T(8,128)(2,1)S(1)}, u32[]{:S(2)}, u32[]{:S(2)}) %collective-permute-start.19) | collective-permute-done | bytes 262176 | tf_op jit(solution)/shard_map/ppermute | solution.py:23
  73.3 4.0 %collective-permute-done.20.p3 = bf16[256,512]{1,0:T(8,128)(2,1)S(1)} collective-permute-done((bf16[256,512]{1,0:T(8,128)(2,1)S(1)}, bf16[256,512]{1,0:T(8,128)(2,1)S(1)}, u32[]{:S(2)}, u32[]{:S(2)}) %collective-permute-start.20) | collective-permute-done | bytes 262176 | tf_op jit(solution)/shard_map/ppermute | solution.py:23
  77.4 0.7 copy-done.5
  78.4 5.6 %all-to-all-start.1 = ((bf16[8,32,512]{2,1,0:T(8,128)(2,1)}), bf16[8,32,512]{2,1,0:T(8,128)(2,1)}, u32[]{:S(2)}, u32[]{:S(2)}) async-start(bf16[8,32,512]{2,1,0:T(8,128)(2,1)} %copy-done.5), calls=%async_computation.1 | async-start | bytes 524288 | tf_op jit(solution)/shard_map/all_to_all | solution.py:413
  84.0 1.0 collective-permute-start.27
  85.0 2.0 %collective-permute-start.26 = (bf16[128,512]{1,0:T(8,128)(2,1)S(1)}, bf16[128,512]{1,0:T(8,128)(2,1)}, u32[]{:S(2)}, u32[]{:S(2)}) collective-permute-start(bf16[128,512]{1,0:T(8,128)(2,1)S(1)} %shard_map.103.refs_0_), channel_id=1, source_target_pairs={{0,2},{1,3},{2,0},{3,1},{4,6},{5,7},{6,4},{7,5},{8,10},{9,11},{10,... | collective-permute-start | bytes 393224 | tf_op jit(solution)/shard_map/ppermute | solution.py:23
  87.3 0.4 shard_map.104.raw_ref
  87.8 0.6 copy-done.6
  88.4 5.3 %all-to-all-done.1.grads_ref = bf16[8,32,512]{2,1,0:T(8,128)(2,1)} async-done(((bf16[8,32,512]{2,1,0:T(8,128)(2,1)}), bf16[8,32,512]{2,1,0:T(8,128)(2,1)}, u32[]{:S(2)}, u32[]{:S(2)}) %all-to-all-start.1) | async-done | bytes 262176 | tf_op jit(solution)/shard_map/all_to_all | solution.py:413
  93.8 1.8 %shard_map.105 = bf16[32,512]{1,0:T(8,128)(2,1)} custom-call(f32[32,512]{1,0:T(8,128)} %copy-done.6, bf16[8,32,512]{2,1,0:T(8,128)(2,1)} %all-to-all-done.1.grads_ref), custom_call_target="tpu_custom_call" | custom-call | flops 1048576 | bytes 1048576 | tf_op jit(solution)/shard_map/pallas_call | solution.py:51
  95.5 0.5 collective-permute-start.28
  96.1 0.5 collective-permute-start.30
  96.7 0.3 collective-permute-done.21
  97.0 0.8 pad_maximum_fusion.b0
  97.7 0.7 collective-permute-start.24
  98.5 2.2 %collective-permute-start.23 = (bf16[64,512]{1,0:T(8,128)(2,1)S(1)}, bf16[64,512]{1,0:T(8,128)(2,1)S(1)}, u32[]{:S(2)}, u32[]{:S(2)}) collective-permute-start(bf16[64,512]{1,0:T(8,128)(2,1)S(1)} %pad_maximum_fusion.b0), channel_id=1, source_target_pairs={{0,2},{1,3},{2,0},{3,1},{4,6},{5,7},{6,4},{7,5},{8,10},{9,11},{10,... | collective-permute-start | bytes 196616 | tf_op jit(solution)/shard_map/ppermute | solution.py:23
  100.7 0.4 collective-permute-start.22
  101.1 1.7 %shard_map.106.query_ref = f32[256,512]{1,0:T(8,128)S(1)} custom-call(bf16[288,512]{1,0:T(8,128)(2,1)S(1)} %get-tuple-element.70.h0, bf16[288,512]{1,0:T(8,128)(2,1)S(1)} %collective-permute-done.15.v1.h1, bf16[288,512]{1,0:T(8,128)(2,1)S(1)} %collective-permute-done.16.v2.h2, bf16[288,512]{1,0:T(8,128)(2,1)S(1)} %collective-permute-done.17.v3.h3, ...), custom_call_target="tpu_custom_call" | custom-call | flops 268435456 | bytes 4194304 | tf_op jit(solution)/shard_map/pallas_call | solution.py:51
  102.9 1.7 %collective-permute-done.23.b2 = bf16[64,512]{1,0:T(8,128)(2,1)S(1)} collective-permute-done((bf16[64,512]{1,0:T(8,128)(2,1)S(1)}, bf16[64,512]{1,0:T(8,128)(2,1)S(1)}, u32[]{:S(2)}, u32[]{:S(2)}) %collective-permute-start.23) | collective-permute-done | bytes 65568 | tf_op jit(solution)/shard_map/ppermute | solution.py:23
  104.5 1.7 %collective-permute-done.22.b1 = bf16[64,512]{1,0:T(8,128)(2,1)S(1)} collective-permute-done((bf16[64,512]{1,0:T(8,128)(2,1)S(1)}, bf16[64,512]{1,0:T(8,128)(2,1)S(1)}, u32[]{:S(2)}, u32[]{:S(2)}) %collective-permute-start.22) | collective-permute-done | bytes 65568 | tf_op jit(solution)/shard_map/ppermute | solution.py:23
  106.2 1.3 %shard_map.107 = (f32[64,1024]{1,0:T(8,128)S(1)}, bf16[64,1024]{1,0:T(8,128)(2,1)S(1)}, bf16[64,1024]{1,0:T(8,128)(2,1)S(1)}, bf16[64,1024]{1,0:T(8,128)(2,1)S(1)}) custom-call(s32[4]{0:T(128)S(1)} %pad_add_fusion.place_ref, bf16[288,512]{1,0:T(8,128)(2,1)S(1)} %get-tuple-element.70.h0, bf16[288,512]{1,0:T(8,128)(2,1)S(1)} %collective-permute-done.15.v1.h1, ...), custom_call_target="tpu_custom_call" | custom-call | flops 67108864 | bytes 1048576 | tf_op jit(solution)/shard_map/pallas_call | solution.py:51
  107.6 0.9 collective-permute-start.33
  108.5 1.3 collective-permute-start.34
  109.7 3.3 %collective-permute-done.32.p1 = bf16[64,1024]{1,0:T(8,128)(2,1)S(1)} collective-permute-done((bf16[64,1024]{1,0:T(8,128)(2,1)S(1)}, bf16[64,1024]{1,0:T(8,128)(2,1)S(1)}, u32[]{:S(2)}, u32[]{:S(2)}) %collective-permute-start.32) | collective-permute-done | bytes 131104 | tf_op jit(solution)/shard_map/ppermute | solution.py:23
  113.1 2.2 %collective-permute-done.33.p2 = bf16[64,1024]{1,0:T(8,128)(2,1)S(1)} collective-permute-done((bf16[64,1024]{1,0:T(8,128)(2,1)S(1)}, bf16[64,1024]{1,0:T(8,128)(2,1)S(1)}, u32[]{:S(2)}, u32[]{:S(2)}) %collective-permute-start.33) | collective-permute-done | bytes 131104 | tf_op jit(solution)/shard_map/ppermute | solution.py:23
  115.2 0.8 collective-permute-done.34.p3
  116.1 12.6 %all_to_all.15.parts_ref = bf16[8,8,1024]{2,1,0:T(8,128)(2,1)S(1)} all-to-all(bf16[8,8,1024]{2,1,0:T(8,128)(2,1)S(1)} %shard_map.108), channel_id=1, replica_groups=mesh['y'=4,'zl'=2,'c'=2,'zh'=4,'x'=4] {'zl','zh'}, dimensions={0} | all-to-all | bytes 262144 | tf_op jit(solution)/shard_map/all_to_all | solution.py:426
  128.8 0.6 shard_map.109
  (57 shorter events, 1.5 us)
Async XLA Ops:
  0.6 2.9 %copy-start.9 = (s32[8192]{0:T(1024)S(1)}, s32[8192]{0:T(1024)}, u32[]{:S(2)}) copy-start(s32[8192]{0:T(1024)} %param.12) | copy-start | bytes 98308
  0.6 2.9 %copy-start.1 = (bf16[2048,512]{1,0:T(8,128)(2,1)S(1)}, bf16[2048,512]{1,0:T(8,128)(2,1)}, u32[]{:S(2)}) copy-start(bf16[2048,512]{1,0:T(8,128)(2,1)} %weight_ref.2) | copy-start | bytes 6291460
  0.7 16.1 %copy-start.4 = (bf16[32,2048]{1,0:T(8,128)(2,1)S(1)}, bf16[32,2048]{1,0:T(8,128)(2,1)}, u32[]{:S(2)}) copy-start(bf16[32,2048]{1,0:T(8,128)(2,1)} %hidden_ref.1) | copy-start | bytes 393220
  3.5 1.0 copy-start.2
  4.6 12.2 %copy-start.3 = (bf16[128,2048]{1,0:T(8,128)(2,1)S(1)}, bf16[128,2048]{1,0:T(8,128)(2,1)}, u32[]{:S(2)}) copy-start(bf16[128,2048]{1,0:T(8,128)(2,1)} %query_ref.1) | copy-start | bytes 1572868
  4.6 24.6 %copy-start.10 = (s32[2048]{0:T(1024)S(1)}, s32[2048]{0:T(1024)}, u32[]{:S(2)}) copy-start(s32[2048]{0:T(1024)} %param.13) | copy-start | bytes 24580
  4.6 26.7 %copy-start.11 = (s32[4,8]{1,0:T(4,128)S(1)}, s32[4,8]{1,0:T(4,128)}, u32[]{:S(2)}) copy-start(s32[4,8]{1,0:T(4,128)} %own_tiles) | copy-start | bytes 388
  5.7 0.7 copy-start.7
  6.4 6.8 %collective-permute-start.1 = (bf16[128,512]{1,0:T(8,128)(2,1)S(1)}, bf16[128,512]{1,0:T(8,128)(2,1)S(1)}, u32[]{:S(2)}, u32[]{:S(2)}) collective-permute-start(bf16[128,512]{1,0:T(8,128)(2,1)S(1)} %get-tuple-element.46), channel_id=1, source_target_pairs={{0,16},{16,0},{1,17},{17,1},{2,18},{18,2},{3,19},{19,3},{4,20},{20... | collective-permute-start | bytes 393224 | tf_op jit(solution)/shard_map/ppermute | solution.py:43
  6.4 16.7 %all-to-all-start = ((bf16[8,32,512]{2,1,0:T(8,128)(2,1)}), bf16[8,32,512]{2,1,0:T(8,128)(2,1)S(1)}, u32[]{:S(2)}, u32[]{:S(2)}) async-start(bf16[8,32,512]{2,1,0:T(8,128)(2,1)} %shard_map.94), calls=%async_computation | async-start | bytes 524288 | tf_op jit(solution)/shard_map/all_to_all | solution.py:333
  13.2 14.4 %collective-permute-start.4 = (bf16[256,512]{1,0:T(8,128)(2,1)S(1)}, bf16[256,512]{1,0:T(8,128)(2,1)S(1)}, u32[]{:S(2)}, u32[]{:S(2)}) collective-permute-start(bf16[256,512]{1,0:T(8,128)(2,1)S(1)} %constant_dynamic-update-slice_fusion.refs_0_), channel_id=1, source_target_pairs={{0,3},{1,0},{2,1},{3,2},{4,7},{5,4},{6,5},{7,6},{8,11},{9,8},{10,9... | collective-permute-start | bytes 786440 | tf_op jit(solution)/shard_map/ppermute | solution.py:23
  16.0 13.2 %collective-permute-start.3 = (bf16[256,512]{1,0:T(8,128)(2,1)S(1)}, bf16[256,512]{1,0:T(8,128)(2,1)S(1)}, u32[]{:S(2)}, u32[]{:S(2)}) collective-permute-start(bf16[256,512]{1,0:T(8,128)(2,1)S(1)} %constant_dynamic-update-slice_fusion.refs_0_), channel_id=1, source_target_pairs={{0,2},{1,3},{2,0},{3,1},{4,6},{5,7},{6,4},{7,5},{8,10},{9,11},{10,... | collective-permute-start | bytes 786440 | tf_op jit(solution)/shard_map/ppermute | solution.py:23
  18.2 13.1 %collective-permute-start.2 = (bf16[256,512]{1,0:T(8,128)(2,1)S(1)}, bf16[256,512]{1,0:T(8,128)(2,1)S(1)}, u32[]{:S(2)}, u32[]{:S(2)}) collective-permute-start(bf16[256,512]{1,0:T(8,128)(2,1)S(1)} %constant_dynamic-update-slice_fusion.refs_0_), channel_id=1, source_target_pairs={{0,1},{1,2},{2,3},{3,0},{4,5},{5,6},{6,7},{7,4},{8,9},{9,10},{10,1... | collective-permute-start | bytes 786440 | tf_op jit(solution)/shard_map/ppermute | solution.py:23
  23.1 12.7 %collective-permute-start.7 = (bf16[256,512]{1,0:T(8,128)(2,1)S(1)}, bf16[256,512]{1,0:T(8,128)(2,1)S(1)}, u32[]{:S(2)}, u32[]{:S(2)}) collective-permute-start(bf16[256,512]{1,0:T(8,128)(2,1)S(1)} %bitcast.8), channel_id=1, source_target_pairs={{0,192},{64,0},{128,64},{192,128},{1,193},{65,1},{129,65},{193,129... | collective-permute-start | bytes 786440 | tf_op jit(solution)/shard_map/ppermute | solution.py:23
  26.1 10.0 %collective-permute-start.6 = (bf16[256,512]{1,0:T(8,128)(2,1)S(1)}, bf16[256,512]{1,0:T(8,128)(2,1)S(1)}, u32[]{:S(2)}, u32[]{:S(2)}) collective-permute-start(bf16[256,512]{1,0:T(8,128)(2,1)S(1)} %bitcast.9), channel_id=1, source_target_pairs={{0,128},{64,192},{128,0},{192,64},{1,129},{65,193},{129,1},{193,65... | collective-permute-start | bytes 786440 | tf_op jit(solution)/shard_map/ppermute | solution.py:23
  27.6 11.9 %collective-permute-start.5 = (bf16[256,512]{1,0:T(8,128)(2,1)S(1)}, bf16[256,512]{1,0:T(8,128)(2,1)S(1)}, u32[]{:S(2)}, u32[]{:S(2)}) collective-permute-start(bf16[256,512]{1,0:T(8,128)(2,1)S(1)} %bitcast.10), channel_id=1, source_target_pairs={{0,64},{64,128},{128,192},{192,0},{1,65},{65,129},{129,193},{193,1... | collective-permute-start | bytes 786440 | tf_op jit(solution)/shard_map/ppermute | solution.py:23
  29.2 3.3 %collective-permute-start.8 = (s32[16,128]{1,0:T(8,128)S(1)}, s32[16,128]{1,0:T(8,128)S(1)}, u32[]{:S(2)}, u32[]{:S(2)}) collective-permute-start(s32[16,128]{1,0:T(8,128)S(1)} %bitcast.14), channel_id=1, source_target_pairs={{0,16},{16,0},{1,17},{17,1},{2,18},{18,2},{3,19},{19,3},{4,20},{20... | collective-permute-start | bytes 24584 | tf_op jit(solution)/shard_map/ppermute | solution.py:43
  31.3 1.2 collective-permute-start
  43.3 1.3 collective-permute-start.9
  44.6 7.9 %collective-permute-start.12 = (f32[32,128]{1,0:T(8,128)S(1)}, f32[32,128]{1,0:T(8,128)S(1)}, u32[]{:S(2)}, u32[]{:S(2)}) collective-permute-start(f32[32,128]{1,0:T(8,128)S(1)} %constant_dynamic-update-slice_fusion.2.s0), channel_id=1, source_target_pairs={{0,3},{1,0},{2,1},{3,2},{4,7},{5,4},{6,5},{7,6},{8,11},{9,8},{10,9... | collective-permute-start | bytes 49160 | tf_op jit(solution)/shard_map/ppermute | solution.py:23
  47.4 5.2 %collective-permute-start.11 = (f32[32,128]{1,0:T(8,128)S(1)}, f32[32,128]{1,0:T(8,128)S(1)}, u32[]{:S(2)}, u32[]{:S(2)}) collective-permute-start(f32[32,128]{1,0:T(8,128)S(1)} %constant_dynamic-update-slice_fusion.2.s0), channel_id=1, source_target_pairs={{0,2},{1,3},{2,0},{3,1},{4,6},{5,7},{6,4},{7,5},{8,10},{9,11},{10,... | collective-permute-start | bytes 49160 | tf_op jit(solution)/shard_map/ppermute | solution.py:23
  48.1 5.0 %collective-permute-start.10 = (f32[32,128]{1,0:T(8,128)S(1)}, f32[32,128]{1,0:T(8,128)S(1)}, u32[]{:S(2)}, u32[]{:S(2)}) collective-permute-start(f32[32,128]{1,0:T(8,128)S(1)} %constant_dynamic-update-slice_fusion.2.s0), channel_id=1, source_target_pairs={{0,1},{1,2},{2,3},{3,0},{4,5},{5,6},{6,7},{7,4},{8,9},{9,10},{10,1... | collective-permute-start | bytes 49160 | tf_op jit(solution)/shard_map/ppermute | solution.py:23
  55.7 22.4 %copy-start.8 = (f32[128,512]{1,0:T(8,128)S(1)}, f32[128,512]{1,0:T(8,128)}, u32[]{:S(2)}) copy-start(f32[128,512]{1,0:T(8,128)} %copy-done.7) | copy-start | bytes 786436
  55.7 2.4 %collective-permute-start.13 = (bf16[512,512]{1,0:T(8,128)(2,1)S(1)}, bf16[512,512]{1,0:T(8,128)(2,1)S(1)}, u32[]{:S(2)}, u32[]{:S(2)}) collective-permute-start(bf16[512,512]{1,0:T(8,128)(2,1)S(1)} %get-tuple-element.64), channel_id=1, source_target_pairs={{0,16},{16,0},{1,17},{17,1},{2,18},{18,2},{3,19},{19,3},{4,20},{20... | collective-permute-start | bytes 1572872 | tf_op jit(solution)/shard_map/ppermute | solution.py:43
  55.7 2.4 %collective-permute-start.14 = (bf16[4,160,256]{2,1,0:T(8,128)(2,1)S(1)}, bf16[4,160,256]{2,1,0:T(8,128)(2,1)S(1)}, u32[]{:S(2)}, u32[]{:S(2)}) collective-permute-start(bf16[4,160,256]{2,1,0:T(8,128)(2,1)S(1)} %get-tuple-element.69), channel_id=1, source_target_pairs={{0,16},{16,0},{1,17},{17,1},{2,18},{18,2},{3,19},{19,3},{4,20},{20... | collective-permute-start | bytes 983048 | tf_op jit(solution)/shard_map/ppermute | solution.py:43
  56.2 8.6 %collective-permute-start.18 = (bf16[256,512]{1,0:T(8,128)(2,1)S(1)}, bf16[256,512]{1,0:T(8,128)(2,1)S(1)}, u32[]{:S(2)}, u32[]{:S(2)}) collective-permute-start(bf16[256,512]{1,0:T(8,128)(2,1)S(1)} %get-tuple-element.75), channel_id=1, source_target_pairs={{0,192},{64,0},{128,64},{192,128},{1,193},{65,1},{129,65},{193,129... | collective-permute-start | bytes 786440 | tf_op jit(solution)/shard_map/ppermute | solution.py:23
  58.2 29.1 %copy-start = (bf16[2048,512]{1,0:T(8,128)(2,1)S(1)}, bf16[2048,512]{1,0:T(8,128)(2,1)}, u32[]{:S(2)}) copy-start(bf16[2048,512]{1,0:T(8,128)(2,1)} %weight_ref.3) | copy-start | bytes 6291460
  58.2 19.9 %collective-permute-start.15 = (bf16[288,512]{1,0:T(8,128)(2,1)S(1)}, bf16[288,512]{1,0:T(8,128)(2,1)S(1)}, u32[]{:S(2)}, u32[]{:S(2)}) collective-permute-start(bf16[288,512]{1,0:T(8,128)(2,1)S(1)} %get-tuple-element.71), channel_id=1, source_target_pairs={{0,1},{1,2},{2,3},{3,0},{4,5},{5,6},{6,7},{7,4},{8,9},{9,10},{10,1... | collective-permute-start | bytes 884744 | tf_op jit(solution)/shard_map/ppermute | solution.py:23
  59.6 18.5 %collective-permute-start.16 = (bf16[288,512]{1,0:T(8,128)(2,1)S(1)}, bf16[288,512]{1,0:T(8,128)(2,1)S(1)}, u32[]{:S(2)}, u32[]{:S(2)}) collective-permute-start(bf16[288,512]{1,0:T(8,128)(2,1)S(1)} %get-tuple-element.72), channel_id=1, source_target_pairs={{0,2},{1,3},{2,0},{3,1},{4,6},{5,7},{6,4},{7,5},{8,10},{9,11},{10,... | collective-permute-start | bytes 884744 | tf_op jit(solution)/shard_map/ppermute | solution.py:23
  61.5 16.6 %collective-permute-start.17 = (bf16[288,512]{1,0:T(8,128)(2,1)S(1)}, bf16[288,512]{1,0:T(8,128)(2,1)S(1)}, u32[]{:S(2)}, u32[]{:S(2)}) collective-permute-start(bf16[288,512]{1,0:T(8,128)(2,1)S(1)} %get-tuple-element.73), channel_id=1, source_target_pairs={{0,3},{1,0},{2,1},{3,2},{4,7},{5,4},{6,5},{7,6},{8,11},{9,8},{10,9... | collective-permute-start | bytes 884744 | tf_op jit(solution)/shard_map/ppermute | solution.py:23
  62.5 10.8 %collective-permute-start.19 = (bf16[256,512]{1,0:T(8,128)(2,1)S(1)}, bf16[256,512]{1,0:T(8,128)(2,1)S(1)}, u32[]{:S(2)}, u32[]{:S(2)}) collective-permute-start(bf16[256,512]{1,0:T(8,128)(2,1)S(1)} %get-tuple-element.76), channel_id=1, source_target_pairs={{0,128},{64,192},{128,0},{192,64},{1,129},{65,193},{129,1},{193,65... | collective-permute-start | bytes 786440 | tf_op jit(solution)/shard_map/ppermute | solution.py:23
  64.8 12.5 %collective-permute-start.20 = (bf16[256,512]{1,0:T(8,128)(2,1)S(1)}, bf16[256,512]{1,0:T(8,128)(2,1)S(1)}, u32[]{:S(2)}, u32[]{:S(2)}) collective-permute-start(bf16[256,512]{1,0:T(8,128)(2,1)S(1)} %get-tuple-element.60), channel_id=1, source_target_pairs={{0,64},{64,128},{128,192},{192,0},{1,65},{65,129},{129,193},{193,1... | collective-permute-start | bytes 786440 | tf_op jit(solution)/shard_map/ppermute | solution.py:23
  77.4 0.7 copy-start.5
  78.4 15.4 %all-to-all-start.1 = ((bf16[8,32,512]{2,1,0:T(8,128)(2,1)}), bf16[8,32,512]{2,1,0:T(8,128)(2,1)}, u32[]{:S(2)}, u32[]{:S(2)}) async-start(bf16[8,32,512]{2,1,0:T(8,128)(2,1)} %copy-done.5), calls=%async_computation.1 | async-start | bytes 524288 | tf_op jit(solution)/shard_map/all_to_all | solution.py:413
  84.0 12.0 %collective-permute-start.27 = (bf16[128,512]{1,0:T(8,128)(2,1)S(1)}, bf16[128,512]{1,0:T(8,128)(2,1)}, u32[]{:S(2)}, u32[]{:S(2)}) collective-permute-start(bf16[128,512]{1,0:T(8,128)(2,1)S(1)} %shard_map.103.refs_0_), channel_id=1, source_target_pairs={{0,3},{1,0},{2,1},{3,2},{4,7},{5,4},{6,5},{7,6},{8,11},{9,8},{10,9... | collective-permute-start | bytes 393224 | tf_op jit(solution)/shard_map/ppermute | solution.py:23
  85.0 11.0 %collective-permute-start.26 = (bf16[128,512]{1,0:T(8,128)(2,1)S(1)}, bf16[128,512]{1,0:T(8,128)(2,1)}, u32[]{:S(2)}, u32[]{:S(2)}) collective-permute-start(bf16[128,512]{1,0:T(8,128)(2,1)S(1)} %shard_map.103.refs_0_), channel_id=1, source_target_pairs={{0,2},{1,3},{2,0},{3,1},{4,6},{5,7},{6,4},{7,5},{8,10},{9,11},{10,... | collective-permute-start | bytes 393224 | tf_op jit(solution)/shard_map/ppermute | solution.py:23
  87.1 9.5 %collective-permute-start.25 = (bf16[128,512]{1,0:T(8,128)(2,1)S(1)}, bf16[128,512]{1,0:T(8,128)(2,1)}, u32[]{:S(2)}, u32[]{:S(2)}) collective-permute-start(bf16[128,512]{1,0:T(8,128)(2,1)S(1)} %shard_map.103.refs_0_), channel_id=1, source_target_pairs={{0,1},{1,2},{2,3},{3,0},{4,5},{5,6},{6,7},{7,4},{8,9},{9,10},{10,1... | collective-permute-start | bytes 393224 | tf_op jit(solution)/shard_map/ppermute | solution.py:23
  87.8 0.6 copy-start.6
  95.5 1.4 %collective-permute-start.21 = (bf16[32,512]{1,0:T(8,128)(2,1)}, bf16[32,512]{1,0:T(8,128)(2,1)S(1)}, u32[]{:S(2)}, u32[]{:S(2)}) collective-permute-start(bf16[32,512]{1,0:T(8,128)(2,1)} %shard_map.105), channel_id=1, source_target_pairs={{0,16},{16,0},{1,17},{17,1},{2,18},{18,2},{3,19},{19,3},{4,20},{20... | collective-permute-start | bytes 98312 | tf_op jit(solution)/shard_map/ppermute | solution.py:43
  95.5 2.9 %collective-permute-start.28 = (bf16[128,512]{1,0:T(8,128)(2,1)S(1)}, bf16[128,512]{1,0:T(8,128)(2,1)S(1)}, u32[]{:S(2)}, u32[]{:S(2)}) collective-permute-start(bf16[128,512]{1,0:T(8,128)(2,1)S(1)} %shard_map.103.refs_0_), channel_id=1, source_target_pairs={{0,16},{16,0},{1,17},{17,1},{2,18},{18,2},{3,19},{19,3},{4,20},{20... | collective-permute-start | bytes 393224 | tf_op jit(solution)/shard_map/ppermute | solution.py:43
  96.0 4.7 %collective-permute-start.31 = (bf16[128,512]{1,0:T(8,128)(2,1)}, bf16[128,512]{1,0:T(8,128)(2,1)S(1)}, u32[]{:S(2)}, u32[]{:S(2)}) collective-permute-start(bf16[128,512]{1,0:T(8,128)(2,1)} %collective-permute-done.27.refs_3_), channel_id=1, source_target_pairs={{0,16},{16,0},{1,17},{17,1},{2,18},{18,2},{3,19},{19,3},{4,20},{20... | collective-permute-start | bytes 393224 | tf_op jit(solution)/shard_map/ppermute | solution.py:43
  96.1 5.0 %collective-permute-start.30 = (bf16[128,512]{1,0:T(8,128)(2,1)}, bf16[128,512]{1,0:T(8,128)(2,1)S(1)}, u32[]{:S(2)}, u32[]{:S(2)}) collective-permute-start(bf16[128,512]{1,0:T(8,128)(2,1)} %collective-permute-done.26.refs_2_), channel_id=1, source_target_pairs={{0,16},{16,0},{1,17},{17,1},{2,18},{18,2},{3,19},{19,3},{4,20},{20... | collective-permute-start | bytes 393224 | tf_op jit(solution)/shard_map/ppermute | solution.py:43
  96.6 4.5 %collective-permute-start.29 = (bf16[128,512]{1,0:T(8,128)(2,1)}, bf16[128,512]{1,0:T(8,128)(2,1)S(1)}, u32[]{:S(2)}, u32[]{:S(2)}) collective-permute-start(bf16[128,512]{1,0:T(8,128)(2,1)} %collective-permute-done.25.refs_1_), channel_id=1, source_target_pairs={{0,16},{16,0},{1,17},{17,1},{2,18},{18,2},{3,19},{19,3},{4,20},{20... | collective-permute-start | bytes 393224 | tf_op jit(solution)/shard_map/ppermute | solution.py:43
  97.7 5.1 %collective-permute-start.24 = (bf16[64,512]{1,0:T(8,128)(2,1)S(1)}, bf16[64,512]{1,0:T(8,128)(2,1)S(1)}, u32[]{:S(2)}, u32[]{:S(2)}) collective-permute-start(bf16[64,512]{1,0:T(8,128)(2,1)S(1)} %pad_maximum_fusion.b0), channel_id=1, source_target_pairs={{0,3},{1,0},{2,1},{3,2},{4,7},{5,4},{6,5},{7,6},{8,11},{9,8},{10,9... | collective-permute-start | bytes 196616 | tf_op jit(solution)/shard_map/ppermute | solution.py:23
  98.5 6.0 %collective-permute-start.23 = (bf16[64,512]{1,0:T(8,128)(2,1)S(1)}, bf16[64,512]{1,0:T(8,128)(2,1)S(1)}, u32[]{:S(2)}, u32[]{:S(2)}) collective-permute-start(bf16[64,512]{1,0:T(8,128)(2,1)S(1)} %pad_maximum_fusion.b0), channel_id=1, source_target_pairs={{0,2},{1,3},{2,0},{3,1},{4,6},{5,7},{6,4},{7,5},{8,10},{9,11},{10,... | collective-permute-start | bytes 196616 | tf_op jit(solution)/shard_map/ppermute | solution.py:23
  100.7 5.5 %collective-permute-start.22 = (bf16[64,512]{1,0:T(8,128)(2,1)S(1)}, bf16[64,512]{1,0:T(8,128)(2,1)S(1)}, u32[]{:S(2)}, u32[]{:S(2)}) collective-permute-start(bf16[64,512]{1,0:T(8,128)(2,1)S(1)} %pad_maximum_fusion.b0), channel_id=1, source_target_pairs={{0,1},{1,2},{2,3},{3,0},{4,5},{5,6},{6,7},{7,4},{8,9},{9,10},{10,1... | collective-permute-start | bytes 196616 | tf_op jit(solution)/shard_map/ppermute | solution.py:23
  107.5 5.6 %collective-permute-start.32 = (bf16[64,1024]{1,0:T(8,128)(2,1)S(1)}, bf16[64,1024]{1,0:T(8,128)(2,1)S(1)}, u32[]{:S(2)}, u32[]{:S(2)}) collective-permute-start(bf16[64,1024]{1,0:T(8,128)(2,1)S(1)} %get-tuple-element.82), channel_id=1, source_target_pairs={{0,192},{64,0},{128,64},{192,128},{1,193},{65,1},{129,65},{193,129... | collective-permute-start | bytes 393224 | tf_op jit(solution)/shard_map/ppermute | solution.py:23
  107.6 7.6 %collective-permute-start.33 = (bf16[64,1024]{1,0:T(8,128)(2,1)S(1)}, bf16[64,1024]{1,0:T(8,128)(2,1)S(1)}, u32[]{:S(2)}, u32[]{:S(2)}) collective-permute-start(bf16[64,1024]{1,0:T(8,128)(2,1)S(1)} %get-tuple-element.83), channel_id=1, source_target_pairs={{0,128},{64,192},{128,0},{192,64},{1,129},{65,193},{129,1},{193,65... | collective-permute-start | bytes 393224 | tf_op jit(solution)/shard_map/ppermute | solution.py:23
  108.5 7.6 %collective-permute-start.34 = (bf16[64,1024]{1,0:T(8,128)(2,1)S(1)}, bf16[64,1024]{1,0:T(8,128)(2,1)S(1)}, u32[]{:S(2)}, u32[]{:S(2)}) collective-permute-start(bf16[64,1024]{1,0:T(8,128)(2,1)S(1)} %get-tuple-element.84), channel_id=1, source_target_pairs={{0,64},{64,128},{128,192},{192,0},{1,65},{65,129},{129,193},{193,1... | collective-permute-start | bytes 393224 | tf_op jit(solution)/shard_map/ppermute | solution.py:23
